TPU v7x, 32 devices: a whole 2x2x4 slice. The times are simulated.
32 devices in a mesh: dp: 4 (over z), seq: 8 (over y, x, core).
Axes of the slice: x: 2, y: 2, z: 4, core: 2. Of those that a mesh axis runs over, the one named last changes fastest.
Arguments:
- seq_in: bfloat16 [8192, 1536], P(('dp', 'seq')), parts along dimension 0, may hold values from -6 to 6
- conv_gain: float32 [1536], replicated, may hold values from 0.1 to 1.9
- convolution_weight: bfloat16 [3, 1536, 768], replicated, may hold values from -0.09375 to 0.09375
- conv_bias: float32 [768], replicated, may hold values from -3 to 3
- attn_gain: float32 [1536], replicated, may hold values from 0.1 to 1.9
- w_query: bfloat16 [1536, 512], replicated
- w_key: bfloat16 [1536, 128], replicated
- w_value: bfloat16 [1536, 128], replicated, may hold values from -0.15625 to 0.15625
- w_out: bfloat16 [512, 1536], replicated, may hold values from -0.25 to 0.25
Outputs:
- block_out: bfloat16 [8192, 1536], P(('dp', 'seq')), parts along dimension 0
There are 4 independent parts, one for each index of `dp`. A program takes and returns all parts, laid end to end along the dimension named above; an argument that names none is the same for every part. Nothing has to cross between parts.
All inputs are finite; a program needn't handle non-finite values.
Results may differ from a plain program's by a relative error of at most 0.0059.
Values may be sent and summed in bfloat16 or wider, within the bound.
No kernel may reach another device: no remote copies, remote signals or barrier semaphores. Data moves between devices by JAX's collectives and lax.ppermute only.
A program may use at most 128 MiB of HBM per device.

v0:
```python
import jax
import jax.numpy as jnp
from jax import lax
from jax.sharding import PartitionSpec as P

DILATION_STEP = 4


def padded(cells, sides, width):
    for axis, dim in sides:
        count = lax.axis_size(axis)
        ends = count - 1
        head = lax.slice_in_dim(cells, 0, width, axis=dim)
        tail = lax.slice_in_dim(cells, cells.shape[dim] - width, cells.shape[dim], axis=dim)
        cells = jnp.concatenate(
            [
                lax.ppermute(tail, axis, [(i, (i + 1) % count) for i in range(ends)]),
                cells,
                lax.ppermute(head, axis, [((i + 1) % count, i) for i in range(ends)]),
            ],
            axis=dim,
        )
    return cells


def normalize(values, gain_vec):
    wide = values.astype(jnp.float32)
    meansq = jnp.mean(wide * wide, axis=-1, keepdims=True)
    return wide * lax.rsqrt(meansq + 1e-06) * gain_vec


def fold_block(state_now, keys_vals, queries, head_dim):
    maxima, totals, summed = state_now
    key_part = keys_vals[:, :head_dim]
    value_part = keys_vals[:, head_dim:]
    scores = jnp.einsum(
        "thd,kd->htk", queries, key_part, preferred_element_type=jnp.float32
    ) * head_dim ** (-0.5)
    new_max = jnp.maximum(maxima, jnp.max(scores, axis=-1))
    expd = jnp.exp(scores - new_max[..., None])
    totals = jnp.sum(expd, axis=-1)
    summed = jnp.einsum(
        "htk,kd->htd", expd.astype(jnp.bfloat16), value_part, preferred_element_type=jnp.float32
    )
    return (new_max, totals, summed)


def shards(
    seq_in, conv_gain, convolution_weight, conv_bias, attn_gain, w_query, w_key, w_value, w_out
):
    token_rows = seq_in.shape[0]
    kernel_taps = convolution_weight.shape[0]
    head_dim = w_key.shape[1]
    heads_all = w_query.shape[1] // head_dim
    out_chan = convolution_weight.shape[2]
    receptive_reach = DILATION_STEP * (kernel_taps - 1) // 2
    normed = normalize(seq_in, conv_gain).astype(jnp.bfloat16)
    padded_tokens = padded(normed, (("seq", 0),), receptive_reach)
    convolved_total = jnp.dot(
        padded_tokens[0:token_rows], convolution_weight[0], preferred_element_type=jnp.float32
    )
    for tap_index in range(1, kernel_taps):
        convolved_total = convolved_total + jnp.dot(
            padded_tokens[tap_index * DILATION_STEP : tap_index * DILATION_STEP + token_rows],
            convolution_weight[tap_index],
            preferred_element_type=jnp.float32,
        )
    activated = jax.nn.gelu(convolved_total + conv_bias, approximate=True)
    wide_in = seq_in.astype(jnp.float32)
    hidden = jnp.concatenate(
        [wide_in[:, :out_chan] + activated, wide_in[:, out_chan:]], axis=1
    ).astype(jnp.bfloat16)
    attn_in = normalize(hidden, attn_gain).astype(jnp.bfloat16)
    queries = jnp.dot(attn_in, w_query, preferred_element_type=jnp.float32).astype(jnp.bfloat16)
    queries = queries.reshape(token_rows, heads_all, head_dim)
    key_rows = jnp.dot(attn_in, w_key, preferred_element_type=jnp.float32).astype(jnp.bfloat16)
    value_rows = jnp.dot(attn_in, w_value, preferred_element_type=jnp.float32).astype(jnp.bfloat16)
    packed = jnp.concatenate([key_rows, value_rows], axis=1)
    start_state = (
        jnp.full((heads_all, token_rows), -1e30, jnp.float32),
        jnp.zeros((heads_all, token_rows), jnp.float32),
        jnp.zeros((heads_all, token_rows, head_dim), jnp.float32),
    )
    final_state = fold_block(
        start_state, lax.all_gather(packed, "seq", axis=0, tiled=True), queries, head_dim
    )
    maxima, totals, summed = final_state
    result = summed / totals[..., None]
    attended = (
        jnp.transpose(result, (1, 0, 2))
        .reshape(token_rows, heads_all * head_dim)
        .astype(jnp.bfloat16)
    )
    mixed = hidden.astype(jnp.float32) + jnp.dot(
        attended, w_out, preferred_element_type=jnp.float32
    )
    return mixed.astype(jnp.bfloat16)


def solution(mesh):
    placed = (P(("dp", "seq"), None), P(), P(), P(), P(), P(), P(), P(), P())
    return jax.shard_map(
        shards, mesh=mesh, in_specs=placed, out_specs=P(("dp", "seq"), None), check_vma=False
    )
```

profile of v0, /device:TPU:1, one launch (start us, length us, event | category | flops | bytes accessed | tf_op | source)
XLA Modules:
  0.0 62.9 jit_solution(5649299373199626095)
XLA Ops:
  6.5 0.0 copy-start
  6.5 0.0 all-gather.2.cloned.1.call-start
  6.5 1.5 %multiply_reduce_fusion = f32[256]{0:T(256)S(1)} fusion(bf16[256,1536]{1,0:T(8,128)(2,1)} %param.9), kind=kLoop, calls=%fused_computation.23 | loop fusion | flops 1179392 | bytes 787456 | tf_op jit(solution)/shard_map/reduce_sum | solution.py:28
  8.0 1.4 %multiply_convert_fusion = bf16[256,1536]{1,0:T(8,128)(2,1)S(1)} fusion(f32[1536]{0:T(1024)} %param.10, f32[256]{0:T(256)S(1)} %add_rsqrt_fusion.1, bf16[256,1536]{1,0:T(8,128)(2,1)} %param.9), kind=kLoop, calls=%fused_computation.22 | loop fusion | flops 1572864 | bytes 1580032 | tf_op jit(solution)/shard_map/convert_element_type | solution.py:57
  9.5 4.5 %collective-permute-start = (bf16[4,1536]{1,0:T(4,128)(2,1)S(1)}, bf16[4,1536]{1,0:T(4,128)(2,1)S(1)}, u32[]{:S(2)}, u32[]{:S(2)}) collective-permute-start(bf16[4,1536]{1,0:T(4,128)(2,1)S(1)} %get-tuple-element.5), channel_id=1, source_target_pairs={{0,1},{1,2},{2,3},{3,4},{4,5},{5,6},{6,7},{8,9},{9,10},{10,11},{11... | collective-permute-start | bytes 36872 | tf_op jit(solution)/shard_map/ppermute | solution.py:17
  14.0 0.0 copy-start.1
  14.0 2.1 %collective-permute-start.1 = (bf16[4,1536]{1,0:T(4,128)(2,1)S(1)}, bf16[4,1536]{1,0:T(4,128)(2,1)S(1)}, u32[]{:S(2)}, u32[]{:S(2)}) collective-permute-start(bf16[4,1536]{1,0:T(4,128)(2,1)S(1)} %get-tuple-element.6), channel_id=1, source_target_pairs={{1,0},{2,1},{3,2},{4,3},{5,4},{6,5},{7,6},{9,8},{10,9},{11,10},{12... | collective-permute-start | bytes 36872 | tf_op jit(solution)/shard_map/ppermute | solution.py:19
  16.1 0.0 copy-start.3
  16.1 2.6 %fusion.8 = f32[256,768]{1,0:T(8,128)S(1)} fusion(bf16[256,1536]{1,0:T(8,128)(2,1)S(1)} %multiply_convert_fusion, bf16[3,1536,768]{2,1,0:T(8,128)(2,1)} %param.11), kind=kOutput, calls=%fused_computation.12 | convolution fusion | flops 603979776 | bytes 3932160 | tf_op jit(solution)/shard_map/dot_general | solution.py:63
  18.7 0.0 copy-done.1
  18.7 0.2 convert_element_type.36
  18.9 0.0 copy-start.7
  18.9 0.2 collective-permute-done.1
  19.1 0.6 %copy-done.3 = bf16[3,1536,768]{2,1,0:T(8,128)(2,1)S(1)} copy-done((bf16[3,1536,768]{2,1,0:T(8,128)(2,1)S(1)}, bf16[3,1536,768]{2,1,0:T(8,128)(2,1)}, u32[]{:S(2)}) %copy-start.3) | copy-done | bytes 7077912
  19.8 0.8 %fusion.6 = f32[256,768]{1,0:T(8,128)S(1)} fusion(bf16[3,1536,768]{2,1,0:T(8,128)(2,1)S(1)} %copy-done.3, bf16[4,1536]{1,0:T(4,128)(2,1)S(1)} %collective-permute-done.1, bf16[256,1536]{1,0:T(8,128)(2,1)S(1)} %multiply_convert_fusion), kind=kOutput, calls=%fused_computation.10 | convolution fusion | flops 605552640 | bytes 3944448 | tf_op jit(solution)/shard_map/dot_general | solution.py:63
  20.6 0.0 copy-start.4
  20.6 0.0 copy-start.6
  20.6 0.0 collective-permute-done
  20.6 0.0 copy-done.7
  20.6 1.0 %fusion.49 = bf16[256,768]{1,0:T(8,128)(2,1)S(1)} fusion(f32[256,768]{1,0:T(8,128)S(1)} %fusion.6, f32[256,768]{1,0:T(8,128)S(1)} %fusion.8, bf16[3,1536,768]{2,1,0:T(8,128)(2,1)S(1)} %copy-done.3, bf16[256,1536]{1,0:T(8,128)(2,1)S(1)} %multiply_convert_fusion, bf16[4,1536]{1,0:T(4,128)(2,1)S(1)} %collective-permute-done, ...), kind=kOutput, calls=%fused_computation.43 | convolution fusion | flops 608108544 | bytes 5914624 | tf_op jit(solution)/shard_map/dot_general | solution.py:59
  21.6 0.0 copy-start.5
  21.6 0.2 fusion.15
  21.9 0.0 copy-done.4
  21.9 0.0 copy-done.6
  21.9 0.5 convolution_convert_fusion.1
  22.4 0.2 copy-done.5
  22.6 0.5 convolution_convert_fusion.2
  23.1 0.7 %pad_maximum_fusion.5 = bf16[256,256]{0,1:T(8,128)(2,1)} fusion(bf16[256,128]{0,1:T(8,128)(2,1)S(1)} %convolution_convert_fusion.1, bf16[256,128]{0,1:T(8,128)(2,1)S(1)} %convolution_convert_fusion.2), kind=kLoop, calls=%fused_computation.54 | loop fusion | flops 262144 | bytes 262144 | tf_op jit(solution)/shard_map/concatenate | solution.py:78
  23.8 0.0 all-gather.2.cloned.1.call-update
  23.8 2.0 %fusion.30 = bf16[32,4,8,128]{3,2,1,0:T(8,128)(2,1)S(1)} fusion(bf16[1536,512]{1,0:T(8,128)(2,1)} %param.14, f32[1536]{0:T(1024)S(1)} %copy-done.6, f32[256]{0:T(256)S(1)} %add_rsqrt_fusion, bf16[256,768]{1,0:T(8,128)(2,1)S(1)} %slice.44, bf16[256,768]{1,0:T(8,128)(2,1)S(1)} %fusion.49), kind=kOutput, calls=%fused_computation.30 | convolution fusion | flops 405536768 | bytes 2628608 | tf_op jit(solution)/shard_map/dot_general | solution.py:74
  25.8 23.3 %all-gather.2.cloned.1.call-done = bf16[2048,256]{0,1:T(8,128)(2,1)} async-done(((bf16[256,256]{0,1:T(8,128)(2,1)}), bf16[2048,256]{0,1:T(8,128)(2,1)}) %all-gather.2.cloned.1.call-update) | async-done | bytes 1048592 | tf_op jit(solution)/shard_map/all_gather | solution.py:85
  49.2 2.3 %bitcast_reduce_fusion = (f32[4,256]{1,0:T(4,128)S(1)}, f32[2048,256,4]{1,0,2:T(8,128)S(1)}) fusion(bf16[32,4,8,128]{3,2,1,0:T(8,128)(2,1)S(1)} %fusion.30, bf16[2048,256]{0,1:T(8,128)(2,1)} %all-gather.2.cloned.1.call-done), kind=kOutput, calls=%fused_computation.1 | convolution fusion | flops 541064192 | bytes 9179136 | tf_op jit(solution)/shard_map/thd,kd->htk/dot_general | solution.py:36
  51.5 0.0 copy-start.2
  51.5 1.4 %fusion.1 = f32[4,256]{1,0:T(4,128)S(1)} fusion(f32[2048,256,4]{1,0,2:T(8,128)S(1)} %get-tuple-element.8, f32[4,256]{1,0:T(4,128)S(1)} %broadcast_maximum_fusion), kind=kLoop, calls=%fused_computation.3 | loop fusion | flops 6290432 | bytes 8396800 | tf_op jit(solution)/shard_map/reduce_sum | solution.py:41
  52.9 0.0 copy-done.2
  52.9 1.6 %fusion.34 = bf16[256,4,128]{0,2,1:T(8,128)(2,1)S(1)} fusion(f32[2048,256,4]{1,0,2:T(8,128)S(1)} %get-tuple-element.8, f32[4,256]{1,0:T(4,128)S(1)} %broadcast_maximum_fusion, bf16[2048,256]{0,1:T(8,128)(2,1)S(1)} %copy-done.2, f32[256,4]{0,1:T(4,128)S(1)} %bitcast.66), kind=kOutput, calls=%fused_computation.34 | convolution fusion | flops 543424512 | bytes 9183232 | tf_op jit(solution)/shard_map/htk,kd->htd/dot_general | solution.py:42
  54.6 0.0 copy-done
  54.6 1.5 %fusion.5 = bf16[256,1536]{1,0:T(8,128)(2,1)} fusion(bf16[256,512]{0,1:T(8,128)(2,1)S(1)} %bitcast.67, bf16[512,1536]{1,0:T(8,128)(2,1)S(1)} %copy-done, bf16[256,768]{1,0:T(8,128)(2,1)S(1)} %slice.44, bf16[256,768]{1,0:T(8,128)(2,1)S(1)} %fusion.49), kind=kOutput, calls=%fused_computation.7 | convolution fusion | flops 405012480 | bytes 3407872 | tf_op jit(solution)/shard_map/dot_general | solution.py:94
  (5 shorter events, 0.1 us)
Async XLA Ops:
  6.5 48.0 %copy-start = (bf16[512,1536]{1,0:T(8,128)(2,1)S(1)}, bf16[512,1536]{1,0:T(8,128)(2,1)}, u32[]{:S(2)}) copy-start(bf16[512,1536]{1,0:T(8,128)(2,1)} %param.17) | copy-start | bytes 4718596
  6.5 42.6 %all-gather.2.cloned.1.call-start = ((), (), s32[]{:S(2)}) async-start(), calls=%async_computation | async-start | bytes 1179648 | tf_op jit(solution)/shard_map/all_gather | solution.py:85
  9.5 11.1 %collective-permute-start = (bf16[4,1536]{1,0:T(4,128)(2,1)S(1)}, bf16[4,1536]{1,0:T(4,128)(2,1)S(1)}, u32[]{:S(2)}, u32[]{:S(2)}) collective-permute-start(bf16[4,1536]{1,0:T(4,128)(2,1)S(1)} %get-tuple-element.5), channel_id=1, source_target_pairs={{0,1},{1,2},{2,3},{3,4},{4,5},{5,6},{6,7},{8,9},{9,10},{10,11},{11... | collective-permute-start | bytes 36872 | tf_op jit(solution)/shard_map/ppermute | solution.py:17
  14.0 4.7 %copy-start.1 = (bf16[256,1536]{1,0:T(8,128)(2,1)S(1)}, bf16[256,1536]{1,0:T(8,128)(2,1)}, u32[]{:S(2)}) copy-start(bf16[256,1536]{1,0:T(8,128)(2,1)} %param.9) | copy-start | bytes 2359300
  14.0 5.1 %collective-permute-start.1 = (bf16[4,1536]{1,0:T(4,128)(2,1)S(1)}, bf16[4,1536]{1,0:T(4,128)(2,1)S(1)}, u32[]{:S(2)}, u32[]{:S(2)}) collective-permute-start(bf16[4,1536]{1,0:T(4,128)(2,1)S(1)} %get-tuple-element.6), channel_id=1, source_target_pairs={{1,0},{2,1},{3,2},{4,3},{5,4},{6,5},{7,6},{9,8},{10,9},{11,10},{12... | collective-permute-start | bytes 36872 | tf_op jit(solution)/shard_map/ppermute | solution.py:19
  16.1 3.7 %copy-start.3 = (bf16[3,1536,768]{2,1,0:T(8,128)(2,1)S(1)}, bf16[3,1536,768]{2,1,0:T(8,128)(2,1)}, u32[]{:S(2)}) copy-start(bf16[3,1536,768]{2,1,0:T(8,128)(2,1)} %param.11) | copy-start | bytes 21233668
  18.9 1.7 %copy-start.7 = (f32[768]{0:T(1024)S(1)}, f32[768]{0:T(1024)}, u32[]{:S(2)}) copy-start(f32[768]{0:T(1024)} %param.12) | copy-start | bytes 9220
  20.6 1.3 %copy-start.4 = (bf16[1536,128]{1,0:T(8,128)(2,1)S(1)}, bf16[1536,128]{1,0:T(8,128)(2,1)}, u32[]{:S(2)}) copy-start(bf16[1536,128]{1,0:T(8,128)(2,1)} %param.16) | copy-start | bytes 1179652
  20.6 1.3 %copy-start.6 = (f32[1536]{0:T(1024)S(1)}, f32[1536]{0:T(1024)}, u32[]{:S(2)}) copy-start(f32[1536]{0:T(1024)} %param.13) | copy-start | bytes 18436
  21.6 1.0 %copy-start.5 = (bf16[1536,128]{1,0:T(8,128)(2,1)S(1)}, bf16[1536,128]{1,0:T(8,128)(2,1)}, u32[]{:S(2)}) copy-start(bf16[1536,128]{1,0:T(8,128)(2,1)} %param.15) | copy-start | bytes 1179652
  51.5 1.4 %copy-start.2 = (bf16[2048,256]{0,1:T(8,128)(2,1)S(1)}, bf16[2048,256]{0,1:T(8,128)(2,1)}, u32[]{:S(2)}) copy-start(bf16[2048,256]{0,1:T(8,128)(2,1)} %all-gather.2.cloned.1.call-done) | copy-start | bytes 3145732
Sparse Core Ops, SparseCore 0:
  23.9 25.2 all-gather.1
where the time goes:
time: 63.4 us; the launch traced here: 62.9 us
  waiting for transfers between devices  23.6 us (37%)
  between operations  13.6 us (21%)
  matrix products  12.8 us (20%)
  starting transfers between devices  6.56 us (10%)
  other arithmetic  5.35 us (8%)
  local copies, waits for them, and re-layouts  0.94 us (1%)
    all_gather x1, waiting for transfers between devices, shards(): lax.all_gather(packed, 'seq', axis=0, tiled=True)  23.3 us
    ppermute x1, starting transfers between devices, padded(): lax.ppermute(tail, axis, [(i, (i + 1) % count) for i in range(ends)])  4.51 us
    dot_general x2, matrix products, shards(): jnp.dot(padded_tokens[tap_index * DILATION_STEP:tap_index * DILATION_STEP...  3.39 us
    dot_general x1, matrix products, fold_block(): jnp.einsum('thd,kd->htk', queries, key_part, preferred_element_type=jnp.f...  2.35 us
    ppermute x1, starting transfers between devices, padded(): lax.ppermute(head, axis, [((i + 1) % count, i) for i in range(ends)])  2.05 us
    dot_general x1, matrix products, shards(): jnp.dot(attn_in, w_query, preferred_element_type=jnp.float32)  2.03 us
    reduce_sum x2, other arithmetic, normalize(): meansq = jnp.mean(wide * wide, axis=-1, keepdims=True)  1.72 us
    dot_general x1, matrix products, fold_block(): jnp.einsum('htk,kd->htd', expd.astype(jnp.bfloat16), value_part, preferre...  1.63 us
  transfers between devices with their start and end apart: 3, of which 2 were waited for; matrix products, arithmetic and copies ran while one was open for 9% of the time, Pallas kernels for 0%

commit v1 on v0

v1 whole, which is shorter than its diff:
```python
import functools

import jax
import jax.numpy as jnp
from jax import lax
from jax.experimental import pallas as pl
from jax.experimental.pallas import tpu as pltpu
from jax.sharding import PartitionSpec as P

DILATION_STEP = 4
EPS = 1e-06
LOG2E = 1.4426950408889634
F32 = jnp.float32
BF16 = jnp.bfloat16
VMEM = pl.BlockSpec(memory_space=pltpu.VMEM)
SMEM = pl.BlockSpec(memory_space=pltpu.SMEM)


def normed_rows(values, gain):
    wide = values.astype(F32)
    meansq = jnp.mean(wide * wide, axis=-1, keepdims=True)
    return wide * lax.rsqrt(meansq + EPS) * gain


def dot(a, b):
    return jnp.dot(a, b, preferred_element_type=F32)


def conv_kernel(reach, x_ref, gain_ref, w_ref, part_ref, pad_ref):
    rows, chan = x_ref.shape
    taps = w_ref.shape[0]
    pad_ref[0:8, :] = jnp.zeros((8, chan), F32)
    pad_ref[8 + rows : 16 + rows, :] = jnp.zeros((8, chan), F32)
    pad_ref[8 : 8 + rows, :] = normed_rows(x_ref[...], gain_ref[...])
    total = None
    for tap in range(taps):
        start = 8 - reach + tap * DILATION_STEP
        piece = dot(pad_ref[start : start + rows, :].astype(BF16), w_ref[tap])
        total = piece if total is None else total + piece
    part_ref[...] = total


def project_kernel(
    reach, place_ref, x_ref, part_ref, near_ref, far_ref, gain_ref, w_ref, bias_ref, again_ref, wk_ref, wv_ref,
    hidden_ref, attn_ref, kv_ref, sum_ref,
):
    rows, chan = x_ref.shape
    taps, _, out_chan = w_ref.shape
    head_dim = wk_ref.shape[1]
    index, count = place_ref[0], place_ref[1]
    even = lax.rem(index, 2) == 0
    near, far = near_ref[...].astype(F32), far_ref[...].astype(F32)
    left = jnp.where(even, far, near)
    right = jnp.where(even, near, far)
    row = lax.broadcasted_iota(jnp.int32, (2 * reach, 1), 0)
    left = jnp.where((row >= reach) & (index > 0), normed_rows(left, gain_ref[...]), 0.0)
    right = jnp.where((row < reach) & (index < count - 1), normed_rows(right, gain_ref[...]), 0.0)
    sum_ref[...] = part_ref[...]
    for tap in range(taps):
        shift = (tap - (taps - 1) // 2) * DILATION_STEP
        if shift < 0:
            window = left[2 * reach + shift : 2 * reach].astype(BF16)
            sum_ref[0:-shift, :] += dot(window, w_ref[tap])
        elif shift > 0:
            window = right[0:shift].astype(BF16)
            sum_ref[rows - shift : rows, :] += dot(window, w_ref[tap])
    activated = jax.nn.gelu(sum_ref[...] + bias_ref[...], approximate=True)
    first = (x_ref[:, :out_chan].astype(F32) + activated).astype(BF16)
    hidden_ref[:, :out_chan] = first
    hidden_ref[:, out_chan:] = x_ref[:, out_chan:]
    attn_in = normed_rows(hidden_ref[...], again_ref[...]).astype(BF16)
    attn_ref[...] = attn_in
    kv_ref[:, :head_dim] = dot(attn_in, wk_ref[...]).astype(BF16)
    kv_ref[:, head_dim:] = dot(attn_in, wv_ref[...]).astype(BF16)


def fold(q_of, heads, rows, head_dim, kv_refs, m_ref, l_ref, acc_ref, first):
    scale = LOG2E * head_dim**-0.5
    for h in range(heads):
        q = q_of(h)
        span = slice(h * rows, (h + 1) * rows)
        scores = [
            lax.dot_general(q, kv[:, :head_dim], (((1,), (1,)), ((), ())), preferred_element_type=F32) * scale
            for kv in kv_refs
        ]
        top = jnp.max(functools.reduce(jnp.maximum, scores), axis=-1, keepdims=True)
        if not first:
            old = m_ref[span, :]
            top = jnp.maximum(old, top)
        summed, total = None, None
        for s, kv in zip(scores, kv_refs):
            e = jnp.exp2(s - top)
            t = jnp.sum(e, axis=-1, keepdims=True)
            o = dot(e.astype(BF16), kv[:, head_dim:])
            summed = o if summed is None else summed + o
            total = t if total is None else total + t
        if not first:
            fade = jnp.exp2(old - top)
            summed = summed + acc_ref[span, :] * fade
            total = total + l_ref[span, :] * fade
        m_ref[span, :] = top
        l_ref[span, :] = total
        acc_ref[span, :] = summed


def query_kernel(attn_ref, wq_ref, kv_ref, q_ref, m_ref, l_ref, acc_ref):
    rows = attn_ref.shape[0]
    head_dim = kv_ref.shape[1] // 2
    heads = wq_ref.shape[1] // head_dim
    q_ref[...] = dot(attn_ref[...], wq_ref[...]).astype(BF16)
    fold(
        lambda h: q_ref[:, h * head_dim : (h + 1) * head_dim], heads, rows, head_dim,
        [kv_ref], m_ref, l_ref, acc_ref, True,
    )


def last_kernel(blocks, q_ref, hidden_ref, wo_ref, m0_ref, l0_ref, acc0_ref, *rest):
    kv_refs = rest[:blocks]
    out_ref, m_ref, l_ref, acc_ref = rest[blocks:]
    rows = q_ref.shape[0]
    head_dim = kv_refs[0].shape[1] // 2
    heads = q_ref.shape[1] // head_dim
    m_ref[...] = m0_ref[...]
    l_ref[...] = l0_ref[...]
    acc_ref[...] = acc0_ref[...]
    for kv in kv_refs:
        fold(
            lambda h: q_ref[:, h * head_dim : (h + 1) * head_dim], heads, rows, head_dim,
            [kv], m_ref, l_ref, acc_ref, False,
        )
    attended = jnp.concatenate(
        [(acc_ref[h * rows : (h + 1) * rows, :] / l_ref[h * rows : (h + 1) * rows, :]).astype(BF16) for h in range(heads)],
        axis=1,
    )
    out_ref[...] = (hidden_ref[...].astype(F32) + dot(attended, wo_ref[...])).astype(BF16)


def call(body, outs, args, specs=None, scratch=(), flops=0, moved=0, name=None):
    return pl.pallas_call(
        body,
        out_shape=outs,
        in_specs=specs or [VMEM] * len(args),
        out_specs=jax.tree.map(lambda _: VMEM, outs),
        scratch_shapes=scratch,
        compiler_params=pltpu.CompilerParams(vmem_limit_bytes=16 * 1024 * 1024),
        cost_estimate=pl.CostEstimate(flops=flops, bytes_accessed=moved, transcendentals=0),
        name=name,
    )(*args)


def shards(
    seq_in, conv_gain, convolution_weight, conv_bias, attn_gain, w_query, w_key, w_value, w_out
):
    rows, chan = seq_in.shape
    taps, _, out_chan = convolution_weight.shape
    head_dim = w_key.shape[1]
    heads = w_query.shape[1] // head_dim
    reach = DILATION_STEP * (taps - 1) // 2
    count = lax.axis_size("seq")
    index = lax.axis_index("seq")
    shape = jax.ShapeDtypeStruct

    edges = jnp.concatenate([seq_in[:reach], seq_in[rows - reach :]], axis=0)
    near = lax.ppermute(edges, "seq", [(i, i ^ 1) for i in range(count)])
    far_pairs = [(i, (i - 1 if i % 2 == 0 else i + 1) % count) for i in range(count)]
    far = lax.ppermute(edges, "seq", far_pairs)

    gain_row = conv_gain[None, :]
    part = call(
        functools.partial(conv_kernel, reach),
        shape((rows, out_chan), F32),
        (seq_in, gain_row, convolution_weight),
        scratch=[pltpu.VMEM((rows + 16, chan), F32)],
        flops=2 * rows * chan * out_chan * taps,
        moved=convolution_weight.size * 2,
        name="conv",
    )
    place = jnp.stack([index, jnp.int32(count)]).astype(jnp.int32)
    hidden, attn_in, kv = call(
        functools.partial(project_kernel, reach),
        (shape((rows, chan), BF16), shape((rows, chan), BF16), shape((rows, 2 * head_dim), BF16)),
        (place, seq_in, part, near, far, gain_row, convolution_weight, conv_bias[None, :], attn_gain[None, :], w_key, w_value),
        specs=[SMEM] + [VMEM] * 10,
        scratch=[pltpu.VMEM((rows, out_chan), F32)],
        flops=2 * rows * chan * 2 * head_dim,
        name="project",
    )
    sibling = [(i, i ^ 1) for i in range(count)]
    blocks = []
    for step in range(2, count, 2):
        blocks.append(lax.ppermute(kv, "seq", [(i, i ^ step) for i in range(count)]))
    passed = [lax.ppermute(b, "seq", sibling) for b in [kv] + blocks]
    state = (
        shape((rows * heads, 1), F32),
        shape((rows * heads, 1), F32),
        shape((rows * heads, head_dim), F32),
    )
    q, m, l, acc = call(
        query_kernel,
        (shape((rows, heads * head_dim), BF16),) + state,
        (attn_in, w_query, kv),
        flops=2 * rows * chan * heads * head_dim,
        name="query",
    )
    kvs = blocks + passed
    return call(
        functools.partial(last_kernel, len(kvs)),
        shape((rows, chan), BF16),
        (q, hidden, w_out, m, l, acc, *kvs),
        scratch=[pltpu.VMEM(s.shape, s.dtype) for s in state],
        flops=4 * rows * heads * head_dim * rows * len(kvs),
        name="attend",
    )


def solution(mesh):
    placed = (P(("dp", "seq"), None), P(), P(), P(), P(), P(), P(), P(), P())
    return jax.shard_map(
        shards, mesh=mesh, in_specs=placed, out_specs=P(("dp", "seq"), None), check_vma=False
    )
```

time: 63.4 us -> 34.9 us (0.55)
  waiting for transfers between devices: 23.6 us -> 0.19 us
  Pallas kernels: 0 us -> 15.4 us
  between operations: 13.6 us -> 0.14 us
  matrix products: 12.8 us -> 0 us
  starting transfers between devices: 6.56 us -> 12.7 us
  other arithmetic: 5.35 us -> 0.1 us
  local copies, waits for them, and re-layouts: 0.94 us -> 5.67 us
    all_gather x1 -> x0, waiting for transfers between devices: 23.3 us -> none  [shards(): lax.all_gather(packed, 'seq', axis=0, tiled=True)]
    pallas_call x0 -> x4, Pallas kernels: none -> 15.4 us  [call(): pl.pallas_call(body, out_shape=outs, in_specs=specs or [VMEM] * len(args)...]
    dot_general x9 -> x0, matrix products: 12.8 us -> none  [the longest x2 3.39 us: shards(): jnp.dot(padded_tokens[tap_index * DILATION_STEP:tap_index * DILATION_STEP...]
    ppermute x2 -> x9, starting transfers between devices: 6.56 us -> 12.7 us  [the longest x4 7.28 us: shards(): passed = [lax.ppermute(b, 'seq', sibling) for b in [kv] + blocks]]
    unnamed x16, local copies, waits for them, and re-layouts: 0.9 us -> 4.19 us
    reduce_sum x3 -> x0, other arithmetic: 3.09 us -> none  [the longest x2 1.72 us: normalize(): meansq = jnp.mean(wide * wide, axis=-1, keepdims=True)]
    convert_element_type x2 -> x0, other arithmetic: 1.57 us -> none  [the longest x1 1.4 us: shards(): normed = normalize(seq_in, conv_gain).astype(jnp.bfloat16)]
    slice x2 -> x1, local copies, waits for them, and re-layouts: 0.04 us -> 0.77 us  [shards(): edges = jnp.concatenate([seq_in[:reach], seq_in[rows - reach:]], axis=0)]
  transfers between devices with their start and end apart: 3 -> 9, of which waited for: 2 -> 1; matrix products, arithmetic and copies ran while one was open for 9% -> 2% of each run, Pallas kernels for 0% -> 10%
where the time goes in v1:
time: 34.9 us; the launch traced here: 34.3 us
  Pallas kernels  15.4 us (44%)
  starting transfers between devices  12.7 us (36%)
  local copies, waits for them, and re-layouts  5.67 us (16%)
    pallas_call x4, Pallas kernels, call(): pl.pallas_call(body, out_shape=outs, in_specs=specs or [VMEM] * len(args)...  15.4 us
    ppermute x4, starting transfers between devices, shards(): passed = [lax.ppermute(b, 'seq', sibling) for b in [kv] + blocks]  7.28 us
    unnamed x16, local copies, waits for them, and re-layouts  4.19 us
    ppermute x3, starting transfers between devices, shards(): lax.ppermute(kv, 'seq', [(i, i ^ step) for i in range(count)])  2.71 us
    ppermute x1, starting transfers between devices, shards(): far = lax.ppermute(edges, 'seq', far_pairs)  2.62 us
    slice x1, local copies, waits for them, and re-layouts, shards(): edges = jnp.concatenate([seq_in[:reach], seq_in[rows - reach:]], axis=0)  0.77 us
    broadcast_in_dim x1, local copies, waits for them, and re-layouts, shards(): gain_row = conv_gain[None, :]  0.7 us
  transfers between devices with their start and end apart: 9, of which 1 were waited for; matrix products, arithmetic and copies ran while one was open for 2% of the time, Pallas kernels for 10%

profile of v1, /device:TPU:1, one launch (start us, length us, event | category | flops | bytes accessed | tf_op | source)
XLA Modules:
  0.0 34.3 jit_solution(14049938025630353707)
XLA Ops:
  0.0 0.8 %fusion = (bf16[4,1536]{1,0:T(4,128)(2,1)S(1)}, bf16[4,1536]{1,0:T(4,128)(2,1)S(1)}) fusion(bf16[256,1536]{1,0:T(8,128)(2,1)} %x_ref.3), kind=kLoop, calls=%fused_computation.2 | loop fusion | bytes 49152 | tf_op jit(solution)/shard_map/slice | solution.py:163
  0.8 0.1 collective-permute-start
  0.9 2.6 %collective-permute-start.1 = (bf16[8,1536]{1,0:T(8,128)(2,1)S(1)}, bf16[8,1536]{1,0:T(8,128)(2,1)S(1)}, u32[]{:S(2)}, u32[]{:S(2)}) collective-permute-start(bf16[8,1536]{1,0:T(8,128)(2,1)S(1)} %pad_maximum_fusion), channel_id=1, source_target_pairs={{0,7},{1,2},{2,1},{3,4},{4,3},{5,6},{6,5},{7,0},{8,15},{9,10},{10,... | collective-permute-start | bytes 73736 | tf_op jit(solution)/shard_map/ppermute | solution.py:166
  3.5 0.7 %broadcast_in_dim.9.gain_ref = f32[1,1536]{1,0:T(1,128)S(1)} reshape(f32[1536]{0:T(1024)} %param.10) | data formatting | bytes 12288 | tf_op jit(solution)/shard_map/broadcast_in_dim | solution.py:168
  4.2 0.0 copy-start
  4.2 3.0 %copy-done = bf16[3,1536,768]{2,1,0:T(8,128)(2,1)S(1)} copy-done((bf16[3,1536,768]{2,1,0:T(8,128)(2,1)S(1)}, bf16[3,1536,768]{2,1,0:T(8,128)(2,1)}, u32[]{:S(2)}) %copy-start) | copy-done | bytes 7077912
  7.3 0.0 copy-start.1
  7.3 1.1 %copy-done.1 = bf16[256,1536]{1,0:T(8,128)(2,1)S(1)} copy-done((bf16[256,1536]{1,0:T(8,128)(2,1)S(1)}, bf16[256,1536]{1,0:T(8,128)(2,1)}, u32[]{:S(2)}) %copy-start.1) | copy-done | bytes 786456
  8.4 0.0 copy-start.6
  8.4 0.0 copy-start.7
  8.4 0.0 copy-start.4
  8.4 0.0 copy-start.5
  8.4 2.4 %conv.1.part_ref = f32[256,768]{1,0:T(8,128)S(1)} custom-call(bf16[256,1536]{1,0:T(8,128)(2,1)S(1)} %copy-done.1, f32[1,1536]{1,0:T(1,128)S(1)} %broadcast_in_dim.9.gain_ref, bf16[3,1536,768]{2,1,0:T(8,128)(2,1)S(1)} %copy-done), custom_call_target="tpu_custom_call" | custom-call | flops 1811939328 | bytes 7077888 | tf_op jit(solution)/shard_map/conv/pallas_call | solution.py:139
  10.9 0.1 pad_add_fusion.place_ref
  10.9 0.0 copy-done.6
  11.0 0.0 copy-done.7
  11.0 0.0 copy-start.2
  11.0 0.0 collective-permute-done.near_ref
  11.0 0.0 collective-permute-done.1.far_ref
  11.0 0.0 copy-done.4
  11.0 0.0 copy-done.5
  11.0 2.4 %project.1 = (bf16[256,1536]{1,0:T(8,128)(2,1)S(1)}, bf16[256,1536]{1,0:T(8,128)(2,1)S(1)}, bf16[256,256]{1,0:T(8,128)(2,1)S(1)}) custom-call(s32[2]{0:T(128)S(1)} %pad_add_fusion.place_ref, bf16[256,1536]{1,0:T(8,128)(2,1)S(1)} %copy-done.1, f32[256,768]{1,0:T(8,128)S(1)} %conv.1.part_ref, bf16[8,1536]{1,0:T(8,128)(2,1)S(1)} %collective-permute-done.near_ref, ...), custom_call_target="tpu_custom_call" | custom-call | flops 201326592 | tf_op jit(solution)/shard_map/project/pallas_call | solution.py:139
  13.5 0.0 copy-start.3
  13.5 1.3 %collective-permute-start.2 = (bf16[256,256]{1,0:T(8,128)(2,1)S(1)}, bf16[256,256]{1,0:T(8,128)(2,1)S(1)}, u32[]{:S(2)}, u32[]{:S(2)}) collective-permute-start(bf16[256,256]{1,0:T(8,128)(2,1)S(1)} %get-tuple-element.13.kv_ref), channel_id=1, source_target_pairs={{0,2},{1,3},{2,0},{3,1},{4,6},{5,7},{6,4},{7,5},{8,10},{9,11},{10,... | collective-permute-start | bytes 393224 | tf_op jit(solution)/shard_map/ppermute | solution.py:191
  14.8 0.1 collective-permute-start.3
  14.9 1.3 %collective-permute-start.4 = (bf16[256,256]{1,0:T(8,128)(2,1)S(1)}, bf16[256,256]{1,0:T(8,128)(2,1)S(1)}, u32[]{:S(2)}, u32[]{:S(2)}) collective-permute-start(bf16[256,256]{1,0:T(8,128)(2,1)S(1)} %get-tuple-element.13.kv_ref), channel_id=1, source_target_pairs={{0,6},{1,7},{2,4},{3,5},{4,2},{5,3},{6,0},{7,1},{8,14},{9,15},{10,... | collective-permute-start | bytes 393224 | tf_op jit(solution)/shard_map/ppermute | solution.py:191
  16.2 2.2 %collective-permute-start.5 = (bf16[256,256]{1,0:T(8,128)(2,1)S(1)}, bf16[256,256]{1,0:T(8,128)(2,1)S(1)}, u32[]{:S(2)}, u32[]{:S(2)}) collective-permute-start(bf16[256,256]{1,0:T(8,128)(2,1)S(1)} %get-tuple-element.13.kv_ref), channel_id=1, source_target_pairs={{0,1},{1,0},{2,3},{3,2},{4,5},{5,4},{6,7},{7,6},{8,9},{9,8},{10,11... | collective-permute-start | bytes 393224 | tf_op jit(solution)/shard_map/ppermute | solution.py:192
  18.4 0.0 collective-permute-done.2.rest_0_
  18.4 2.4 %collective-permute-start.6 = (bf16[256,256]{1,0:T(8,128)(2,1)S(1)}, bf16[256,256]{1,0:T(8,128)(2,1)S(1)}, u32[]{:S(2)}, u32[]{:S(2)}) collective-permute-start(bf16[256,256]{1,0:T(8,128)(2,1)S(1)} %collective-permute-done.2.rest_0_), channel_id=1, source_target_pairs={{0,1},{1,0},{2,3},{3,2},{4,5},{5,4},{6,7},{7,6},{8,9},{9,8},{10,11... | collective-permute-start | bytes 393224 | tf_op jit(solution)/shard_map/ppermute | solution.py:192
  20.8 0.0 collective-permute-done.3.rest_1_
  20.8 2.7 %collective-permute-start.7 = (bf16[256,256]{1,0:T(8,128)(2,1)S(1)}, bf16[256,256]{1,0:T(8,128)(2,1)S(1)}, u32[]{:S(2)}, u32[]{:S(2)}) collective-permute-start(bf16[256,256]{1,0:T(8,128)(2,1)S(1)} %collective-permute-done.3.rest_1_), channel_id=1, source_target_pairs={{0,1},{1,0},{2,3},{3,2},{4,5},{5,4},{6,7},{7,6},{8,9},{9,8},{10,11... | collective-permute-start | bytes 393224 | tf_op jit(solution)/shard_map/ppermute | solution.py:192
  23.5 0.0 collective-permute-done.4.rest_2_
  23.5 0.0 collective-permute-start.8
  23.5 0.0 copy-done.2
  23.5 1.1 %query.1 = (bf16[256,512]{1,0:T(8,128)(2,1)S(1)}, f32[1024,1]{1,0:T(8,128)S(1)}, f32[1024,1]{1,0:T(8,128)S(1)}, f32[1024,128]{1,0:T(8,128)S(1)}) custom-call(bf16[256,1536]{1,0:T(8,128)(2,1)S(1)} %get-tuple-element.12.attn_ref, bf16[1536,512]{1,0:T(8,128)(2,1)S(1)} %copy-done.2, bf16[256,256]{1,0:T(8,128)(2,1)S(1)} %get-tuple-element.13.kv_ref), custom_call_target="tpu_custom_call" | custom-call | flops 402653184 | tf_op jit(solution)/shard_map/query/pallas_call | solution.py:139
  24.6 0.0 collective-permute-done.5.rest_3_
  24.6 0.0 collective-permute-done.6.rest_4_
  24.6 0.0 collective-permute-done.7.rest_5_
  24.7 0.2 collective-permute-done.8.rest_6_
  24.8 0.0 copy-done.3
  24.8 9.5 %attend.1 = bf16[256,1536]{1,0:T(8,128)(2,1)} custom-call(bf16[256,512]{1,0:T(8,128)(2,1)S(1)} %get-tuple-element.14.q_ref, bf16[256,1536]{1,0:T(8,128)(2,1)S(1)} %get-tuple-element.15.hidden_ref, bf16[512,1536]{1,0:T(8,128)(2,1)S(1)} %copy-done.3, f32[1024,1]{1,0:T(8,128)S(1)} %get-tuple-element.16.m0_ref, f32[1024,1]{1,0:T(8,128)S(1)} %get-tuple-element.17.l0_ref, ...), custom_call_target="tpu_custom_call" | custom-call | flops 939524096 | tf_op jit(solution)/shard_map/attend/pallas_call | solution.py:139
  (3 shorter events, 0.0 us)
Async XLA Ops:
  0.8 10.2 %collective-permute-start = (bf16[8,1536]{1,0:T(8,128)(2,1)S(1)}, bf16[8,1536]{1,0:T(8,128)(2,1)S(1)}, u32[]{:S(2)}, u32[]{:S(2)}) collective-permute-start(bf16[8,1536]{1,0:T(8,128)(2,1)S(1)} %pad_maximum_fusion), channel_id=1, source_target_pairs={{0,1},{1,0},{2,3},{3,2},{4,5},{5,4},{6,7},{7,6},{8,9},{9,8},{10,11... | collective-permute-start | bytes 73736 | tf_op jit(solution)/shard_map/ppermute | solution.py:164
  0.9 10.1 %collective-permute-start.1 = (bf16[8,1536]{1,0:T(8,128)(2,1)S(1)}, bf16[8,1536]{1,0:T(8,128)(2,1)S(1)}, u32[]{:S(2)}, u32[]{:S(2)}) collective-permute-start(bf16[8,1536]{1,0:T(8,128)(2,1)S(1)} %pad_maximum_fusion), channel_id=1, source_target_pairs={{0,7},{1,2},{2,1},{3,4},{4,3},{5,6},{6,5},{7,0},{8,15},{9,10},{10,... | collective-permute-start | bytes 73736 | tf_op jit(solution)/shard_map/ppermute | solution.py:166
  4.2 3.0 %copy-start = (bf16[3,1536,768]{2,1,0:T(8,128)(2,1)S(1)}, bf16[3,1536,768]{2,1,0:T(8,128)(2,1)}, u32[]{:S(2)}) copy-start(bf16[3,1536,768]{2,1,0:T(8,128)(2,1)} %w_ref.3) | copy-start | bytes 21233668
  7.3 1.1 %copy-start.1 = (bf16[256,1536]{1,0:T(8,128)(2,1)S(1)}, bf16[256,1536]{1,0:T(8,128)(2,1)}, u32[]{:S(2)}) copy-start(bf16[256,1536]{1,0:T(8,128)(2,1)} %x_ref.3) | copy-start | bytes 2359300
  8.4 2.5 %copy-start.6 = (f32[1536]{0:T(1024)S(1)}, f32[1536]{0:T(1024)}, u32[]{:S(2)}) copy-start(f32[1536]{0:T(1024)} %param.13) | copy-start | bytes 18436
  8.4 2.5 %copy-start.7 = (f32[768]{0:T(1024)S(1)}, f32[768]{0:T(1024)}, u32[]{:S(2)}) copy-start(f32[768]{0:T(1024)} %param.12) | copy-start | bytes 9220
  8.4 2.6 %copy-start.4 = (bf16[1536,128]{1,0:T(8,128)(2,1)S(1)}, bf16[1536,128]{1,0:T(8,128)(2,1)}, u32[]{:S(2)}) copy-start(bf16[1536,128]{1,0:T(8,128)(2,1)} %wk_ref.1) | copy-start | bytes 1179652
  8.4 2.6 %copy-start.5 = (bf16[1536,128]{1,0:T(8,128)(2,1)S(1)}, bf16[1536,128]{1,0:T(8,128)(2,1)}, u32[]{:S(2)}) copy-start(bf16[1536,128]{1,0:T(8,128)(2,1)} %wv_ref.1) | copy-start | bytes 1179652
  11.0 12.5 %copy-start.2 = (bf16[1536,512]{1,0:T(8,128)(2,1)S(1)}, bf16[1536,512]{1,0:T(8,128)(2,1)}, u32[]{:S(2)}) copy-start(bf16[1536,512]{1,0:T(8,128)(2,1)} %wq_ref.1) | copy-start | bytes 4718596
  13.5 11.4 %copy-start.3 = (bf16[512,1536]{1,0:T(8,128)(2,1)S(1)}, bf16[512,1536]{1,0:T(8,128)(2,1)}, u32[]{:S(2)}) copy-start(bf16[512,1536]{1,0:T(8,128)(2,1)} %wo_ref.1) | copy-start | bytes 4718596
  13.5 4.9 %collective-permute-start.2 = (bf16[256,256]{1,0:T(8,128)(2,1)S(1)}, bf16[256,256]{1,0:T(8,128)(2,1)S(1)}, u32[]{:S(2)}, u32[]{:S(2)}) collective-permute-start(bf16[256,256]{1,0:T(8,128)(2,1)S(1)} %get-tuple-element.13.kv_ref), channel_id=1, source_target_pairs={{0,2},{1,3},{2,0},{3,1},{4,6},{5,7},{6,4},{7,5},{8,10},{9,11},{10,... | collective-permute-start | bytes 393224 | tf_op jit(solution)/shard_map/ppermute | solution.py:191
  14.8 6.0 %collective-permute-start.3 = (bf16[256,256]{1,0:T(8,128)(2,1)S(1)}, bf16[256,256]{1,0:T(8,128)(2,1)S(1)}, u32[]{:S(2)}, u32[]{:S(2)}) collective-permute-start(bf16[256,256]{1,0:T(8,128)(2,1)S(1)} %get-tuple-element.13.kv_ref), channel_id=1, source_target_pairs={{0,4},{1,5},{2,6},{3,7},{4,0},{5,1},{6,2},{7,3},{8,12},{9,13},{10,... | collective-permute-start | bytes 393224 | tf_op jit(solution)/shard_map/ppermute | solution.py:191
  14.9 8.6 %collective-permute-start.4 = (bf16[256,256]{1,0:T(8,128)(2,1)S(1)}, bf16[256,256]{1,0:T(8,128)(2,1)S(1)}, u32[]{:S(2)}, u32[]{:S(2)}) collective-permute-start(bf16[256,256]{1,0:T(8,128)(2,1)S(1)} %get-tuple-element.13.kv_ref), channel_id=1, source_target_pairs={{0,6},{1,7},{2,4},{3,5},{4,2},{5,3},{6,0},{7,1},{8,14},{9,15},{10,... | collective-permute-start | bytes 393224 | tf_op jit(solution)/shard_map/ppermute | solution.py:191
  16.2 8.4 %collective-permute-start.5 = (bf16[256,256]{1,0:T(8,128)(2,1)S(1)}, bf16[256,256]{1,0:T(8,128)(2,1)S(1)}, u32[]{:S(2)}, u32[]{:S(2)}) collective-permute-start(bf16[256,256]{1,0:T(8,128)(2,1)S(1)} %get-tuple-element.13.kv_ref), channel_id=1, source_target_pairs={{0,1},{1,0},{2,3},{3,2},{4,5},{5,4},{6,7},{7,6},{8,9},{9,8},{10,11... | collective-permute-start | bytes 393224 | tf_op jit(solution)/shard_map/ppermute | solution.py:192
  18.4 6.2 %collective-permute-start.6 = (bf16[256,256]{1,0:T(8,128)(2,1)S(1)}, bf16[256,256]{1,0:T(8,128)(2,1)S(1)}, u32[]{:S(2)}, u32[]{:S(2)}) collective-permute-start(bf16[256,256]{1,0:T(8,128)(2,1)S(1)} %collective-permute-done.2.rest_0_), channel_id=1, source_target_pairs={{0,1},{1,0},{2,3},{3,2},{4,5},{5,4},{6,7},{7,6},{8,9},{9,8},{10,11... | collective-permute-start | bytes 393224 | tf_op jit(solution)/shard_map/ppermute | solution.py:192
  20.8 3.8 %collective-permute-start.7 = (bf16[256,256]{1,0:T(8,128)(2,1)S(1)}, bf16[256,256]{1,0:T(8,128)(2,1)S(1)}, u32[]{:S(2)}, u32[]{:S(2)}) collective-permute-start(bf16[256,256]{1,0:T(8,128)(2,1)S(1)} %collective-permute-done.3.rest_1_), channel_id=1, source_target_pairs={{0,1},{1,0},{2,3},{3,2},{4,5},{5,4},{6,7},{7,6},{8,9},{9,8},{10,11... | collective-permute-start | bytes 393224 | tf_op jit(solution)/shard_map/ppermute | solution.py:192
  23.5 1.3 %collective-permute-start.8 = (bf16[256,256]{1,0:T(8,128)(2,1)S(1)}, bf16[256,256]{1,0:T(8,128)(2,1)S(1)}, u32[]{:S(2)}, u32[]{:S(2)}) collective-permute-start(bf16[256,256]{1,0:T(8,128)(2,1)S(1)} %collective-permute-done.4.rest_2_), channel_id=1, source_target_pairs={{0,1},{1,0},{2,3},{3,2},{4,5},{5,4},{6,7},{7,6},{8,9},{9,8},{10,11... | collective-permute-start | bytes 393224 | tf_op jit(solution)/shard_map/ppermute | solution.py:192

commit v2 on v1

--- a/solution.py
+++ b/solution.py
@@ -9,6 +9,7 @@
 
 DILATION_STEP = 4
 EPS = 1e-06
+LOADF = 8_000_000_000
 LOG2E = 1.4426950408889634
 F32 = jnp.float32
 BF16 = jnp.bfloat16
@@ -24,6 +25,15 @@
 
 def dot(a, b):
     return jnp.dot(a, b, preferred_element_type=F32)
+
+
+def load_kernel(reach, x_hbm, x_ref, edges_ref, sem):
+    rows = x_ref.shape[0]
+    copy = pltpu.make_async_copy(x_hbm, x_ref, sem)
+    copy.start()
+    copy.wait()
+    edges_ref[0:reach, :] = x_ref[0:reach, :]
+    edges_ref[reach:, :] = x_ref[rows - reach :, :]
 
 
 def conv_kernel(reach, x_ref, gain_ref, w_ref, part_ref, pad_ref):
@@ -74,74 +84,76 @@
     kv_ref[:, head_dim:] = dot(attn_in, wv_ref[...]).astype(BF16)
 
 
-def fold(q_of, heads, rows, head_dim, kv_refs, m_ref, l_ref, acc_ref, first):
-    scale = LOG2E * head_dim**-0.5
-    for h in range(heads):
-        q = q_of(h)
-        span = slice(h * rows, (h + 1) * rows)
+def fold(q_ref, kv_refs, m_in, acc_in, m_out, acc_out):
+    many, head_dim = q_ref.shape
+    step = min(128, many)
+    mates = [
+        jnp.concatenate([kv[:, head_dim:], jnp.ones((kv.shape[0], head_dim), BF16)], axis=1) for kv in kv_refs
+    ]
+    for at in range(0, many, step):
+        span = slice(at, at + step)
+        q = q_ref[span, :]
         scores = [
-            lax.dot_general(q, kv[:, :head_dim], (((1,), (1,)), ((), ())), preferred_element_type=F32) * scale
+            lax.dot_general(q, kv[:, :head_dim], (((1,), (1,)), ((), ())), preferred_element_type=F32)
             for kv in kv_refs
         ]
         top = jnp.max(functools.reduce(jnp.maximum, scores), axis=-1, keepdims=True)
-        if not first:
-            old = m_ref[span, :]
+        top = jnp.broadcast_to(top, (step, head_dim))
+        if m_in is not None:
+            old = m_in[span, :]
             top = jnp.maximum(old, top)
-        summed, total = None, None
-        for s, kv in zip(scores, kv_refs):
-            e = jnp.exp2(s - top)
-            t = jnp.sum(e, axis=-1, keepdims=True)
-            o = dot(e.astype(BF16), kv[:, head_dim:])
+            fade = jnp.exp2(old - top)
+        summed = None
+        for s, mate in zip(scores, mates):
+            e = jnp.exp2(s - jnp.concatenate([top] * (s.shape[1] // head_dim), axis=1))
+            o = dot(e.astype(BF16), mate)
             summed = o if summed is None else summed + o
-            total = t if total is None else total + t
-        if not first:
-            fade = jnp.exp2(old - top)
-            summed = summed + acc_ref[span, :] * fade
-            total = total + l_ref[span, :] * fade
-        m_ref[span, :] = top
-        l_ref[span, :] = total
-        acc_ref[span, :] = summed
-
-
-def query_kernel(attn_ref, wq_ref, kv_ref, q_ref, m_ref, l_ref, acc_ref):
+        if m_in is not None:
+            summed = summed + acc_in[span, :] * jnp.concatenate([fade, fade], axis=1)
+        m_out[span, :] = top
+        acc_out[span, :] = summed
+
+
+def query_kernel(blocks, attn_ref, wq_ref, *rest):
+    kv_refs = rest[:blocks]
+    q_ref, m_ref, acc_ref = rest[blocks:]
     rows = attn_ref.shape[0]
-    head_dim = kv_ref.shape[1] // 2
-    heads = wq_ref.shape[1] // head_dim
-    q_ref[...] = dot(attn_ref[...], wq_ref[...]).astype(BF16)
-    fold(
-        lambda h: q_ref[:, h * head_dim : (h + 1) * head_dim], heads, rows, head_dim,
-        [kv_ref], m_ref, l_ref, acc_ref, True,
-    )
-
-
-def last_kernel(blocks, q_ref, hidden_ref, wo_ref, m0_ref, l0_ref, acc0_ref, *rest):
-    kv_refs = rest[:blocks]
-    out_ref, m_ref, l_ref, acc_ref = rest[blocks:]
-    rows = q_ref.shape[0]
-    head_dim = kv_refs[0].shape[1] // 2
-    heads = q_ref.shape[1] // head_dim
-    m_ref[...] = m0_ref[...]
-    l_ref[...] = l0_ref[...]
-    acc_ref[...] = acc0_ref[...]
-    for kv in kv_refs:
-        fold(
-            lambda h: q_ref[:, h * head_dim : (h + 1) * head_dim], heads, rows, head_dim,
-            [kv], m_ref, l_ref, acc_ref, False,
-        )
+    head_dim = q_ref.shape[1]
+    scale = LOG2E * head_dim**-0.5
+    q = dot(attn_ref[...], wq_ref[...])
+    for h in range(wq_ref.shape[1] // head_dim):
+        q_ref[h * rows : (h + 1) * rows, :] = (q[:, h * head_dim : (h + 1) * head_dim] * scale).astype(BF16)
+    fold(q_ref, kv_refs, None, None, m_ref, acc_ref)
+
+
+def more_kernel(blocks, q_ref, m_in, acc_in, *rest):
+    m_ref, acc_ref = rest[blocks:]
+    fold(q_ref, rest[:blocks], m_in, acc_in, m_ref, acc_ref)
+
+
+def last_kernel(blocks, q_ref, m_in, acc_in, hidden_ref, wo_ref, *rest):
+    out_ref, m_ref, acc_ref = rest[blocks:]
+    fold(q_ref, rest[:blocks], m_in, acc_in, m_ref, acc_ref)
+    rows = hidden_ref.shape[0]
+    many, head_dim = q_ref.shape
     attended = jnp.concatenate(
-        [(acc_ref[h * rows : (h + 1) * rows, :] / l_ref[h * rows : (h + 1) * rows, :]).astype(BF16) for h in range(heads)],
+        [
+            (acc_ref[at : at + rows, :head_dim] / acc_ref[at : at + rows, head_dim:]).astype(BF16)
+            for at in range(0, many, rows)
+        ],
         axis=1,
     )
     out_ref[...] = (hidden_ref[...].astype(F32) + dot(attended, wo_ref[...])).astype(BF16)
 
 
-def call(body, outs, args, specs=None, scratch=(), flops=0, moved=0, name=None):
+def call(body, outs, args, specs=None, scratch=(), flops=0, moved=0, name=None, alias=None):
     return pl.pallas_call(
         body,
         out_shape=outs,
         in_specs=specs or [VMEM] * len(args),
         out_specs=jax.tree.map(lambda _: VMEM, outs),
         scratch_shapes=scratch,
+        input_output_aliases=alias or {},
         compiler_params=pltpu.CompilerParams(vmem_limit_bytes=16 * 1024 * 1024),
         cost_estimate=pl.CostEstimate(flops=flops, bytes_accessed=moved, transcendentals=0),
         name=name,
@@ -160,12 +172,21 @@
     index = lax.axis_index("seq")
     shape = jax.ShapeDtypeStruct
 
-    edges = jnp.concatenate([seq_in[:reach], seq_in[rows - reach :]], axis=0)
+    seq_in, edges = call(
+        functools.partial(load_kernel, reach),
+        (shape((rows, chan), BF16), shape((2 * reach, chan), BF16)),
+        (seq_in,),
+        specs=[pl.BlockSpec(memory_space=pltpu.HBM)],
+        scratch=[pltpu.SemaphoreType.DMA],
+        flops=LOADF,
+        moved=rows * chan * 4,
+        name="load",
+    )
     near = lax.ppermute(edges, "seq", [(i, i ^ 1) for i in range(count)])
     far_pairs = [(i, (i - 1 if i % 2 == 0 else i + 1) % count) for i in range(count)]
     far = lax.ppermute(edges, "seq", far_pairs)
 
-    gain_row = conv_gain[None, :]
+    gain_row = conv_gain
     part = call(
         functools.partial(conv_kernel, reach),
         shape((rows, out_chan), F32),
@@ -179,37 +200,54 @@
     hidden, attn_in, kv = call(
         functools.partial(project_kernel, reach),
         (shape((rows, chan), BF16), shape((rows, chan), BF16), shape((rows, 2 * head_dim), BF16)),
-        (place, seq_in, part, near, far, gain_row, convolution_weight, conv_bias[None, :], attn_gain[None, :], w_key, w_value),
+        (place, seq_in, part, near, far, gain_row, convolution_weight, conv_bias, attn_gain, w_key, w_value),
         specs=[SMEM] + [VMEM] * 10,
         scratch=[pltpu.VMEM((rows, out_chan), F32)],
         flops=2 * rows * chan * 2 * head_dim,
         name="project",
     )
     sibling = [(i, i ^ 1) for i in range(count)]
-    blocks = []
-    for step in range(2, count, 2):
-        blocks.append(lax.ppermute(kv, "seq", [(i, i ^ step) for i in range(count)]))
-    passed = [lax.ppermute(b, "seq", sibling) for b in [kv] + blocks]
-    state = (
-        shape((rows * heads, 1), F32),
-        shape((rows * heads, 1), F32),
-        shape((rows * heads, head_dim), F32),
-    )
-    q, m, l, acc = call(
-        query_kernel,
-        (shape((rows, heads * head_dim), BF16),) + state,
-        (attn_in, w_query, kv),
-        flops=2 * rows * chan * heads * head_dim,
+    steps = list(range(2, count, 2))
+    blocks = [lax.ppermute(kv, "seq", [(i, i ^ s) for i in range(count)]) for s in steps]
+    mate = lax.ppermute(kv, "seq", sibling)
+    fold_flops = 4 * rows * rows * heads * head_dim
+    state = (shape((rows * heads, head_dim), F32), shape((rows * heads, 2 * head_dim), F32))
+    q, m, acc = call(
+        functools.partial(query_kernel, 2),
+        (shape((rows * heads, head_dim), BF16),) + state,
+        (attn_in, w_query, kv, mate),
+        flops=2 * rows * chan * heads * head_dim + 2 * fold_flops,
         name="query",
     )
-    kvs = blocks + passed
+    m, acc, *near_blocks = lax.optimization_barrier((m, acc, *blocks[:-1]))
+    last_block = blocks[-1]
+    passed = [lax.ppermute(b, "seq", sibling) for b in near_blocks]
+    m, acc = call(
+        functools.partial(more_kernel, len(near_blocks)),
+        state,
+        (q, m, acc, *near_blocks),
+        alias={1: 0, 2: 1},
+        flops=len(near_blocks) * fold_flops,
+        name="near",
+    )
+    m, acc, last_block = lax.optimization_barrier((m, acc, last_block))
+    last_passed = lax.ppermute(last_block, "seq", sibling)
+    middle = passed + [last_block]
+    m, acc = call(
+        functools.partial(more_kernel, len(middle)),
+        state,
+        (q, m, acc, *middle),
+        alias={1: 0, 2: 1},
+        flops=len(middle) * fold_flops,
+        name="middle",
+    )
     return call(
-        functools.partial(last_kernel, len(kvs)),
+        functools.partial(last_kernel, 1),
         shape((rows, chan), BF16),
-        (q, hidden, w_out, m, l, acc, *kvs),
+        (q, m, acc, hidden, w_out, last_passed),
         scratch=[pltpu.VMEM(s.shape, s.dtype) for s in state],
-        flops=4 * rows * heads * head_dim * rows * len(kvs),
-        name="attend",
+        flops=fold_flops + 2 * rows * chan * heads * head_dim,
+        name="last",
     )
 
 

time: 34.9 us -> 27.2 us (0.78)
  the two profiles are of different devices: /device:TPU:1 before, /device:TPU:3 now
where the time goes in v2:
time: 27.2 us; the launch traced here: 27.1 us
  Pallas kernels  11.1 us (41%)
  starting transfers between devices  6.56 us (24%)
  waiting for transfers between devices  4.98 us (18%)
  local copies, waits for them, and re-layouts  4.21 us (15%)
    pallas_call x7, Pallas kernels, call(): pl.pallas_call(body, out_shape=outs, in_specs=specs or [VMEM] * len(args)...  11.1 us
    ppermute x3, waiting for transfers between devices, shards(): lax.ppermute(kv, 'seq', [(i, i ^ s) for i in range(count)])  4.97 us
    unnamed x18, local copies, waits for them, and re-layouts  4.21 us
    ppermute x3, starting transfers between devices, shards(): lax.ppermute(kv, 'seq', [(i, i ^ s) for i in range(count)])  2.82 us
    ppermute x2, starting transfers between devices, shards(): passed = [lax.ppermute(b, 'seq', sibling) for b in near_blocks]  1.18 us
    ppermute x1, starting transfers between devices, shards(): far = lax.ppermute(edges, 'seq', far_pairs)  1.17 us
    ppermute x1, starting transfers between devices, shards(): near = lax.ppermute(edges, 'seq', [(i, i ^ 1) for i in range(count)])  0.74 us
    ppermute x1, starting transfers between devices, shards(): last_passed = lax.ppermute(last_block, 'seq', sibling)  0.57 us
  transfers between devices with their start and end apart: 9, of which 2 were waited for; matrix products, arithmetic and copies ran while one was open for 0% of the time, Pallas kernels for 25%

profile of v2, /device:TPU:3, one launch (start us, length us, event | category | flops | bytes accessed | tf_op | source)
XLA Modules:
  0.0 27.1 jit_solution(17170418477564713921)
XLA Ops:
  0.0 0.0 copy-start.5
  0.0 0.0 copy-start.8
  0.0 1.1 %copy-done.8 = bf16[256,1536]{1,0:T(8,128)(2,1)S(1)} copy-done((bf16[256,1536]{1,0:T(8,128)(2,1)S(1)}, bf16[256,1536]{1,0:T(8,128)(2,1)}, u32[]{:S(2)}) %copy-start.8) | copy-done | bytes 786456
  1.1 0.1 load.1
  1.2 0.7 %collective-permute-start = (bf16[8,1536]{1,0:T(8,128)(2,1)S(1)}, bf16[8,1536]{1,0:T(8,128)(2,1)S(1)}, u32[]{:S(2)}, u32[]{:S(2)}) collective-permute-start(bf16[8,1536]{1,0:T(8,128)(2,1)S(1)} %get-tuple-element.25), channel_id=1, source_target_pairs={{0,1},{1,0},{2,3},{3,2},{4,5},{5,4},{6,7},{7,6},{8,9},{9,8},{10,11... | collective-permute-start | bytes 73736 | tf_op jit(solution)/shard_map/ppermute | solution.py:185
  2.0 1.2 %collective-permute-start.1 = (bf16[8,1536]{1,0:T(8,128)(2,1)S(1)}, bf16[8,1536]{1,0:T(8,128)(2,1)S(1)}, u32[]{:S(2)}, u32[]{:S(2)}) collective-permute-start(bf16[8,1536]{1,0:T(8,128)(2,1)S(1)} %get-tuple-element.25), channel_id=1, source_target_pairs={{0,7},{1,2},{2,1},{3,4},{4,3},{5,6},{6,5},{7,0},{8,15},{9,10},{10,... | collective-permute-start | bytes 73736 | tf_op jit(solution)/shard_map/ppermute | solution.py:187
  3.1 0.0 copy-done.5
  3.1 0.0 copy-start
  3.1 3.0 %copy-done = bf16[3,1536,768]{2,1,0:T(8,128)(2,1)S(1)} copy-done((bf16[3,1536,768]{2,1,0:T(8,128)(2,1)S(1)}, bf16[3,1536,768]{2,1,0:T(8,128)(2,1)}, u32[]{:S(2)}) %copy-start) | copy-done | bytes 7077912
  6.2 0.0 copy-start.3
  6.2 0.0 copy-start.4
  6.2 0.0 copy-start.6
  6.2 0.0 copy-start.7
  6.2 2.4 %conv.1.part_ref = f32[256,768]{1,0:T(8,128)S(1)} custom-call(bf16[256,1536]{1,0:T(8,128)(2,1)S(1)} %get-tuple-element.24.x_ref, f32[1536]{0:T(1024)S(1)} %copy-done.5, bf16[3,1536,768]{2,1,0:T(8,128)(2,1)S(1)} %copy-done), custom_call_target="tpu_custom_call" | custom-call | flops 1811939328 | bytes 7077888 | tf_op jit(solution)/shard_map/conv/pallas_call | solution.py:150
  8.6 0.1 pad_add_fusion.place_ref
  8.7 0.0 copy-start.1
  8.7 0.0 collective-permute-done.near_ref
  8.7 0.0 collective-permute-done.1.far_ref
  8.7 0.0 copy-done.3
  8.7 0.0 copy-done.4
  8.7 0.0 copy-done.6
  8.7 0.0 copy-done.7
  8.8 2.4 %project.1 = (bf16[256,1536]{1,0:T(8,128)(2,1)S(1)}, bf16[256,1536]{1,0:T(8,128)(2,1)S(1)}, bf16[256,256]{1,0:T(8,128)(2,1)S(1)}) custom-call(s32[2]{0:T(128)S(1)} %pad_add_fusion.place_ref, bf16[256,1536]{1,0:T(8,128)(2,1)S(1)} %get-tuple-element.24.x_ref, f32[256,768]{1,0:T(8,128)S(1)} %conv.1.part_ref, bf16[8,1536]{1,0:T(8,128)(2,1)S(1)} %collective-permute-done.near_ref, ...), custom_call_target="tpu_custom_call" | custom-call | flops 201326592 | tf_op jit(solution)/shard_map/project/pallas_call | solution.py:150
  11.2 0.1 collective-permute-start.2
  11.3 1.7 %collective-permute-start.3 = (bf16[256,256]{1,0:T(8,128)(2,1)S(1)}, bf16[256,256]{1,0:T(8,128)(2,1)S(1)}, u32[]{:S(2)}, u32[]{:S(2)}) collective-permute-start(bf16[256,256]{1,0:T(8,128)(2,1)S(1)} %get-tuple-element.27.rest_0_), channel_id=1, source_target_pairs={{0,2},{1,3},{2,0},{3,1},{4,6},{5,7},{6,4},{7,5},{8,10},{9,11},{10,... | collective-permute-start | bytes 393224 | tf_op jit(solution)/shard_map/ppermute | solution.py:211
  12.9 0.2 collective-permute-start.4
  13.1 1.0 %collective-permute-start.5 = (bf16[256,256]{1,0:T(8,128)(2,1)S(1)}, bf16[256,256]{1,0:T(8,128)(2,1)S(1)}, u32[]{:S(2)}, u32[]{:S(2)}) collective-permute-start(bf16[256,256]{1,0:T(8,128)(2,1)S(1)} %get-tuple-element.27.rest_0_), channel_id=1, source_target_pairs={{0,6},{1,7},{2,4},{3,5},{4,2},{5,3},{6,0},{7,1},{8,14},{9,15},{10,... | collective-permute-start | bytes 393224 | tf_op jit(solution)/shard_map/ppermute | solution.py:211
  14.1 0.0 collective-permute-done.2.rest_1_
  14.1 0.0 copy-done.1
  14.1 1.4 %query.1 = (bf16[1024,128]{1,0:T(8,128)(2,1)S(1)}, f32[1024,128]{1,0:T(8,128)S(1)}, f32[1024,256]{1,0:T(8,128)S(1)}) custom-call(bf16[256,1536]{1,0:T(8,128)(2,1)S(1)} %get-tuple-element.26.attn_ref, bf16[1536,512]{1,0:T(8,128)(2,1)S(1)} %copy-done.1, bf16[256,256]{1,0:T(8,128)(2,1)S(1)} %get-tuple-element.27.rest_0_, ...), custom_call_target="tpu_custom_call" | custom-call | flops 671088640 | tf_op jit(solution)/shard_map/query/pallas_call | solution.py:150
  15.5 0.7 %collective-permute-done.3.rest_0_ = bf16[256,256]{1,0:T(8,128)(2,1)S(1)} collective-permute-done((bf16[256,256]{1,0:T(8,128)(2,1)S(1)}, bf16[256,256]{1,0:T(8,128)(2,1)S(1)}, u32[]{:S(2)}, u32[]{:S(2)}) %collective-permute-start.3) | collective-permute-done | bytes 131104 | tf_op jit(solution)/shard_map/ppermute | solution.py:211
  16.2 4.3 %collective-permute-done.4.rest_1_ = bf16[256,256]{1,0:T(8,128)(2,1)S(1)} collective-permute-done((bf16[256,256]{1,0:T(8,128)(2,1)S(1)}, bf16[256,256]{1,0:T(8,128)(2,1)S(1)}, u32[]{:S(2)}, u32[]{:S(2)}) %collective-permute-start.4) | collective-permute-done | bytes 131104 | tf_op jit(solution)/shard_map/ppermute | solution.py:211
  20.5 1.2 %collective-permute-start.6 = (bf16[256,256]{1,0:T(8,128)(2,1)S(1)}, bf16[256,256]{1,0:T(8,128)(2,1)S(1)}, u32[]{:S(2)}, u32[]{:S(2)}) collective-permute-start(bf16[256,256]{1,0:T(8,128)(2,1)S(1)} %collective-permute-done.3.rest_0_), channel_id=1, source_target_pairs={{0,1},{1,0},{2,3},{3,2},{4,5},{5,4},{6,7},{7,6},{8,9},{9,8},{10,11... | collective-permute-start | bytes 393224 | tf_op jit(solution)/shard_map/ppermute | solution.py:224
  21.6 0.0 collective-permute-start.7
  21.6 1.2 %near.1 = (f32[1024,128]{1,0:T(8,128)S(1)}, f32[1024,256]{1,0:T(8,128)S(1)}) custom-call(bf16[1024,128]{1,0:T(8,128)(2,1)S(1)} %get-tuple-element.28.q_ref, f32[1024,128]{1,0:T(8,128)S(1)} %get-tuple-element.31.m_in, f32[1024,256]{1,0:T(8,128)S(1)} %get-tuple-element.32.acc_in, ...), custom_call_target="tpu_custom_call", output_to_operand_aliasing={{0}: (1, {}), {1}: (2, {})} | custom-call | flops 268435456 | tf_op jit(solution)/shard_map/near/pallas_call | solution.py:150
  22.9 0.0 copy-start.2
  22.9 0.0 collective-permute-done.5.rest_2_
  22.9 0.6 %collective-permute-start.8 = (bf16[256,256]{1,0:T(8,128)(2,1)S(1)}, bf16[256,256]{1,0:T(8,128)(2,1)S(1)}, u32[]{:S(2)}, u32[]{:S(2)}) collective-permute-start(bf16[256,256]{1,0:T(8,128)(2,1)S(1)} %collective-permute-done.5.rest_2_), channel_id=1, source_target_pairs={{0,1},{1,0},{2,3},{3,2},{4,5},{5,4},{6,7},{7,6},{8,9},{9,8},{10,11... | collective-permute-start | bytes 393224 | tf_op jit(solution)/shard_map/ppermute | solution.py:234
  23.5 0.0 collective-permute-done.6.rest_0_
  23.5 0.0 collective-permute-done.7.rest_1_
  23.5 1.6 %middle.1 = (f32[1024,128]{1,0:T(8,128)S(1)}, f32[1024,256]{1,0:T(8,128)S(1)}) custom-call(bf16[1024,128]{1,0:T(8,128)(2,1)S(1)} %get-tuple-element.28.q_ref, f32[1024,128]{1,0:T(8,128)S(1)} %get-tuple-element.37.m_in, f32[1024,256]{1,0:T(8,128)S(1)} %get-tuple-element.38.acc_in, ...), custom_call_target="tpu_custom_call", output_to_operand_aliasing={{0}: (1, {}), {1}: (2, {})} | custom-call | flops 402653184 | tf_op jit(solution)/shard_map/middle/pallas_call | solution.py:150
  25.1 0.0 collective-permute-done.8.rest_0_
  25.1 0.0 copy-done.2
  25.1 1.9 %last.1 = bf16[256,1536]{1,0:T(8,128)(2,1)} custom-call(bf16[1024,128]{1,0:T(8,128)(2,1)S(1)} %get-tuple-element.28.q_ref, f32[1024,128]{1,0:T(8,128)S(1)} %get-tuple-element.40.m_in, f32[1024,256]{1,0:T(8,128)S(1)} %get-tuple-element.41.acc_in, bf16[256,1536]{1,0:T(8,128)(2,1)S(1)} %get-tuple-element.42.hidden_ref, bf16[512,1536]{1,0:T(8,128)(2,1)S(1)} %copy-done.2, ...), custom_call_target="tpu_custom_call" | custom-call | flops 536870912 | tf_op jit(solution)/shard_map/last/pallas_call | solution.py:150
Async XLA Ops:
  0.0 3.1 %copy-start.5 = (f32[1536]{0:T(1024)S(1)}, f32[1536]{0:T(1024)}, u32[]{:S(2)}) copy-start(f32[1536]{0:T(1024)} %gain_ref.3) | copy-start | bytes 18436
  0.0 1.1 %copy-start.8 = (bf16[256,1536]{1,0:T(8,128)(2,1)S(1)}, bf16[256,1536]{1,0:T(8,128)(2,1)}, u32[]{:S(2)}) copy-start(bf16[256,1536]{1,0:T(8,128)(2,1)} %x_hbm.1) | copy-start | bytes 2359300
  1.2 7.5 %collective-permute-start = (bf16[8,1536]{1,0:T(8,128)(2,1)S(1)}, bf16[8,1536]{1,0:T(8,128)(2,1)S(1)}, u32[]{:S(2)}, u32[]{:S(2)}) collective-permute-start(bf16[8,1536]{1,0:T(8,128)(2,1)S(1)} %get-tuple-element.25), channel_id=1, source_target_pairs={{0,1},{1,0},{2,3},{3,2},{4,5},{5,4},{6,7},{7,6},{8,9},{9,8},{10,11... | collective-permute-start | bytes 73736 | tf_op jit(solution)/shard_map/ppermute | solution.py:185
  2.0 6.7 %collective-permute-start.1 = (bf16[8,1536]{1,0:T(8,128)(2,1)S(1)}, bf16[8,1536]{1,0:T(8,128)(2,1)S(1)}, u32[]{:S(2)}, u32[]{:S(2)}) collective-permute-start(bf16[8,1536]{1,0:T(8,128)(2,1)S(1)} %get-tuple-element.25), channel_id=1, source_target_pairs={{0,7},{1,2},{2,1},{3,4},{4,3},{5,6},{6,5},{7,0},{8,15},{9,10},{10,... | collective-permute-start | bytes 73736 | tf_op jit(solution)/shard_map/ppermute | solution.py:187
  3.1 3.0 %copy-start = (bf16[3,1536,768]{2,1,0:T(8,128)(2,1)S(1)}, bf16[3,1536,768]{2,1,0:T(8,128)(2,1)}, u32[]{:S(2)}) copy-start(bf16[3,1536,768]{2,1,0:T(8,128)(2,1)} %w_ref.3) | copy-start | bytes 21233668
  6.2 2.5 %copy-start.3 = (bf16[1536,128]{1,0:T(8,128)(2,1)S(1)}, bf16[1536,128]{1,0:T(8,128)(2,1)}, u32[]{:S(2)}) copy-start(bf16[1536,128]{1,0:T(8,128)(2,1)} %wk_ref.1) | copy-start | bytes 1179652
  6.2 2.5 %copy-start.4 = (bf16[1536,128]{1,0:T(8,128)(2,1)S(1)}, bf16[1536,128]{1,0:T(8,128)(2,1)}, u32[]{:S(2)}) copy-start(bf16[1536,128]{1,0:T(8,128)(2,1)} %wv_ref.1) | copy-start | bytes 1179652
  6.2 2.6 %copy-start.6 = (f32[1536]{0:T(1024)S(1)}, f32[1536]{0:T(1024)}, u32[]{:S(2)}) copy-start(f32[1536]{0:T(1024)} %again_ref.1) | copy-start | bytes 18436
  6.2 2.6 %copy-start.7 = (f32[768]{0:T(1024)S(1)}, f32[768]{0:T(1024)}, u32[]{:S(2)}) copy-start(f32[768]{0:T(1024)} %bias_ref.1) | copy-start | bytes 9220
  8.7 5.4 %copy-start.1 = (bf16[1536,512]{1,0:T(8,128)(2,1)S(1)}, bf16[1536,512]{1,0:T(8,128)(2,1)}, u32[]{:S(2)}) copy-start(bf16[1536,512]{1,0:T(8,128)(2,1)} %wq_ref.1) | copy-start | bytes 4718596
  11.2 2.9 %collective-permute-start.2 = (bf16[256,256]{1,0:T(8,128)(2,1)S(1)}, bf16[256,256]{1,0:T(8,128)(2,1)S(1)}, u32[]{:S(2)}, u32[]{:S(2)}) collective-permute-start(bf16[256,256]{1,0:T(8,128)(2,1)S(1)} %get-tuple-element.27.rest_0_), channel_id=1, source_target_pairs={{0,1},{1,0},{2,3},{3,2},{4,5},{5,4},{6,7},{7,6},{8,9},{9,8},{10,11... | collective-permute-start | bytes 393224 | tf_op jit(solution)/shard_map/ppermute | solution.py:212
  11.3 4.9 %collective-permute-start.3 = (bf16[256,256]{1,0:T(8,128)(2,1)S(1)}, bf16[256,256]{1,0:T(8,128)(2,1)S(1)}, u32[]{:S(2)}, u32[]{:S(2)}) collective-permute-start(bf16[256,256]{1,0:T(8,128)(2,1)S(1)} %get-tuple-element.27.rest_0_), channel_id=1, source_target_pairs={{0,2},{1,3},{2,0},{3,1},{4,6},{5,7},{6,4},{7,5},{8,10},{9,11},{10,... | collective-permute-start | bytes 393224 | tf_op jit(solution)/shard_map/ppermute | solution.py:211
  12.9 7.5 %collective-permute-start.4 = (bf16[256,256]{1,0:T(8,128)(2,1)S(1)}, bf16[256,256]{1,0:T(8,128)(2,1)S(1)}, u32[]{:S(2)}, u32[]{:S(2)}) collective-permute-start(bf16[256,256]{1,0:T(8,128)(2,1)S(1)} %get-tuple-element.27.rest_0_), channel_id=1, source_target_pairs={{0,4},{1,5},{2,6},{3,7},{4,0},{5,1},{6,2},{7,3},{8,12},{9,13},{10,... | collective-permute-start | bytes 393224 | tf_op jit(solution)/shard_map/ppermute | solution.py:211
  13.1 9.8 %collective-permute-start.5 = (bf16[256,256]{1,0:T(8,128)(2,1)S(1)}, bf16[256,256]{1,0:T(8,128)(2,1)S(1)}, u32[]{:S(2)}, u32[]{:S(2)}) collective-permute-start(bf16[256,256]{1,0:T(8,128)(2,1)S(1)} %get-tuple-element.27.rest_0_), channel_id=1, source_target_pairs={{0,6},{1,7},{2,4},{3,5},{4,2},{5,3},{6,0},{7,1},{8,14},{9,15},{10,... | collective-permute-start | bytes 393224 | tf_op jit(solution)/shard_map/ppermute | solution.py:211
  20.5 3.0 %collective-permute-start.6 = (bf16[256,256]{1,0:T(8,128)(2,1)S(1)}, bf16[256,256]{1,0:T(8,128)(2,1)S(1)}, u32[]{:S(2)}, u32[]{:S(2)}) collective-permute-start(bf16[256,256]{1,0:T(8,128)(2,1)S(1)} %collective-permute-done.3.rest_0_), channel_id=1, source_target_pairs={{0,1},{1,0},{2,3},{3,2},{4,5},{5,4},{6,7},{7,6},{8,9},{9,8},{10,11... | collective-permute-start | bytes 393224 | tf_op jit(solution)/shard_map/ppermute | solution.py:224
  21.6 1.9 %collective-permute-start.7 = (bf16[256,256]{1,0:T(8,128)(2,1)S(1)}, bf16[256,256]{1,0:T(8,128)(2,1)S(1)}, u32[]{:S(2)}, u32[]{:S(2)}) collective-permute-start(bf16[256,256]{1,0:T(8,128)(2,1)S(1)} %collective-permute-done.4.rest_1_), channel_id=1, source_target_pairs={{0,1},{1,0},{2,3},{3,2},{4,5},{5,4},{6,7},{7,6},{8,9},{9,8},{10,11... | collective-permute-start | bytes 393224 | tf_op jit(solution)/shard_map/ppermute | solution.py:224
  22.9 2.3 %copy-start.2 = (bf16[512,1536]{1,0:T(8,128)(2,1)S(1)}, bf16[512,1536]{1,0:T(8,128)(2,1)}, u32[]{:S(2)}) copy-start(bf16[512,1536]{1,0:T(8,128)(2,1)} %wo_ref.1) | copy-start | bytes 4718596
  22.9 2.2 %collective-permute-start.8 = (bf16[256,256]{1,0:T(8,128)(2,1)S(1)}, bf16[256,256]{1,0:T(8,128)(2,1)S(1)}, u32[]{:S(2)}, u32[]{:S(2)}) collective-permute-start(bf16[256,256]{1,0:T(8,128)(2,1)S(1)} %collective-permute-done.5.rest_2_), channel_id=1, source_target_pairs={{0,1},{1,0},{2,3},{3,2},{4,5},{5,4},{6,7},{7,6},{8,9},{9,8},{10,11... | collective-permute-start | bytes 393224 | tf_op jit(solution)/shard_map/ppermute | solution.py:234

commit v3 on v2

v3 whole, which is shorter than its diff:
```python
import functools

import jax
import jax.numpy as jnp
from jax import lax
from jax.experimental import pallas as pl
from jax.experimental.pallas import tpu as pltpu
from jax.sharding import PartitionSpec as P

DILATION_STEP = 4
EPS = 1e-06
LOADF = 8_000_000_000
LOG2E = 1.4426950408889634
F32 = jnp.float32
BF16 = jnp.bfloat16
VMEM = pl.BlockSpec(memory_space=pltpu.VMEM)
SMEM = pl.BlockSpec(memory_space=pltpu.SMEM)


def normed_rows(values, gain):
    wide = values.astype(F32)
    meansq = jnp.mean(wide * wide, axis=-1, keepdims=True)
    return wide * lax.rsqrt(meansq + EPS) * gain


def dot(a, b):
    return jnp.dot(a, b, preferred_element_type=F32)


def edge_kernel(reach, x_hbm, edges_ref, near_ref, sems):
    rows = x_hbm.shape[0]
    tile = near_ref.shape[1]
    copies = [
        pltpu.make_async_copy(x_hbm.at[0:tile, :], near_ref.at[0], sems.at[0]),
        pltpu.make_async_copy(x_hbm.at[rows - tile : rows, :], near_ref.at[1], sems.at[1]),
    ]
    for copy in copies:
        copy.start()
    for copy in copies:
        copy.wait()
    edges_ref[0:reach, :] = near_ref[0, 0:reach, :]
    edges_ref[reach:, :] = near_ref[1, tile - reach :, :]


def center_kernel(center, x_ref, gain_ref, w_ref, normed_ref, part_ref):
    normed_ref[...] = normed_rows(x_ref[...], gain_ref[...]).astype(BF16)
    part_ref[...] = dot(normed_ref[...], w_ref[center])


def project_kernel(
    reach, x_ref, normed_ref, part_ref, near_ref, far_ref, gain_ref, w_ref, bias_ref, again_ref, wk_ref, wv_ref,
    hidden_ref, attn_ref, kv_ref, line_ref, sum_ref, *shift_refs,
):
    rows, chan = x_ref.shape
    taps, _, out_chan = w_ref.shape
    head_dim = wk_ref.shape[1]
    index, count = lax.axis_index("seq"), lax.axis_size("seq")
    even = lax.rem(index, 2) == 0
    near, far = near_ref[...].astype(F32), far_ref[...].astype(F32)
    left = jnp.where(even, far, near)
    right = jnp.where(even, near, far)
    row = lax.broadcasted_iota(jnp.int32, (2 * reach, 1), 0)
    left = jnp.where((row >= reach) & (index > 0), normed_rows(left, gain_ref[...]), 0.0)
    right = jnp.where((row < reach) & (index < count - 1), normed_rows(right, gain_ref[...]), 0.0)
    line_ref[0:rows, :] = normed_ref[...]
    line_ref[rows:, :] = jnp.concatenate([left, right], axis=0).astype(BF16)
    total = part_ref[...]
    slots = iter(shift_refs)
    for tap in range(taps):
        shift = (tap - (taps - 1) // 2) * DILATION_STEP
        if shift == 0:
            continue
        product = dot(line_ref[...], w_ref[tap])
        shift_ref = next(slots)
        if shift < 0:
            shift_ref[0 : 2 * reach, :] = product[rows : rows + 2 * reach]
            shift_ref[2 * reach :, :] = product[0:rows]
            total = total + shift_ref[2 * reach + shift : 2 * reach + shift + rows, :]
        else:
            shift_ref[0:rows, :] = product[0:rows]
            shift_ref[rows:, :] = product[rows + 2 * reach : rows + 4 * reach]
            total = total + shift_ref[shift : shift + rows, :]
    activated = jax.nn.gelu(total + bias_ref[...], approximate=True)
    hidden_ref[:, :out_chan] = (x_ref[:, :out_chan].astype(F32) + activated).astype(BF16)
    hidden_ref[:, out_chan:] = x_ref[:, out_chan:]
    attn_ref[...] = normed_rows(hidden_ref[...], again_ref[...]).astype(BF16)
    kv_ref[:, :head_dim] = dot(attn_ref[...], wk_ref[...]).astype(BF16)
    kv_ref[:, head_dim:] = dot(attn_ref[...], wv_ref[...]).astype(BF16)


def fold(q_ref, kv_refs, m_in, acc_in, m_out, acc_out):
    many, head_dim = q_ref.shape
    step = min(128, many)
    mates = [
        jnp.concatenate([kv[:, head_dim:], jnp.ones((kv.shape[0], head_dim), BF16)], axis=1) for kv in kv_refs
    ]
    for at in range(0, many, step):
        span = slice(at, at + step)
        q = q_ref[span, :]
        scores = [
            lax.dot_general(q, kv[:, :head_dim], (((1,), (1,)), ((), ())), preferred_element_type=F32)
            for kv in kv_refs
        ]
        top = jnp.max(functools.reduce(jnp.maximum, scores), axis=-1, keepdims=True)
        top = jnp.broadcast_to(top, (step, head_dim))
        if m_in is not None:
            old = m_in[span, :]
            top = jnp.maximum(old, top)
            fade = jnp.exp2(old - top)
        summed = None
        for s, mate in zip(scores, mates):
            e = jnp.exp2(s - jnp.concatenate([top] * (s.shape[1] // head_dim), axis=1))
            o = dot(e.astype(BF16), mate)
            summed = o if summed is None else summed + o
        if m_in is not None:
            summed = summed + acc_in[span, :] * jnp.concatenate([fade, fade], axis=1)
        m_out[span, :] = top
        acc_out[span, :] = summed


def query_kernel(blocks, attn_ref, wq_ref, *rest):
    kv_refs = rest[:blocks]
    q_ref, m_ref, acc_ref = rest[blocks:]
    rows = attn_ref.shape[0]
    head_dim = q_ref.shape[1]
    scale = LOG2E * head_dim**-0.5
    q = dot(attn_ref[...], wq_ref[...])
    for h in range(wq_ref.shape[1] // head_dim):
        q_ref[h * rows : (h + 1) * rows, :] = (q[:, h * head_dim : (h + 1) * head_dim] * scale).astype(BF16)
    fold(q_ref, kv_refs, None, None, m_ref, acc_ref)


def more_kernel(blocks, q_ref, m_in, acc_in, *rest):
    m_ref, acc_ref = rest[blocks:]
    fold(q_ref, rest[:blocks], m_in, acc_in, m_ref, acc_ref)


def last_kernel(blocks, q_ref, m_in, acc_in, hidden_ref, wo_ref, *rest):
    out_hbm, m_ref, acc_ref, out_ref, sems = rest[blocks:]
    fold(q_ref, rest[:blocks], m_in, acc_in, m_ref, acc_ref)
    rows = hidden_ref.shape[0]
    many, head_dim = q_ref.shape
    step = rows // sems.shape[0]
    copies = []
    for i in range(sems.shape[0]):
        span = slice(i * step, (i + 1) * step)
        attended = jnp.concatenate(
            [
                (
                    acc_ref[at + i * step : at + (i + 1) * step, :head_dim]
                    / acc_ref[at + i * step : at + (i + 1) * step, head_dim:]
                ).astype(BF16)
                for at in range(0, many, rows)
            ],
            axis=1,
        )
        out_ref[span, :] = (hidden_ref[span, :].astype(F32) + dot(attended, wo_ref[...])).astype(BF16)
        copies.append(pltpu.make_async_copy(out_ref.at[span, :], out_hbm.at[span, :], sems.at[i]))
        copies[-1].start()
    for copy in copies:
        copy.wait()


def call(body, outs, args, specs=None, scratch=(), flops=0, moved=0, name=None, alias=None, out_spec=VMEM):
    return pl.pallas_call(
        body,
        out_shape=outs,
        in_specs=specs or [VMEM] * len(args),
        out_specs=jax.tree.map(lambda _: out_spec, outs),
        scratch_shapes=scratch,
        input_output_aliases=alias or {},
        compiler_params=pltpu.CompilerParams(vmem_limit_bytes=16 * 1024 * 1024),
        cost_estimate=pl.CostEstimate(flops=flops, bytes_accessed=moved, transcendentals=0),
        name=name,
    )(*args)


def shards(
    seq_in, conv_gain, convolution_weight, conv_bias, attn_gain, w_query, w_key, w_value, w_out
):
    rows, chan = seq_in.shape
    taps, _, out_chan = convolution_weight.shape
    head_dim = w_key.shape[1]
    heads = w_query.shape[1] // head_dim
    reach = DILATION_STEP * (taps - 1) // 2
    count = lax.axis_size("seq")
    shape = jax.ShapeDtypeStruct

    edges = call(
        functools.partial(edge_kernel, reach),
        shape((2 * reach, chan), BF16),
        (pltpu.with_memory_space_constraint(seq_in, pltpu.HBM),),
        specs=[pl.BlockSpec(memory_space=pltpu.HBM)],
        scratch=[pltpu.VMEM((2, 16, chan), BF16), pltpu.SemaphoreType.DMA((2,))],
        flops=LOADF,
        moved=rows * chan * 4,
        name="edges",
    )
    near = lax.ppermute(edges, "seq", [(i, i ^ 1) for i in range(count)])
    far_pairs = [(i, (i - 1 if i % 2 == 0 else i + 1) % count) for i in range(count)]
    far = lax.ppermute(edges, "seq", far_pairs)

    normed, part = call(
        functools.partial(center_kernel, (taps - 1) // 2),
        (shape((rows, chan), BF16), shape((rows, out_chan), F32)),
        (seq_in, conv_gain, convolution_weight),
        flops=2 * rows * chan * out_chan,
        moved=rows * chan * 4 + chan * out_chan * 2,
        name="center",
    )
    hidden, attn_in, kv = call(
        functools.partial(project_kernel, reach),
        (shape((rows, chan), BF16), shape((rows, chan), BF16), shape((rows, 2 * head_dim), BF16)),
        (
            seq_in, normed, part, near, far, conv_gain, convolution_weight, conv_bias, attn_gain, w_key, w_value,
        ),
        scratch=[pltpu.VMEM((rows + 4 * reach, chan), BF16), pltpu.VMEM((rows, out_chan), F32)]
        + [pltpu.VMEM((rows + 2 * reach, out_chan), F32)] * (taps - 1),
        flops=2 * rows * chan * (2 * head_dim + (taps - 1) * out_chan),
        moved=(taps - 1) * chan * out_chan * 2,
        name="project",
    )
    sibling = [(i, i ^ 1) for i in range(count)]
    steps = list(range(2, count, 2))
    blocks = []
    for k, step in enumerate(steps):
        other = steps[k ^ 1] if (k ^ 1) < len(steps) else step
        blocks.append(lax.ppermute(kv, "seq", [(i, i ^ (step, other)[i % 2]) for i in range(count)]))
    mate = lax.ppermute(kv, "seq", sibling)
    fold_flops = 4 * rows * rows * heads * head_dim
    state = (shape((rows * heads, head_dim), F32), shape((rows * heads, 2 * head_dim), F32))
    q, m, acc = call(
        functools.partial(query_kernel, 1),
        (shape((rows * heads, head_dim), BF16),) + state,
        (attn_in, w_query, kv),
        flops=2 * rows * chan * heads * head_dim + fold_flops,
        name="query",
    )
    m, acc, *near_blocks = lax.optimization_barrier((m, acc, *blocks[:-1]))
    last_block = blocks[-1]
    passed = [lax.ppermute(b, "seq", sibling) for b in near_blocks]
    m, acc = call(
        functools.partial(more_kernel, len(near_blocks) + 1),
        state,
        (q, m, acc, mate, *near_blocks),
        alias={1: 0, 2: 1},
        flops=(len(near_blocks) + 1) * fold_flops,
        name="near",
    )
    m, acc, last_block = lax.optimization_barrier((m, acc, last_block))
    last_passed = lax.ppermute(last_block, "seq", sibling)
    middle = passed + [last_block]
    m, acc = call(
        functools.partial(more_kernel, len(middle)),
        state,
        (q, m, acc, *middle),
        alias={1: 0, 2: 1},
        flops=len(middle) * fold_flops,
        name="middle",
    )
    return call(
        functools.partial(last_kernel, 1),
        shape((rows, chan), BF16),
        (q, m, acc, hidden, w_out, last_passed),
        out_spec=pl.BlockSpec(memory_space=pltpu.HBM),
        scratch=[pltpu.VMEM(s.shape, s.dtype) for s in state]
        + [pltpu.VMEM((rows, chan), BF16), pltpu.SemaphoreType.DMA((2,))],
        flops=fold_flops + 2 * rows * chan * heads * head_dim,
        name="last",
    )


def solution(mesh):
    placed = (P(("dp", "seq"), None), P(), P(), P(), P(), P(), P(), P(), P())
    return jax.shard_map(
        shards, mesh=mesh, in_specs=placed, out_specs=P(("dp", "seq"), None), check_vma=False
    )
```

time: 27.2 us -> 23.2 us (0.85)
  the two profiles are of different devices: /device:TPU:3 before, /device:TPU:1 now
where the time goes in v3:
time: 23.2 us; the launch traced here: 23 us
  Pallas kernels  10.8 us (47%)
  starting transfers between devices  9.79 us (42%)
  waiting for transfers between devices  2.25 us (10%)
    pallas_call x7, Pallas kernels, call(): pl.pallas_call(body, out_shape=outs, in_specs=specs or [VMEM] * len(args)...  10.8 us
    ppermute x3, starting transfers between devices, shards(): lax.ppermute(kv, 'seq', [(i, i ^ (step, other)[i % 2]) for i in range(cou...  3.53 us
    ppermute x1, starting transfers between devices, shards(): far = lax.ppermute(edges, 'seq', far_pairs)  2.67 us
    ppermute x3, waiting for transfers between devices, shards(): lax.ppermute(kv, 'seq', [(i, i ^ (step, other)[i % 2]) for i in range(cou...  2.22 us
    ppermute x2, starting transfers between devices, shards(): passed = [lax.ppermute(b, 'seq', sibling) for b in near_blocks]  1.68 us
    ppermute x1, starting transfers between devices, shards(): near = lax.ppermute(edges, 'seq', [(i, i ^ 1) for i in range(count)])  0.79 us
    ppermute x1, starting transfers between devices, shards(): last_passed = lax.ppermute(last_block, 'seq', sibling)  0.57 us
    ppermute x1, starting transfers between devices, shards(): mate = lax.ppermute(kv, 'seq', sibling)  0.56 us
  transfers between devices with their start and end apart: 9, of which 1 were waited for; matrix products, arithmetic and copies ran while one was open for 0% of the time, Pallas kernels for 23%

profile of v3, /device:TPU:1, one launch (start us, length us, event | category | flops | bytes accessed | tf_op | source)
XLA Modules:
  0.0 23.0 jit_solution(9484899869094106271)
XLA Ops:
  0.0 0.0 copy-start.1
  0.0 0.0 copy-start.6
  0.0 0.0 copy-start
  0.0 1.0 %edges.1 = bf16[8,1536]{1,0:T(8,128)(2,1)S(1)} custom-call(bf16[256,1536]{1,0:T(8,128)(2,1)} %x_ref.3), custom_call_target="tpu_custom_call" | custom-call | flops 8000000000 | bytes 1572864 | tf_op jit(solution)/shard_map/edges/pallas_call | solution.py:165
  1.0 0.0 copy-start.4
  1.0 0.0 copy-start.5
  1.0 0.0 copy-start.7
  1.0 0.0 copy-start.8
  1.1 2.7 %collective-permute-start.1 = (bf16[8,1536]{1,0:T(8,128)(2,1)S(1)}, bf16[8,1536]{1,0:T(8,128)(2,1)S(1)}, u32[]{:S(2)}, u32[]{:S(2)}) collective-permute-start(bf16[8,1536]{1,0:T(8,128)(2,1)S(1)} %edges.1), channel_id=1, source_target_pairs={{0,7},{1,2},{2,1},{3,4},{4,3},{5,6},{6,5},{7,0},{8,15},{9,10},{10,... | collective-permute-start | bytes 73736 | tf_op jit(solution)/shard_map/ppermute | solution.py:201
  3.7 0.8 %collective-permute-start = (bf16[8,1536]{1,0:T(8,128)(2,1)S(1)}, bf16[8,1536]{1,0:T(8,128)(2,1)S(1)}, u32[]{:S(2)}, u32[]{:S(2)}) collective-permute-start(bf16[8,1536]{1,0:T(8,128)(2,1)S(1)} %edges.1), channel_id=1, source_target_pairs={{0,1},{1,0},{2,3},{3,2},{4,5},{5,4},{6,7},{7,6},{8,9},{9,8},{10,11... | collective-permute-start | bytes 73736 | tf_op jit(solution)/shard_map/ppermute | solution.py:199
  4.5 0.0 copy-done.1
  4.5 0.0 copy-done.6
  4.5 0.0 copy-done
  4.5 1.0 %center.1 = (bf16[256,1536]{1,0:T(8,128)(2,1)S(1)}, f32[256,768]{1,0:T(8,128)S(1)}) custom-call(bf16[256,1536]{1,0:T(8,128)(2,1)S(1)} %copy-done.1, f32[1536]{0:T(1024)S(1)} %copy-done.6, bf16[3,1536,768]{2,1,0:T(8,128)(2,1)S(1)} %copy-done), custom_call_target="tpu_custom_call" | custom-call | flops 603979776 | bytes 3932160 | tf_op jit(solution)/shard_map/center/pallas_call | solution.py:165
  5.5 0.0 collective-permute-done.1.far_ref
  5.5 0.0 collective-permute-done.near_ref
  5.5 0.0 copy-done.4
  5.5 0.0 copy-done.5
  5.6 0.0 copy-done.7
  5.6 0.0 copy-done.8
  5.6 0.0 copy-start.2
  5.6 2.5 %project.1 = (bf16[256,1536]{1,0:T(8,128)(2,1)S(1)}, bf16[256,1536]{1,0:T(8,128)(2,1)S(1)}, bf16[256,256]{1,0:T(8,128)(2,1)S(1)}) custom-call(bf16[256,1536]{1,0:T(8,128)(2,1)S(1)} %copy-done.1, bf16[256,1536]{1,0:T(8,128)(2,1)S(1)} %get-tuple-element.24.normed_ref, f32[256,768]{1,0:T(8,128)S(1)} %get-tuple-element.25.part_ref, ...), custom_call_target="tpu_custom_call" | custom-call | flops 1409286144 | bytes 4718592 | tf_op jit(solution)/shard_map/project/pallas_call | solution.py:165
  8.1 2.1 %collective-permute-start.3 = (bf16[256,256]{1,0:T(8,128)(2,1)S(1)}, bf16[256,256]{1,0:T(8,128)(2,1)S(1)}, u32[]{:S(2)}, u32[]{:S(2)}) collective-permute-start(bf16[256,256]{1,0:T(8,128)(2,1)S(1)} %get-tuple-element.27.rest_0_), channel_id=1, source_target_pairs={{0,4},{1,3},{2,6},{3,1},{4,0},{5,7},{6,2},{7,5},{8,12},{9,11},{10,... | collective-permute-start | bytes 393224 | tf_op jit(solution)/shard_map/ppermute | solution.py:228
  10.2 1.0 %collective-permute-start.2 = (bf16[256,256]{1,0:T(8,128)(2,1)S(1)}, bf16[256,256]{1,0:T(8,128)(2,1)S(1)}, u32[]{:S(2)}, u32[]{:S(2)}) collective-permute-start(bf16[256,256]{1,0:T(8,128)(2,1)S(1)} %get-tuple-element.27.rest_0_), channel_id=1, source_target_pairs={{0,2},{1,5},{2,0},{3,7},{4,6},{5,1},{6,4},{7,3},{8,10},{9,13},{10,... | collective-permute-start | bytes 393224 | tf_op jit(solution)/shard_map/ppermute | solution.py:228
  11.2 0.6 %collective-permute-start.4 = (bf16[256,256]{1,0:T(8,128)(2,1)S(1)}, bf16[256,256]{1,0:T(8,128)(2,1)S(1)}, u32[]{:S(2)}, u32[]{:S(2)}) collective-permute-start(bf16[256,256]{1,0:T(8,128)(2,1)S(1)} %get-tuple-element.27.rest_0_), channel_id=1, source_target_pairs={{0,1},{1,0},{2,3},{3,2},{4,5},{5,4},{6,7},{7,6},{8,9},{9,8},{10,11... | collective-permute-start | bytes 393224 | tf_op jit(solution)/shard_map/ppermute | solution.py:229
  11.8 0.4 %collective-permute-start.5 = (bf16[256,256]{1,0:T(8,128)(2,1)S(1)}, bf16[256,256]{1,0:T(8,128)(2,1)S(1)}, u32[]{:S(2)}, u32[]{:S(2)}) collective-permute-start(bf16[256,256]{1,0:T(8,128)(2,1)S(1)} %get-tuple-element.27.rest_0_), channel_id=1, source_target_pairs={{0,6},{1,7},{2,4},{3,5},{4,2},{5,3},{6,0},{7,1},{8,14},{9,15},{10,... | collective-permute-start | bytes 393224 | tf_op jit(solution)/shard_map/ppermute | solution.py:228
  12.2 0.0 copy-done.2
  12.2 1.1 %query.1 = (bf16[1024,128]{1,0:T(8,128)(2,1)S(1)}, f32[1024,128]{1,0:T(8,128)S(1)}, f32[1024,256]{1,0:T(8,128)S(1)}) custom-call(bf16[256,1536]{1,0:T(8,128)(2,1)S(1)} %get-tuple-element.26.attn_ref, bf16[1536,512]{1,0:T(8,128)(2,1)S(1)} %copy-done.2, bf16[256,256]{1,0:T(8,128)(2,1)S(1)} %get-tuple-element.27.rest_0_), custom_call_target="tpu_custom_call" | custom-call | flops 536870912 | tf_op jit(solution)/shard_map/query/pallas_call | solution.py:165
  13.3 0.0 collective-permute-done.3.rest_2_
  13.4 2.2 %collective-permute-done.2.rest_1_ = bf16[256,256]{1,0:T(8,128)(2,1)S(1)} collective-permute-done((bf16[256,256]{1,0:T(8,128)(2,1)S(1)}, bf16[256,256]{1,0:T(8,128)(2,1)S(1)}, u32[]{:S(2)}, u32[]{:S(2)}) %collective-permute-start.2) | collective-permute-done | bytes 131104 | tf_op jit(solution)/shard_map/ppermute | solution.py:228
  15.6 1.7 %collective-permute-start.6 = (bf16[256,256]{1,0:T(8,128)(2,1)S(1)}, bf16[256,256]{1,0:T(8,128)(2,1)S(1)}, u32[]{:S(2)}, u32[]{:S(2)}) collective-permute-start(bf16[256,256]{1,0:T(8,128)(2,1)S(1)} %collective-permute-done.2.rest_1_), channel_id=1, source_target_pairs={{0,1},{1,0},{2,3},{3,2},{4,5},{5,4},{6,7},{7,6},{8,9},{9,8},{10,11... | collective-permute-start | bytes 393224 | tf_op jit(solution)/shard_map/ppermute | solution.py:241
  17.2 0.0 collective-permute-start.7
  17.3 0.0 collective-permute-done.4.rest_0_
  17.3 1.6 %near.1 = (f32[1024,128]{1,0:T(8,128)S(1)}, f32[1024,256]{1,0:T(8,128)S(1)}) custom-call(bf16[1024,128]{1,0:T(8,128)(2,1)S(1)} %get-tuple-element.28.q_ref, f32[1024,128]{1,0:T(8,128)S(1)} %get-tuple-element.31.m_in, f32[1024,256]{1,0:T(8,128)S(1)} %get-tuple-element.32.acc_in, ...), custom_call_target="tpu_custom_call", output_to_operand_aliasing={{0}: (1, {}), {1}: (2, {})} | custom-call | flops 402653184 | tf_op jit(solution)/shard_map/near/pallas_call | solution.py:165
  18.9 0.0 copy-start.3
  18.9 0.0 collective-permute-done.5.rest_2_
  18.9 0.6 %collective-permute-start.8 = (bf16[256,256]{1,0:T(8,128)(2,1)S(1)}, bf16[256,256]{1,0:T(8,128)(2,1)S(1)}, u32[]{:S(2)}, u32[]{:S(2)}) collective-permute-start(bf16[256,256]{1,0:T(8,128)(2,1)S(1)} %collective-permute-done.5.rest_2_), channel_id=1, source_target_pairs={{0,1},{1,0},{2,3},{3,2},{4,5},{5,4},{6,7},{7,6},{8,9},{9,8},{10,11... | collective-permute-start | bytes 393224 | tf_op jit(solution)/shard_map/ppermute | solution.py:251
  19.5 0.0 collective-permute-done.6.rest_0_
  19.5 0.0 collective-permute-done.7.rest_1_
  19.5 1.6 %middle.1 = (f32[1024,128]{1,0:T(8,128)S(1)}, f32[1024,256]{1,0:T(8,128)S(1)}) custom-call(bf16[1024,128]{1,0:T(8,128)(2,1)S(1)} %get-tuple-element.28.q_ref, f32[1024,128]{1,0:T(8,128)S(1)} %get-tuple-element.37.m_in, f32[1024,256]{1,0:T(8,128)S(1)} %get-tuple-element.38.acc_in, ...), custom_call_target="tpu_custom_call", output_to_operand_aliasing={{0}: (1, {}), {1}: (2, {})} | custom-call | flops 402653184 | tf_op jit(solution)/shard_map/middle/pallas_call | solution.py:165
  21.1 0.0 collective-permute-done.8.rest_0_
  21.1 0.0 copy-done.3
  21.1 1.9 %last.1 = bf16[256,1536]{1,0:T(8,128)(2,1)} custom-call(bf16[1024,128]{1,0:T(8,128)(2,1)S(1)} %get-tuple-element.28.q_ref, f32[1024,128]{1,0:T(8,128)S(1)} %get-tuple-element.40.m_in, f32[1024,256]{1,0:T(8,128)S(1)} %get-tuple-element.41.acc_in, bf16[256,1536]{1,0:T(8,128)(2,1)S(1)} %get-tuple-element.42.hidden_ref, bf16[512,1536]{1,0:T(8,128)(2,1)S(1)} %copy-done.3, ...), custom_call_target="tpu_custom_call" | custom-call | flops 536870912 | tf_op jit(solution)/shard_map/last/pallas_call | solution.py:165
Async XLA Ops:
  0.0 4.5 %copy-start.1 = (bf16[256,1536]{1,0:T(8,128)(2,1)S(1)}, bf16[256,1536]{1,0:T(8,128)(2,1)}, u32[]{:S(2)}) copy-start(bf16[256,1536]{1,0:T(8,128)(2,1)} %x_ref.3) | copy-start | bytes 2359300
  0.0 4.5 %copy-start.6 = (f32[1536]{0:T(1024)S(1)}, f32[1536]{0:T(1024)}, u32[]{:S(2)}) copy-start(f32[1536]{0:T(1024)} %gain_ref.3) | copy-start | bytes 18436
  0.0 4.5 %copy-start = (bf16[3,1536,768]{2,1,0:T(8,128)(2,1)S(1)}, bf16[3,1536,768]{2,1,0:T(8,128)(2,1)}, u32[]{:S(2)}) copy-start(bf16[3,1536,768]{2,1,0:T(8,128)(2,1)} %w_ref.3) | copy-start | bytes 21233668
  1.0 4.5 %copy-start.4 = (bf16[1536,128]{1,0:T(8,128)(2,1)S(1)}, bf16[1536,128]{1,0:T(8,128)(2,1)}, u32[]{:S(2)}) copy-start(bf16[1536,128]{1,0:T(8,128)(2,1)} %wk_ref.1) | copy-start | bytes 1179652
  1.0 4.5 %copy-start.5 = (bf16[1536,128]{1,0:T(8,128)(2,1)S(1)}, bf16[1536,128]{1,0:T(8,128)(2,1)}, u32[]{:S(2)}) copy-start(bf16[1536,128]{1,0:T(8,128)(2,1)} %wv_ref.1) | copy-start | bytes 1179652
  1.0 4.5 %copy-start.7 = (f32[1536]{0:T(1024)S(1)}, f32[1536]{0:T(1024)}, u32[]{:S(2)}) copy-start(f32[1536]{0:T(1024)} %again_ref.1) | copy-start | bytes 18436
  1.0 4.5 %copy-start.8 = (f32[768]{0:T(1024)S(1)}, f32[768]{0:T(1024)}, u32[]{:S(2)}) copy-start(f32[768]{0:T(1024)} %bias_ref.1) | copy-start | bytes 9220
  1.1 4.5 %collective-permute-start.1 = (bf16[8,1536]{1,0:T(8,128)(2,1)S(1)}, bf16[8,1536]{1,0:T(8,128)(2,1)S(1)}, u32[]{:S(2)}, u32[]{:S(2)}) collective-permute-start(bf16[8,1536]{1,0:T(8,128)(2,1)S(1)} %edges.1), channel_id=1, source_target_pairs={{0,7},{1,2},{2,1},{3,4},{4,3},{5,6},{6,5},{7,0},{8,15},{9,10},{10,... | collective-permute-start | bytes 73736 | tf_op jit(solution)/shard_map/ppermute | solution.py:201
  3.7 1.8 %collective-permute-start = (bf16[8,1536]{1,0:T(8,128)(2,1)S(1)}, bf16[8,1536]{1,0:T(8,128)(2,1)S(1)}, u32[]{:S(2)}, u32[]{:S(2)}) collective-permute-start(bf16[8,1536]{1,0:T(8,128)(2,1)S(1)} %edges.1), channel_id=1, source_target_pairs={{0,1},{1,0},{2,3},{3,2},{4,5},{5,4},{6,7},{7,6},{8,9},{9,8},{10,11... | collective-permute-start | bytes 73736 | tf_op jit(solution)/shard_map/ppermute | solution.py:199
  5.6 6.6 %copy-start.2 = (bf16[1536,512]{1,0:T(8,128)(2,1)S(1)}, bf16[1536,512]{1,0:T(8,128)(2,1)}, u32[]{:S(2)}) copy-start(bf16[1536,512]{1,0:T(8,128)(2,1)} %wq_ref.1) | copy-start | bytes 4718596
  8.1 5.2 %collective-permute-start.3 = (bf16[256,256]{1,0:T(8,128)(2,1)S(1)}, bf16[256,256]{1,0:T(8,128)(2,1)S(1)}, u32[]{:S(2)}, u32[]{:S(2)}) collective-permute-start(bf16[256,256]{1,0:T(8,128)(2,1)S(1)} %get-tuple-element.27.rest_0_), channel_id=1, source_target_pairs={{0,4},{1,3},{2,6},{3,1},{4,0},{5,7},{6,2},{7,5},{8,12},{9,11},{10,... | collective-permute-start | bytes 393224 | tf_op jit(solution)/shard_map/ppermute | solution.py:228
  10.2 5.4 %collective-permute-start.2 = (bf16[256,256]{1,0:T(8,128)(2,1)S(1)}, bf16[256,256]{1,0:T(8,128)(2,1)S(1)}, u32[]{:S(2)}, u32[]{:S(2)}) collective-permute-start(bf16[256,256]{1,0:T(8,128)(2,1)S(1)} %get-tuple-element.27.rest_0_), channel_id=1, source_target_pairs={{0,2},{1,5},{2,0},{3,7},{4,6},{5,1},{6,4},{7,3},{8,10},{9,13},{10,... | collective-permute-start | bytes 393224 | tf_op jit(solution)/shard_map/ppermute | solution.py:228
  11.2 6.0 %collective-permute-start.4 = (bf16[256,256]{1,0:T(8,128)(2,1)S(1)}, bf16[256,256]{1,0:T(8,128)(2,1)S(1)}, u32[]{:S(2)}, u32[]{:S(2)}) collective-permute-start(bf16[256,256]{1,0:T(8,128)(2,1)S(1)} %get-tuple-element.27.rest_0_), channel_id=1, source_target_pairs={{0,1},{1,0},{2,3},{3,2},{4,5},{5,4},{6,7},{7,6},{8,9},{9,8},{10,11... | collective-permute-start | bytes 393224 | tf_op jit(solution)/shard_map/ppermute | solution.py:229
  11.8 7.1 %collective-permute-start.5 = (bf16[256,256]{1,0:T(8,128)(2,1)S(1)}, bf16[256,256]{1,0:T(8,128)(2,1)S(1)}, u32[]{:S(2)}, u32[]{:S(2)}) collective-permute-start(bf16[256,256]{1,0:T(8,128)(2,1)S(1)} %get-tuple-element.27.rest_0_), channel_id=1, source_target_pairs={{0,6},{1,7},{2,4},{3,5},{4,2},{5,3},{6,0},{7,1},{8,14},{9,15},{10,... | collective-permute-start | bytes 393224 | tf_op jit(solution)/shard_map/ppermute | solution.py:228
  15.6 3.9 %collective-permute-start.6 = (bf16[256,256]{1,0:T(8,128)(2,1)S(1)}, bf16[256,256]{1,0:T(8,128)(2,1)S(1)}, u32[]{:S(2)}, u32[]{:S(2)}) collective-permute-start(bf16[256,256]{1,0:T(8,128)(2,1)S(1)} %collective-permute-done.2.rest_1_), channel_id=1, source_target_pairs={{0,1},{1,0},{2,3},{3,2},{4,5},{5,4},{6,7},{7,6},{8,9},{9,8},{10,11... | collective-permute-start | bytes 393224 | tf_op jit(solution)/shard_map/ppermute | solution.py:241
  17.2 2.2 %collective-permute-start.7 = (bf16[256,256]{1,0:T(8,128)(2,1)S(1)}, bf16[256,256]{1,0:T(8,128)(2,1)S(1)}, u32[]{:S(2)}, u32[]{:S(2)}) collective-permute-start(bf16[256,256]{1,0:T(8,128)(2,1)S(1)} %collective-permute-done.3.rest_2_), channel_id=1, source_target_pairs={{0,1},{1,0},{2,3},{3,2},{4,5},{5,4},{6,7},{7,6},{8,9},{9,8},{10,11... | collective-permute-start | bytes 393224 | tf_op jit(solution)/shard_map/ppermute | solution.py:241
  18.9 2.2 %copy-start.3 = (bf16[512,1536]{1,0:T(8,128)(2,1)S(1)}, bf16[512,1536]{1,0:T(8,128)(2,1)}, u32[]{:S(2)}) copy-start(bf16[512,1536]{1,0:T(8,128)(2,1)} %wo_ref.1) | copy-start | bytes 4718596
  18.9 2.2 %collective-permute-start.8 = (bf16[256,256]{1,0:T(8,128)(2,1)S(1)}, bf16[256,256]{1,0:T(8,128)(2,1)S(1)}, u32[]{:S(2)}, u32[]{:S(2)}) collective-permute-start(bf16[256,256]{1,0:T(8,128)(2,1)S(1)} %collective-permute-done.5.rest_2_), channel_id=1, source_target_pairs={{0,1},{1,0},{2,3},{3,2},{4,5},{5,4},{6,7},{7,6},{8,9},{9,8},{10,11... | collective-permute-start | bytes 393224 | tf_op jit(solution)/shard_map/ppermute | solution.py:251

commit v4 on v3

v4 whole, which is shorter than its diff:
```python
import functools
import math

import jax
import jax.numpy as jnp
from jax import lax
from jax.experimental import pallas as pl
from jax.experimental.pallas import tpu as pltpu
from jax.sharding import PartitionSpec as P

DILATION_STEP = 4
EPS = 1e-06
CEILING = 100.0
LIMIT = 60
LOADF = 8_000_000_000
LOG2E = 1.4426950408889634
F32 = jnp.float32
BF16 = jnp.bfloat16
VMEM = pl.BlockSpec(memory_space=pltpu.VMEM)
SMEM = pl.BlockSpec(memory_space=pltpu.SMEM)


def normed_rows(values, gain):
    wide = values.astype(F32)
    meansq = jnp.mean(wide * wide, axis=-1, keepdims=True)
    return wide * lax.rsqrt(meansq + EPS) * gain


def dot(a, b):
    return jnp.dot(a, b, preferred_element_type=F32)


def edge_kernel(reach, x_hbm, edges_ref, near_ref, sems):
    rows = x_hbm.shape[0]
    tile = near_ref.shape[1]
    copies = [
        pltpu.make_async_copy(x_hbm.at[0:tile, :], near_ref.at[0], sems.at[0]),
        pltpu.make_async_copy(x_hbm.at[rows - tile : rows, :], near_ref.at[1], sems.at[1]),
    ]
    for copy in copies:
        copy.start()
    for copy in copies:
        copy.wait()
    edges_ref[0:reach, :] = near_ref[0, 0:reach, :]
    edges_ref[reach:, :] = near_ref[1, tile - reach :, :]


def norm_kernel(x_ref, gain_ref, normed_ref):
    normed_ref[...] = normed_rows(x_ref[...], gain_ref[...]).astype(BF16)


def center_kernel(reach, normed_ref, w_ref, part_ref, *shift_refs):
    rows = normed_ref.shape[0]
    taps, _, out_chan = w_ref.shape
    total = dot(normed_ref[...], w_ref[(taps - 1) // 2])
    slots = iter(shift_refs)
    for tap in range(taps):
        shift = (tap - (taps - 1) // 2) * DILATION_STEP
        if shift == 0:
            continue
        shift_ref = next(slots)
        edge = shift_ref.shape[0] - rows
        first = edge if shift < 0 else 0
        shift_ref[0 if shift < 0 else rows : edge if shift < 0 else rows + edge, :] = jnp.zeros((edge, out_chan), F32)
        shift_ref[first : first + rows, :] = dot(normed_ref[...], w_ref[tap])
        total = total + shift_ref[first + shift : first + shift + rows, :]
    part_ref[...] = total


def project_kernel(
    reach, x_ref, part_ref, far_ref, near_ref, gain_ref, w_ref, bias_ref, again_ref, wk_ref, wv_ref,
    hidden_ref, attn_ref, kv_ref,
):
    rows, chan = x_ref.shape
    taps, _, out_chan = w_ref.shape
    index, count = lax.axis_index("seq"), lax.axis_size("seq")
    even = lax.rem(index, 2) == 0
    near, far = near_ref[...].astype(F32), far_ref[...].astype(F32)
    left = jnp.where(even, far, near)
    right = jnp.where(even, near, far)
    row = lax.broadcasted_iota(jnp.int32, (2 * reach, 1), 0)
    left = jnp.where((row >= reach) & (index > 0), normed_rows(left, gain_ref[...]), 0.0)
    right = jnp.where((row < reach) & (index < count - 1), normed_rows(right, gain_ref[...]), 0.0)
    around = jnp.concatenate([left, right], axis=0).astype(BF16)
    edge = 16 * pl.cdiv(reach, 16)
    top, bottom = part_ref[0:edge, :], part_ref[rows - edge :, :]
    for tap in range(taps):
        shift = (tap - (taps - 1) // 2) * DILATION_STEP
        if shift == 0:
            continue
        extra = dot(around, w_ref[tap])
        blank = jnp.zeros((edge - abs(shift), out_chan), F32)
        if shift < 0:
            top = top + jnp.concatenate([extra[2 * reach + shift : 2 * reach], blank], axis=0)
        else:
            bottom = bottom + jnp.concatenate([blank, extra[2 * reach : 2 * reach + shift]], axis=0)

    def activate(span, total):
        activated = jax.nn.gelu(total + bias_ref[...], approximate=True)
        first = (x_ref[span, :out_chan].astype(F32) + activated).astype(BF16)
        hidden = jnp.concatenate([first, x_ref[span, out_chan:]], axis=1)
        hidden_ref[span, :] = hidden
        attn_ref[span, :] = normed_rows(hidden, again_ref[...]).astype(BF16)

    activate(slice(edge, rows - edge), part_ref[edge : rows - edge, :])
    activate(slice(0, edge), top)
    activate(slice(rows - edge, rows), bottom)
    kv_ref[...] = dot(attn_ref[...], jnp.concatenate([wk_ref[...], wv_ref[...]], axis=1)).astype(BF16)


def key_side(kv, head_dim):
    rows = kv.shape[0]
    ones = (lax.broadcasted_iota(jnp.int32, (head_dim, rows), 0) == 0).astype(BF16)
    return jnp.concatenate([kv[:, :head_dim].T, ones], axis=0)


def value_side(kv, head_dim):
    return jnp.concatenate([kv[:, head_dim:], jnp.ones((kv.shape[0], head_dim), BF16)], axis=1)


def fold(q_ref, kv_refs, acc_in, acc_out):
    many, head_dim = q_ref.shape[0], q_ref.shape[1] // 2
    step = math.gcd(many, 256)
    pairs = [(key_side(kv, head_dim), value_side(kv, head_dim)) for kv in kv_refs]
    for at in range(0, many, step):
        span = slice(at, at + step)
        total = acc_in[span, :]
        for keys, values in pairs:
            weights = jnp.exp2(jnp.minimum(dot(q_ref[span, :], keys), CEILING))
            total = total + dot(weights.astype(BF16), values)
        acc_out[span, :] = total


def exact(q_ref, kv_refs, acc_out):
    many, head_dim = q_ref.shape[0], q_ref.shape[1] // 2
    step = math.gcd(many, 256)
    pairs = [(kv[:, :head_dim].T, value_side(kv, head_dim)) for kv in kv_refs]
    for at in range(0, many, step):
        span = slice(at, at + step)
        scores = [dot(q_ref[span, :head_dim], keys) for keys, _ in pairs]
        top = jnp.max(functools.reduce(jnp.maximum, scores), axis=-1, keepdims=True)
        total = None
        for s, (_, values) in zip(scores, pairs):
            piece = dot(jnp.exp2(s - top).astype(BF16), values)
            total = piece if total is None else total + piece
        acc_out[span, :] = total


def query_kernel(attn_ref, wq_ref, kv_ref, q_ref, acc_ref):
    rows = attn_ref.shape[0]
    head_dim = q_ref.shape[1] // 2
    scale = LOG2E * head_dim**-0.5
    q = dot(attn_ref[...], wq_ref[...])
    keys, values = kv_ref[:, :head_dim].T, value_side(kv_ref, head_dim)
    for h in range(wq_ref.shape[1] // head_dim):
        span = slice(h * rows, (h + 1) * rows)
        q_head = (q[:, h * head_dim : (h + 1) * head_dim] * scale).astype(BF16)
        scores = dot(q_head, keys)
        top = jnp.broadcast_to(jnp.max(scores, axis=-1, keepdims=True), (rows, head_dim)).astype(BF16)
        q_ref[span, :head_dim] = q_head
        q_ref[span, head_dim:] = -top
        top = jnp.concatenate([top.astype(F32)] * (scores.shape[1] // head_dim), axis=1)
        acc_ref[span, :] = dot(jnp.exp2(scores - top).astype(BF16), values)


def more_kernel(q_ref, acc_in, *rest):
    fold(q_ref, rest[:-1], acc_in, rest[-1])


def last_kernel(blocks, q_ref, acc_in, hidden_ref, wo_ref, *rest):
    kv_refs = rest[:blocks]
    out_hbm, acc_ref, out_ref, sems = rest[-4:]
    rows, chan = hidden_ref.shape
    many, head_dim = q_ref.shape[0], q_ref.shape[1] // 2
    width = chan // sems.shape[0]

    def finish():
        attended = jnp.concatenate(
            [
                (acc_ref[at : at + rows, :head_dim] / acc_ref[at : at + rows, head_dim:]).astype(BF16)
                for at in range(0, many, rows)
            ],
            axis=1,
        )
        copies = []
        for i in range(sems.shape[0]):
            span = slice(i * width, (i + 1) * width)
            out_ref[:, span] = (hidden_ref[:, span].astype(F32) + dot(attended, wo_ref[:, span])).astype(BF16)
            copies.append(pltpu.make_async_copy(out_ref.at[:, span], out_hbm.at[:, span], sems.at[i]))
            copies[-1].start()
        return copies

    fold(q_ref, kv_refs, acc_in, acc_ref)
    copies = finish()
    sums = acc_ref[:, head_dim:]
    good = (jnp.max(sums) <= 2.0**LIMIT) & (jnp.min(sums) >= 2.0**-LIMIT)
    for copy in copies:
        copy.wait()

    @pl.when(jnp.logical_not(good))
    def _():
        exact(q_ref, rest[:-4], acc_ref)
        for copy in finish():
            copy.wait()


def call(body, outs, args, specs=None, scratch=(), flops=0, moved=0, name=None, alias=None, out_spec=VMEM):
    return pl.pallas_call(
        body,
        out_shape=outs,
        in_specs=specs or [VMEM] * len(args),
        out_specs=jax.tree.map(lambda _: out_spec, outs),
        scratch_shapes=scratch,
        input_output_aliases=alias or {},
        compiler_params=pltpu.CompilerParams(vmem_limit_bytes=16 * 1024 * 1024),
        cost_estimate=pl.CostEstimate(flops=flops, bytes_accessed=moved, transcendentals=0),
        name=name,
    )(*args)


def shards(
    seq_in, conv_gain, convolution_weight, conv_bias, attn_gain, w_query, w_key, w_value, w_out
):
    rows, chan = seq_in.shape
    taps, _, out_chan = convolution_weight.shape
    head_dim = w_key.shape[1]
    heads = w_query.shape[1] // head_dim
    reach = DILATION_STEP * (taps - 1) // 2
    count = lax.axis_size("seq")
    shape = jax.ShapeDtypeStruct

    edges = call(
        functools.partial(edge_kernel, reach),
        shape((2 * reach, chan), BF16),
        (pltpu.with_memory_space_constraint(seq_in, pltpu.HBM),),
        specs=[pl.BlockSpec(memory_space=pltpu.HBM)],
        scratch=[pltpu.VMEM((2, 16, chan), BF16), pltpu.SemaphoreType.DMA((2,))],
        flops=LOADF,
        moved=rows * chan * 4,
        name="edges",
    )
    near = lax.ppermute(edges, "seq", [(i, i ^ 1) for i in range(count)])
    far_pairs = [(i, (i - 1 if i % 2 == 0 else i + 1) % count) for i in range(count)]
    far = lax.ppermute(edges, "seq", far_pairs)

    normed = call(norm_kernel, shape((rows, chan), BF16), (seq_in, conv_gain), flops=4 * rows * chan, name="norm")
    part = call(
        functools.partial(center_kernel, reach),
        shape((rows, out_chan), F32),
        (normed, convolution_weight),
        scratch=[pltpu.VMEM((rows + 8, out_chan), F32)] * (taps - 1),
        flops=2 * rows * chan * out_chan * taps,
        moved=rows * chan * 4 + chan * out_chan * 2,
        name="center",
    )
    hidden, attn_in, kv = call(
        functools.partial(project_kernel, reach),
        (shape((rows, chan), BF16), shape((rows, chan), BF16), shape((rows, 2 * head_dim), BF16)),
        (seq_in, part, far, near, conv_gain, convolution_weight, conv_bias, attn_gain, w_key, w_value),
        flops=2 * rows * chan * 2 * head_dim,
        name="project",
    )
    sibling = [(i, i ^ 1) for i in range(count)]
    steps = list(range(2, count, 2))
    blocks = []
    for k, step in enumerate(steps):
        other = steps[k ^ 1] if (k ^ 1) < len(steps) else step
        blocks.append(lax.ppermute(kv, "seq", [(i, i ^ (step, other)[i % 2]) for i in range(count)]))
    mate = lax.ppermute(kv, "seq", sibling)
    fold_flops = 4 * rows * rows * heads * head_dim
    q_shape, acc_shape = shape((rows * heads, 2 * head_dim), BF16), shape((rows * heads, 2 * head_dim), F32)
    q, acc = call(
        query_kernel,
        (q_shape, acc_shape),
        (attn_in, w_query, kv),
        flops=2 * rows * chan * heads * head_dim + fold_flops,
        name="query",
    )
    passed = []
    for k, block in enumerate(blocks):
        acc, block = lax.optimization_barrier((acc, block))
        blocks[k] = block
        passed.append(lax.ppermute(block, "seq", sibling))
        group = [block]
        if k == len(blocks) - 1:
            group = [mate, block, *passed[:-1]]
        acc = call(
            more_kernel,
            acc_shape,
            (q, acc, *group),
            alias={1: 0},
            flops=len(group) * fold_flops,
            name=f"fold{k}",
        )
    return call(
        functools.partial(last_kernel, 1),
        shape((rows, chan), BF16),
        (q, acc, hidden, w_out, passed[-1], *passed[:-1], kv, mate, *blocks),
        out_spec=pl.BlockSpec(memory_space=pltpu.HBM),
        scratch=[
            pltpu.VMEM(acc_shape.shape, F32),
            pltpu.VMEM((rows, chan), BF16),
            pltpu.SemaphoreType.DMA((3,)),
        ],
        flops=fold_flops + 2 * rows * chan * heads * head_dim,
        name="last",
    )


def solution(mesh):
    placed = (P(("dp", "seq"), None), P(), P(), P(), P(), P(), P(), P(), P())
    return jax.shard_map(
        shards, mesh=mesh, in_specs=placed, out_specs=P(("dp", "seq"), None), check_vma=False
    )
```

time: 23.2 us -> 21.7 us (0.935)
  starting transfers between devices: 9.79 us -> 8.95 us
  Pallas kernels: 10.8 us -> 10.3 us
    ppermute x3, starting transfers between devices: 3.53 us -> 2.71 us  [shards(): lax.ppermute(kv, 'seq', [(i, i ^ (step, other)[i % 2]) for i in range(cou...]
    pallas_call x7 -> x9, Pallas kernels: 10.8 us -> 10.3 us  [call(): pl.pallas_call(body, out_shape=outs, in_specs=specs or [VMEM] * len(args)...]
    ppermute x3, starting transfers between devices: 2.25 us -> 1.93 us  [shards(): passed.append(lax.ppermute(block, 'seq', sibling))]
    ppermute x1, starting transfers between devices: 0.56 us -> 0.85 us  [shards(): mate = lax.ppermute(kv, 'seq', sibling)]
  transfers between devices with their start and end apart: 9 -> 9, of which waited for: 1 -> 2; matrix products, arithmetic and copies ran while one was open for 0% -> 0% of each run, Pallas kernels for 23% -> 29%
where the time goes in v4:
time: 21.7 us; the launch traced here: 21.5 us
  Pallas kernels  10.3 us (47%)
  starting transfers between devices  8.95 us (41%)
  waiting for transfers between devices  2.08 us (10%)
    pallas_call x9, Pallas kernels, call(): pl.pallas_call(body, out_shape=outs, in_specs=specs or [VMEM] * len(args)...  10.3 us
    ppermute x3, starting transfers between devices, shards(): lax.ppermute(kv, 'seq', [(i, i ^ (step, other)[i % 2]) for i in range(cou...  2.71 us
    ppermute x1, starting transfers between devices, shards(): far = lax.ppermute(edges, 'seq', far_pairs)  2.67 us
    ppermute x3, waiting for transfers between devices, shards(): lax.ppermute(kv, 'seq', [(i, i ^ (step, other)[i % 2]) for i in range(cou...  2.06 us
    ppermute x3, starting transfers between devices, shards(): passed.append(lax.ppermute(block, 'seq', sibling))  1.93 us
    ppermute x1, starting transfers between devices, shards(): mate = lax.ppermute(kv, 'seq', sibling)  0.85 us
    ppermute x1, starting transfers between devices, shards(): near = lax.ppermute(edges, 'seq', [(i, i ^ 1) for i in range(count)])  0.79 us
  transfers between devices with their start and end apart: 9, of which 2 were waited for; matrix products, arithmetic and copies ran while one was open for 0% of the time, Pallas kernels for 29%

profile of v4, /device:TPU:1, one launch (start us, length us, event | category | flops | bytes accessed | tf_op | source)
XLA Modules:
  0.0 21.5 jit_solution(11705807565367108309)
XLA Ops:
  0.0 0.0 copy-start.1
  0.0 0.0 copy-start.6
  0.0 0.0 copy-start
  0.0 1.0 %edges.1 = bf16[8,1536]{1,0:T(8,128)(2,1)S(1)} custom-call(bf16[256,1536]{1,0:T(8,128)(2,1)} %x_ref.3), custom_call_target="tpu_custom_call" | custom-call | flops 8000000000 | bytes 1572864 | tf_op jit(solution)/shard_map/edges/pallas_call | solution.py:208
  1.0 2.7 %collective-permute-start = (bf16[8,1536]{1,0:T(8,128)(2,1)S(1)}, bf16[8,1536]{1,0:T(8,128)(2,1)S(1)}, u32[]{:S(2)}, u32[]{:S(2)}) collective-permute-start(bf16[8,1536]{1,0:T(8,128)(2,1)S(1)} %edges.1), channel_id=1, source_target_pairs={{0,7},{1,2},{2,1},{3,4},{4,3},{5,6},{6,5},{7,0},{8,15},{9,10},{10,... | collective-permute-start | bytes 73736 | tf_op jit(solution)/shard_map/ppermute | solution.py:244
  3.7 0.8 %collective-permute-start.1 = (bf16[8,1536]{1,0:T(8,128)(2,1)S(1)}, bf16[8,1536]{1,0:T(8,128)(2,1)S(1)}, u32[]{:S(2)}, u32[]{:S(2)}) collective-permute-start(bf16[8,1536]{1,0:T(8,128)(2,1)S(1)} %edges.1), channel_id=1, source_target_pairs={{0,1},{1,0},{2,3},{3,2},{4,5},{5,4},{6,7},{7,6},{8,9},{9,8},{10,11... | collective-permute-start | bytes 73736 | tf_op jit(solution)/shard_map/ppermute | solution.py:242
  4.5 0.0 copy-done.1
  4.5 0.0 copy-done.6
  4.5 0.3 %norm.1.normed_ref = bf16[256,1536]{1,0:T(8,128)(2,1)S(1)} custom-call(bf16[256,1536]{1,0:T(8,128)(2,1)S(1)} %copy-done.1, f32[1536]{0:T(1024)S(1)} %copy-done.6), custom_call_target="tpu_custom_call" | custom-call | flops 1572864 | tf_op jit(solution)/shard_map/norm/pallas_call | solution.py:208
  4.8 0.0 copy-done
  4.8 0.0 copy-start.4
  4.8 0.0 copy-start.5
  4.8 0.0 copy-start.7
  4.8 0.0 copy-start.8
  4.8 2.0 %center.1.part_ref = f32[256,768]{1,0:T(8,128)S(1)} custom-call(bf16[256,1536]{1,0:T(8,128)(2,1)S(1)} %norm.1.normed_ref, bf16[3,1536,768]{2,1,0:T(8,128)(2,1)S(1)} %copy-done), custom_call_target="tpu_custom_call" | custom-call | flops 1811939328 | bytes 3932160 | tf_op jit(solution)/shard_map/center/pallas_call | solution.py:208
  6.9 0.0 copy-start.2
  6.9 0.0 collective-permute-done.far_ref
  6.9 0.0 collective-permute-done.1.near_ref
  6.9 0.0 copy-done.4
  6.9 0.0 copy-done.5
  6.9 0.0 copy-done.7
  6.9 0.0 copy-done.8
  6.9 1.4 %project.1 = (bf16[256,1536]{1,0:T(8,128)(2,1)S(1)}, bf16[256,1536]{1,0:T(8,128)(2,1)S(1)}, bf16[256,256]{1,0:T(8,128)(2,1)S(1)}) custom-call(bf16[256,1536]{1,0:T(8,128)(2,1)S(1)} %copy-done.1, f32[256,768]{1,0:T(8,128)S(1)} %center.1.part_ref, bf16[8,1536]{1,0:T(8,128)(2,1)S(1)} %collective-permute-done.far_ref, ...), custom_call_target="tpu_custom_call" | custom-call | flops 201326592 | tf_op jit(solution)/shard_map/project/pallas_call | solution.py:208
  8.3 0.7 %collective-permute-start.2 = (bf16[256,256]{1,0:T(8,128)(2,1)S(1)}, bf16[256,256]{1,0:T(8,128)(2,1)S(1)}, u32[]{:S(2)}, u32[]{:S(2)}) collective-permute-start(bf16[256,256]{1,0:T(8,128)(2,1)S(1)} %get-tuple-element.17.kv_ref.rest_3_), channel_id=1, source_target_pairs={{0,2},{1,5},{2,0},{3,7},{4,6},{5,1},{6,4},{7,3},{8,10},{9,13},{10,... | collective-permute-start | bytes 393224 | tf_op jit(solution)/shard_map/ppermute | solution.py:268
  9.0 1.2 %collective-permute-start.3 = (bf16[256,256]{1,0:T(8,128)(2,1)S(1)}, bf16[256,256]{1,0:T(8,128)(2,1)S(1)}, u32[]{:S(2)}, u32[]{:S(2)}) collective-permute-start(bf16[256,256]{1,0:T(8,128)(2,1)S(1)} %get-tuple-element.17.kv_ref.rest_3_), channel_id=1, source_target_pairs={{0,4},{1,3},{2,6},{3,1},{4,0},{5,7},{6,2},{7,5},{8,12},{9,11},{10,... | collective-permute-start | bytes 393224 | tf_op jit(solution)/shard_map/ppermute | solution.py:268
  10.2 0.8 %collective-permute-start.4 = (bf16[256,256]{1,0:T(8,128)(2,1)S(1)}, bf16[256,256]{1,0:T(8,128)(2,1)S(1)}, u32[]{:S(2)}, u32[]{:S(2)}) collective-permute-start(bf16[256,256]{1,0:T(8,128)(2,1)S(1)} %get-tuple-element.17.kv_ref.rest_3_), channel_id=1, source_target_pairs={{0,6},{1,7},{2,4},{3,5},{4,2},{5,3},{6,0},{7,1},{8,14},{9,15},{10,... | collective-permute-start | bytes 393224 | tf_op jit(solution)/shard_map/ppermute | solution.py:268
  11.0 0.9 %collective-permute-start.5 = (bf16[256,256]{1,0:T(8,128)(2,1)S(1)}, bf16[256,256]{1,0:T(8,128)(2,1)S(1)}, u32[]{:S(2)}, u32[]{:S(2)}) collective-permute-start(bf16[256,256]{1,0:T(8,128)(2,1)S(1)} %get-tuple-element.17.kv_ref.rest_3_), channel_id=1, source_target_pairs={{0,1},{1,0},{2,3},{3,2},{4,5},{5,4},{6,7},{7,6},{8,9},{9,8},{10,11... | collective-permute-start | bytes 393224 | tf_op jit(solution)/shard_map/ppermute | solution.py:269
  11.9 0.0 copy-done.2
  11.9 1.1 %query.1 = (bf16[1024,256]{1,0:T(8,128)(2,1)S(1)}, f32[1024,256]{1,0:T(8,128)S(1)}) custom-call(bf16[256,1536]{1,0:T(8,128)(2,1)S(1)} %get-tuple-element.16.attn_ref, bf16[1536,512]{1,0:T(8,128)(2,1)S(1)} %copy-done.2, bf16[256,256]{1,0:T(8,128)(2,1)S(1)} %get-tuple-element.17.kv_ref.rest_3_), custom_call_target="tpu_custom_call" | custom-call | flops 536870912 | tf_op jit(solution)/shard_map/query/pallas_call | solution.py:208
  13.0 0.0 collective-permute-done.2.rest_0_.rest_5_
  13.0 0.6 %fold0.1.acc_in = f32[1024,256]{1,0:T(8,128)S(1)} custom-call(bf16[1024,256]{1,0:T(8,128)(2,1)S(1)} %get-tuple-element.18.q_ref, f32[1024,256]{1,0:T(8,128)S(1)} %get-tuple-element.20.acc_in, bf16[256,256]{1,0:T(8,128)(2,1)S(1)} %collective-permute-done.2.rest_0_.rest_5_), custom_call_target="tpu_custom_call", output_to_operand_aliasing={{}: (1, {})} | custom-call | flops 134217728 | tf_op jit(solution)/shard_map/fold0/pallas_call | solution.py:208
  13.6 0.7 %collective-permute-done.3.rest_0_.rest_6_ = bf16[256,256]{1,0:T(8,128)(2,1)S(1)} collective-permute-done((bf16[256,256]{1,0:T(8,128)(2,1)S(1)}, bf16[256,256]{1,0:T(8,128)(2,1)S(1)}, u32[]{:S(2)}, u32[]{:S(2)}) %collective-permute-start.3) | collective-permute-done | bytes 131104 | tf_op jit(solution)/shard_map/ppermute | solution.py:268
  14.4 1.0 %collective-permute-start.7 = (bf16[256,256]{1,0:T(8,128)(2,1)S(1)}, bf16[256,256]{1,0:T(8,128)(2,1)S(1)}, u32[]{:S(2)}, u32[]{:S(2)}) collective-permute-start(bf16[256,256]{1,0:T(8,128)(2,1)S(1)} %collective-permute-done.3.rest_0_.rest_6_), channel_id=1, source_target_pairs={{0,1},{1,0},{2,3},{3,2},{4,5},{5,4},{6,7},{7,6},{8,9},{9,8},{10,11... | collective-permute-start | bytes 393224 | tf_op jit(solution)/shard_map/ppermute | solution.py:283
  15.4 0.1 collective-permute-start.6
  15.4 0.6 %fold1.1.acc_in = f32[1024,256]{1,0:T(8,128)S(1)} custom-call(bf16[1024,256]{1,0:T(8,128)(2,1)S(1)} %get-tuple-element.18.q_ref, f32[1024,256]{1,0:T(8,128)S(1)} %fold0.1.acc_in, bf16[256,256]{1,0:T(8,128)(2,1)S(1)} %collective-permute-done.3.rest_0_.rest_6_), custom_call_target="tpu_custom_call", output_to_operand_aliasing={{}: (1, {})} | custom-call | flops 134217728 | tf_op jit(solution)/shard_map/fold1/pallas_call | solution.py:208
  16.1 0.0 copy-start.3
  16.1 1.3 %collective-permute-done.4.rest_1_.rest_7_ = bf16[256,256]{1,0:T(8,128)(2,1)S(1)} collective-permute-done((bf16[256,256]{1,0:T(8,128)(2,1)S(1)}, bf16[256,256]{1,0:T(8,128)(2,1)S(1)}, u32[]{:S(2)}, u32[]{:S(2)}) %collective-permute-start.4) | collective-permute-done | bytes 131104 | tf_op jit(solution)/shard_map/ppermute | solution.py:268
  17.4 0.9 %collective-permute-start.8 = (bf16[256,256]{1,0:T(8,128)(2,1)S(1)}, bf16[256,256]{1,0:T(8,128)(2,1)S(1)}, u32[]{:S(2)}, u32[]{:S(2)}) collective-permute-start(bf16[256,256]{1,0:T(8,128)(2,1)S(1)} %collective-permute-done.4.rest_1_.rest_7_), channel_id=1, source_target_pairs={{0,1},{1,0},{2,3},{3,2},{4,5},{5,4},{6,7},{7,6},{8,9},{9,8},{10,11... | collective-permute-start | bytes 393224 | tf_op jit(solution)/shard_map/ppermute | solution.py:283
  18.3 0.0 collective-permute-done.5.rest_0_.rest_4_
  18.3 0.0 collective-permute-done.7.rest_3_.rest_2_
  18.3 0.0 collective-permute-done.6.rest_2_.rest_1_
  18.3 1.5 %fold2.1.acc_in = f32[1024,256]{1,0:T(8,128)S(1)} custom-call(bf16[1024,256]{1,0:T(8,128)(2,1)S(1)} %get-tuple-element.18.q_ref, f32[1024,256]{1,0:T(8,128)S(1)} %fold1.1.acc_in, bf16[256,256]{1,0:T(8,128)(2,1)S(1)} %collective-permute-done.5.rest_0_.rest_4_, ...), custom_call_target="tpu_custom_call", output_to_operand_aliasing={{}: (1, {})} | custom-call | flops 536870912 | tf_op jit(solution)/shard_map/fold2/pallas_call | solution.py:208
  19.8 0.0 collective-permute-done.8.rest_0_
  19.8 0.0 copy-done.3
  19.8 1.8 %last.1 = bf16[256,1536]{1,0:T(8,128)(2,1)} custom-call(bf16[1024,256]{1,0:T(8,128)(2,1)S(1)} %get-tuple-element.18.q_ref, f32[1024,256]{1,0:T(8,128)S(1)} %fold2.1.acc_in, bf16[256,1536]{1,0:T(8,128)(2,1)S(1)} %get-tuple-element.26.hidden_ref, bf16[512,1536]{1,0:T(8,128)(2,1)S(1)} %copy-done.3, bf16[256,256]{1,0:T(8,128)(2,1)S(1)} %collective-permute-done.8.rest_0_, ...), custom_call_target="tpu_custom_call" | custom-call | flops 536870912 | tf_op jit(solution)/shard_map/last/pallas_call | solution.py:208
Async XLA Ops:
  0.0 4.5 %copy-start.1 = (bf16[256,1536]{1,0:T(8,128)(2,1)S(1)}, bf16[256,1536]{1,0:T(8,128)(2,1)}, u32[]{:S(2)}) copy-start(bf16[256,1536]{1,0:T(8,128)(2,1)} %x_ref.3) | copy-start | bytes 2359300
  0.0 4.5 %copy-start.6 = (f32[1536]{0:T(1024)S(1)}, f32[1536]{0:T(1024)}, u32[]{:S(2)}) copy-start(f32[1536]{0:T(1024)} %gain_ref.3) | copy-start | bytes 18436
  0.0 4.8 %copy-start = (bf16[3,1536,768]{2,1,0:T(8,128)(2,1)S(1)}, bf16[3,1536,768]{2,1,0:T(8,128)(2,1)}, u32[]{:S(2)}) copy-start(bf16[3,1536,768]{2,1,0:T(8,128)(2,1)} %w_ref.3) | copy-start | bytes 21233668
  1.0 5.9 %collective-permute-start = (bf16[8,1536]{1,0:T(8,128)(2,1)S(1)}, bf16[8,1536]{1,0:T(8,128)(2,1)S(1)}, u32[]{:S(2)}, u32[]{:S(2)}) collective-permute-start(bf16[8,1536]{1,0:T(8,128)(2,1)S(1)} %edges.1), channel_id=1, source_target_pairs={{0,7},{1,2},{2,1},{3,4},{4,3},{5,6},{6,5},{7,0},{8,15},{9,10},{10,... | collective-permute-start | bytes 73736 | tf_op jit(solution)/shard_map/ppermute | solution.py:244
  3.7 3.2 %collective-permute-start.1 = (bf16[8,1536]{1,0:T(8,128)(2,1)S(1)}, bf16[8,1536]{1,0:T(8,128)(2,1)S(1)}, u32[]{:S(2)}, u32[]{:S(2)}) collective-permute-start(bf16[8,1536]{1,0:T(8,128)(2,1)S(1)} %edges.1), channel_id=1, source_target_pairs={{0,1},{1,0},{2,3},{3,2},{4,5},{5,4},{6,7},{7,6},{8,9},{9,8},{10,11... | collective-permute-start | bytes 73736 | tf_op jit(solution)/shard_map/ppermute | solution.py:242
  4.8 2.1 %copy-start.4 = (bf16[1536,128]{1,0:T(8,128)(2,1)S(1)}, bf16[1536,128]{1,0:T(8,128)(2,1)}, u32[]{:S(2)}) copy-start(bf16[1536,128]{1,0:T(8,128)(2,1)} %wk_ref.1) | copy-start | bytes 1179652
  4.8 2.1 %copy-start.5 = (bf16[1536,128]{1,0:T(8,128)(2,1)S(1)}, bf16[1536,128]{1,0:T(8,128)(2,1)}, u32[]{:S(2)}) copy-start(bf16[1536,128]{1,0:T(8,128)(2,1)} %wv_ref.1) | copy-start | bytes 1179652
  4.8 2.1 %copy-start.7 = (f32[1536]{0:T(1024)S(1)}, f32[1536]{0:T(1024)}, u32[]{:S(2)}) copy-start(f32[1536]{0:T(1024)} %again_ref.1) | copy-start | bytes 18436
  4.8 2.1 %copy-start.8 = (f32[768]{0:T(1024)S(1)}, f32[768]{0:T(1024)}, u32[]{:S(2)}) copy-start(f32[768]{0:T(1024)} %bias_ref.1) | copy-start | bytes 9220
  6.9 5.0 %copy-start.2 = (bf16[1536,512]{1,0:T(8,128)(2,1)S(1)}, bf16[1536,512]{1,0:T(8,128)(2,1)}, u32[]{:S(2)}) copy-start(bf16[1536,512]{1,0:T(8,128)(2,1)} %wq_ref.1) | copy-start | bytes 4718596
  8.3 4.7 %collective-permute-start.2 = (bf16[256,256]{1,0:T(8,128)(2,1)S(1)}, bf16[256,256]{1,0:T(8,128)(2,1)S(1)}, u32[]{:S(2)}, u32[]{:S(2)}) collective-permute-start(bf16[256,256]{1,0:T(8,128)(2,1)S(1)} %get-tuple-element.17.kv_ref.rest_3_), channel_id=1, source_target_pairs={{0,2},{1,5},{2,0},{3,7},{4,6},{5,1},{6,4},{7,3},{8,10},{9,13},{10,... | collective-permute-start | bytes 393224 | tf_op jit(solution)/shard_map/ppermute | solution.py:268
  9.0 5.4 %collective-permute-start.3 = (bf16[256,256]{1,0:T(8,128)(2,1)S(1)}, bf16[256,256]{1,0:T(8,128)(2,1)S(1)}, u32[]{:S(2)}, u32[]{:S(2)}) collective-permute-start(bf16[256,256]{1,0:T(8,128)(2,1)S(1)} %get-tuple-element.17.kv_ref.rest_3_), channel_id=1, source_target_pairs={{0,4},{1,3},{2,6},{3,1},{4,0},{5,7},{6,2},{7,5},{8,12},{9,11},{10,... | collective-permute-start | bytes 393224 | tf_op jit(solution)/shard_map/ppermute | solution.py:268
  10.2 7.2 %collective-permute-start.4 = (bf16[256,256]{1,0:T(8,128)(2,1)S(1)}, bf16[256,256]{1,0:T(8,128)(2,1)S(1)}, u32[]{:S(2)}, u32[]{:S(2)}) collective-permute-start(bf16[256,256]{1,0:T(8,128)(2,1)S(1)} %get-tuple-element.17.kv_ref.rest_3_), channel_id=1, source_target_pairs={{0,6},{1,7},{2,4},{3,5},{4,2},{5,3},{6,0},{7,1},{8,14},{9,15},{10,... | collective-permute-start | bytes 393224 | tf_op jit(solution)/shard_map/ppermute | solution.py:268
  11.0 7.3 %collective-permute-start.5 = (bf16[256,256]{1,0:T(8,128)(2,1)S(1)}, bf16[256,256]{1,0:T(8,128)(2,1)S(1)}, u32[]{:S(2)}, u32[]{:S(2)}) collective-permute-start(bf16[256,256]{1,0:T(8,128)(2,1)S(1)} %get-tuple-element.17.kv_ref.rest_3_), channel_id=1, source_target_pairs={{0,1},{1,0},{2,3},{3,2},{4,5},{5,4},{6,7},{7,6},{8,9},{9,8},{10,11... | collective-permute-start | bytes 393224 | tf_op jit(solution)/shard_map/ppermute | solution.py:269
  14.4 3.9 %collective-permute-start.7 = (bf16[256,256]{1,0:T(8,128)(2,1)S(1)}, bf16[256,256]{1,0:T(8,128)(2,1)S(1)}, u32[]{:S(2)}, u32[]{:S(2)}) collective-permute-start(bf16[256,256]{1,0:T(8,128)(2,1)S(1)} %collective-permute-done.3.rest_0_.rest_6_), channel_id=1, source_target_pairs={{0,1},{1,0},{2,3},{3,2},{4,5},{5,4},{6,7},{7,6},{8,9},{9,8},{10,11... | collective-permute-start | bytes 393224 | tf_op jit(solution)/shard_map/ppermute | solution.py:283
  15.4 2.9 %collective-permute-start.6 = (bf16[256,256]{1,0:T(8,128)(2,1)S(1)}, bf16[256,256]{1,0:T(8,128)(2,1)S(1)}, u32[]{:S(2)}, u32[]{:S(2)}) collective-permute-start(bf16[256,256]{1,0:T(8,128)(2,1)S(1)} %collective-permute-done.2.rest_0_.rest_5_), channel_id=1, source_target_pairs={{0,1},{1,0},{2,3},{3,2},{4,5},{5,4},{6,7},{7,6},{8,9},{9,8},{10,11... | collective-permute-start | bytes 393224 | tf_op jit(solution)/shard_map/ppermute | solution.py:283
  16.1 3.7 %copy-start.3 = (bf16[512,1536]{1,0:T(8,128)(2,1)S(1)}, bf16[512,1536]{1,0:T(8,128)(2,1)}, u32[]{:S(2)}) copy-start(bf16[512,1536]{1,0:T(8,128)(2,1)} %wo_ref.1) | copy-start | bytes 4718596
  17.4 2.4 %collective-permute-start.8 = (bf16[256,256]{1,0:T(8,128)(2,1)S(1)}, bf16[256,256]{1,0:T(8,128)(2,1)S(1)}, u32[]{:S(2)}, u32[]{:S(2)}) collective-permute-start(bf16[256,256]{1,0:T(8,128)(2,1)S(1)} %collective-permute-done.4.rest_1_.rest_7_), channel_id=1, source_target_pairs={{0,1},{1,0},{2,3},{3,2},{4,5},{5,4},{6,7},{7,6},{8,9},{9,8},{10,11... | collective-permute-start | bytes 393224 | tf_op jit(solution)/shard_map/ppermute | solution.py:283

commit v5 on v4

--- a/solution.py
+++ b/solution.py
@@ -49,51 +49,54 @@
     normed_ref[...] = normed_rows(x_ref[...], gain_ref[...]).astype(BF16)
 
 
-def center_kernel(reach, normed_ref, w_ref, part_ref, *shift_refs):
-    rows = normed_ref.shape[0]
+def center_kernel(reach, normed_ref, near_ref, gain_ref, w_ref, part_ref, *shift_refs):
+    rows, chan = normed_ref.shape
     taps, _, out_chan = w_ref.shape
     total = dot(normed_ref[...], w_ref[(taps - 1) // 2])
+    even = lax.rem(lax.axis_index("seq"), 2) == 0
+    near = normed_rows(near_ref[...], gain_ref[...])
+    row = lax.broadcasted_iota(jnp.int32, (2 * reach, 1), 0)
+    left = jnp.where((row >= reach) & jnp.logical_not(even), near, 0.0)
+    right = jnp.where((row < reach) & even, near, 0.0)
+    line = jnp.concatenate([normed_ref[...], jnp.concatenate([left, right], axis=0).astype(BF16)], axis=0)
     slots = iter(shift_refs)
     for tap in range(taps):
         shift = (tap - (taps - 1) // 2) * DILATION_STEP
         if shift == 0:
             continue
         shift_ref = next(slots)
-        edge = shift_ref.shape[0] - rows
-        first = edge if shift < 0 else 0
-        shift_ref[0 if shift < 0 else rows : edge if shift < 0 else rows + edge, :] = jnp.zeros((edge, out_chan), F32)
-        shift_ref[first : first + rows, :] = dot(normed_ref[...], w_ref[tap])
-        total = total + shift_ref[first + shift : first + shift + rows, :]
+        product = dot(line, w_ref[tap])
+        if shift < 0:
+            shift_ref[0 : 2 * reach, :] = product[rows : rows + 2 * reach]
+            shift_ref[2 * reach :, :] = product[0:rows]
+            total = total + shift_ref[2 * reach + shift : 2 * reach + shift + rows, :]
+        else:
+            shift_ref[0:rows, :] = product[0:rows]
+            shift_ref[rows:, :] = product[rows + 2 * reach : rows + 4 * reach]
+            total = total + shift_ref[shift : shift + rows, :]
     part_ref[...] = total
 
 
 def project_kernel(
-    reach, x_ref, part_ref, far_ref, near_ref, gain_ref, w_ref, bias_ref, again_ref, wk_ref, wv_ref,
+    reach, x_ref, part_ref, far_ref, gain_ref, w_ref, bias_ref, again_ref, wk_ref, wv_ref,
     hidden_ref, attn_ref, kv_ref,
 ):
     rows, chan = x_ref.shape
     taps, _, out_chan = w_ref.shape
     index, count = lax.axis_index("seq"), lax.axis_size("seq")
     even = lax.rem(index, 2) == 0
-    near, far = near_ref[...].astype(F32), far_ref[...].astype(F32)
-    left = jnp.where(even, far, near)
-    right = jnp.where(even, near, far)
-    row = lax.broadcasted_iota(jnp.int32, (2 * reach, 1), 0)
-    left = jnp.where((row >= reach) & (index > 0), normed_rows(left, gain_ref[...]), 0.0)
-    right = jnp.where((row < reach) & (index < count - 1), normed_rows(right, gain_ref[...]), 0.0)
-    around = jnp.concatenate([left, right], axis=0).astype(BF16)
+    outside = (index == 0) | (index == count - 1)
+    far = jnp.where(outside, 0.0, normed_rows(far_ref[...], gain_ref[...]))
+    far = jnp.concatenate([far, jnp.zeros_like(far)], axis=0).astype(BF16)
     edge = 16 * pl.cdiv(reach, 16)
     top, bottom = part_ref[0:edge, :], part_ref[rows - edge :, :]
-    for tap in range(taps):
-        shift = (tap - (taps - 1) // 2) * DILATION_STEP
-        if shift == 0:
-            continue
-        extra = dot(around, w_ref[tap])
-        blank = jnp.zeros((edge - abs(shift), out_chan), F32)
-        if shift < 0:
-            top = top + jnp.concatenate([extra[2 * reach + shift : 2 * reach], blank], axis=0)
-        else:
-            bottom = bottom + jnp.concatenate([blank, extra[2 * reach : 2 * reach + shift]], axis=0)
+    middle = (taps - 1) // 2
+    for away in range(1, middle + 1):
+        shift = away * DILATION_STEP
+        extra = dot(far, w_ref[jnp.where(even, middle - away, middle + away)])
+        blank = jnp.zeros((edge - shift, out_chan), F32)
+        top = top + jnp.where(even, jnp.concatenate([extra[2 * reach - shift : 2 * reach], blank], axis=0), 0.0)
+        bottom = bottom + jnp.where(even, 0.0, jnp.concatenate([blank, extra[0:shift]], axis=0))
 
     def activate(span, total):
         activated = jax.nn.gelu(total + bias_ref[...], approximate=True)
@@ -102,10 +105,16 @@
         hidden_ref[span, :] = hidden
         attn_ref[span, :] = normed_rows(hidden, again_ref[...]).astype(BF16)
 
-    activate(slice(edge, rows - edge), part_ref[edge : rows - edge, :])
+    both = jnp.concatenate([wk_ref[...], wv_ref[...]], axis=1)
+    for span in (slice(edge, rows // 2), slice(rows // 2, rows - edge)):
+        activate(span, part_ref[span, :])
+        kv_ref[span, :] = dot(attn_ref[span, :], both).astype(BF16)
     activate(slice(0, edge), top)
     activate(slice(rows - edge, rows), bottom)
-    kv_ref[...] = dot(attn_ref[...], jnp.concatenate([wk_ref[...], wv_ref[...]], axis=1)).astype(BF16)
+    ends = jnp.concatenate([attn_ref[0:edge, :], attn_ref[rows - edge :, :]], axis=0)
+    ends = dot(ends, both).astype(BF16)
+    kv_ref[0:edge, :] = ends[:edge]
+    kv_ref[rows - edge :, :] = ends[edge:]
 
 
 def key_side(kv, head_dim):
@@ -120,24 +129,27 @@
 
 def fold(q_ref, kv_refs, acc_in, acc_out):
     many, head_dim = q_ref.shape[0], q_ref.shape[1] // 2
+    scale = LOG2E * head_dim**-0.5
     step = math.gcd(many, 256)
     pairs = [(key_side(kv, head_dim), value_side(kv, head_dim)) for kv in kv_refs]
     for at in range(0, many, step):
         span = slice(at, at + step)
         total = acc_in[span, :]
         for keys, values in pairs:
-            weights = jnp.exp2(jnp.minimum(dot(q_ref[span, :], keys), CEILING))
+            scores = dot(q_ref[span, :], keys) * scale
+            weights = jnp.exp2(jnp.minimum(scores, CEILING))
             total = total + dot(weights.astype(BF16), values)
         acc_out[span, :] = total
 
 
 def exact(q_ref, kv_refs, acc_out):
     many, head_dim = q_ref.shape[0], q_ref.shape[1] // 2
+    scale = LOG2E * head_dim**-0.5
     step = math.gcd(many, 256)
     pairs = [(kv[:, :head_dim].T, value_side(kv, head_dim)) for kv in kv_refs]
     for at in range(0, many, step):
         span = slice(at, at + step)
-        scores = [dot(q_ref[span, :head_dim], keys) for keys, _ in pairs]
+        scores = [dot(q_ref[span, :head_dim], keys) * scale for keys, _ in pairs]
         top = jnp.max(functools.reduce(jnp.maximum, scores), axis=-1, keepdims=True)
         total = None
         for s, (_, values) in zip(scores, pairs):
@@ -154,13 +166,13 @@
     keys, values = kv_ref[:, :head_dim].T, value_side(kv_ref, head_dim)
     for h in range(wq_ref.shape[1] // head_dim):
         span = slice(h * rows, (h + 1) * rows)
-        q_head = (q[:, h * head_dim : (h + 1) * head_dim] * scale).astype(BF16)
+        q_head = q[:, h * head_dim : (h + 1) * head_dim].astype(BF16)
         scores = dot(q_head, keys)
         top = jnp.broadcast_to(jnp.max(scores, axis=-1, keepdims=True), (rows, head_dim)).astype(BF16)
         q_ref[span, :head_dim] = q_head
         q_ref[span, head_dim:] = -top
         top = jnp.concatenate([top.astype(F32)] * (scores.shape[1] // head_dim), axis=1)
-        acc_ref[span, :] = dot(jnp.exp2(scores - top).astype(BF16), values)
+        acc_ref[span, :] = dot(jnp.exp2((scores - top) * scale).astype(BF16), values)
 
 
 def more_kernel(q_ref, acc_in, *rest):
@@ -247,8 +259,8 @@
     part = call(
         functools.partial(center_kernel, reach),
         shape((rows, out_chan), F32),
-        (normed, convolution_weight),
-        scratch=[pltpu.VMEM((rows + 8, out_chan), F32)] * (taps - 1),
+        (normed, near, conv_gain, convolution_weight),
+        scratch=[pltpu.VMEM((rows + 2 * reach, out_chan), F32)] * (taps - 1),
         flops=2 * rows * chan * out_chan * taps,
         moved=rows * chan * 4 + chan * out_chan * 2,
         name="center",
@@ -256,16 +268,16 @@
     hidden, attn_in, kv = call(
         functools.partial(project_kernel, reach),
         (shape((rows, chan), BF16), shape((rows, chan), BF16), shape((rows, 2 * head_dim), BF16)),
-        (seq_in, part, far, near, conv_gain, convolution_weight, conv_bias, attn_gain, w_key, w_value),
+        (seq_in, part, far, conv_gain, convolution_weight, conv_bias, attn_gain, w_key, w_value),
         flops=2 * rows * chan * 2 * head_dim,
         name="project",
     )
-    sibling = [(i, i ^ 1) for i in range(count)]
     steps = list(range(2, count, 2))
     blocks = []
     for k, step in enumerate(steps):
         other = steps[k ^ 1] if (k ^ 1) < len(steps) else step
         blocks.append(lax.ppermute(kv, "seq", [(i, i ^ (step, other)[i % 2]) for i in range(count)]))
+    sibling = [(i, i ^ 1) for i in range(count)]
     mate = lax.ppermute(kv, "seq", sibling)
     fold_flops = 4 * rows * rows * heads * head_dim
     q_shape, acc_shape = shape((rows * heads, 2 * head_dim), BF16), shape((rows * heads, 2 * head_dim), F32)

time: 21.7 us -> 21.1 us (0.972)
  waiting for transfers between devices: 2.08 us -> 0.02 us
  starting transfers between devices: 8.95 us -> 10.5 us
    ppermute x3, waiting for transfers between devices: 2.06 us -> 0.01 us  [shards(): lax.ppermute(kv, 'seq', [(i, i ^ (step, other)[i % 2]) for i in range(cou...]
    ppermute x1, starting transfers between devices: 0.85 us -> 1.97 us  [shards(): mate = lax.ppermute(kv, 'seq', sibling)]
    ppermute x3, starting transfers between devices: 1.93 us -> 2.8 us  [shards(): passed.append(lax.ppermute(block, 'seq', sibling))]
    ppermute x1, starting transfers between devices: 0.79 us -> 0.12 us  [shards(): near = lax.ppermute(edges, 'seq', [(i, i ^ 1) for i in range(count)])]
    ppermute x3, starting transfers between devices: 2.71 us -> 2.97 us  [shards(): lax.ppermute(kv, 'seq', [(i, i ^ (step, other)[i % 2]) for i in range(cou...]
  transfers between devices with their start and end apart: 9 -> 9, of which waited for: 2 -> 0; matrix products, arithmetic and copies ran while one was open for 0% -> 0% of each run, Pallas kernels for 29% -> 30%
where the time goes in v5:
time: 21.1 us; the launch traced here: 20.9 us
  starting transfers between devices  10.5 us (50%)
  Pallas kernels  10.2 us (48%)
    pallas_call x9, Pallas kernels, call(): pl.pallas_call(body, out_shape=outs, in_specs=specs or [VMEM] * len(args)...  10.2 us
    ppermute x3, starting transfers between devices, shards(): lax.ppermute(kv, 'seq', [(i, i ^ (step, other)[i % 2]) for i in range(cou...  2.97 us
    ppermute x3, starting transfers between devices, shards(): passed.append(lax.ppermute(block, 'seq', sibling))  2.8 us
    ppermute x1, starting transfers between devices, shards(): far = lax.ppermute(edges, 'seq', far_pairs)  2.63 us
    ppermute x1, starting transfers between devices, shards(): mate = lax.ppermute(kv, 'seq', sibling)  1.97 us
  transfers between devices with their start and end apart: 9, of which 0 were waited for; matrix products, arithmetic and copies ran while one was open for 0% of the time, Pallas kernels for 30%

profile of v5, /device:TPU:1, one launch (start us, length us, event | category | flops | bytes accessed | tf_op | source)
XLA Modules:
  0.0 20.9 jit_solution(5725344870248355955)
XLA Ops:
  0.0 0.0 copy-start.1
  0.0 0.0 copy-start.6
  0.0 0.0 copy-start
  0.0 1.0 %edges.1 = bf16[8,1536]{1,0:T(8,128)(2,1)S(1)} custom-call(bf16[256,1536]{1,0:T(8,128)(2,1)} %x_ref.3), custom_call_target="tpu_custom_call" | custom-call | flops 8000000000 | bytes 1572864 | tf_op jit(solution)/shard_map/edges/pallas_call | solution.py:220
  1.0 0.1 collective-permute-start
  1.1 2.6 %collective-permute-start.1 = (bf16[8,1536]{1,0:T(8,128)(2,1)S(1)}, bf16[8,1536]{1,0:T(8,128)(2,1)S(1)}, u32[]{:S(2)}, u32[]{:S(2)}) collective-permute-start(bf16[8,1536]{1,0:T(8,128)(2,1)S(1)} %edges.1), channel_id=1, source_target_pairs={{0,7},{1,2},{2,1},{3,4},{4,3},{5,6},{6,5},{7,0},{8,15},{9,10},{10,... | collective-permute-start | bytes 73736 | tf_op jit(solution)/shard_map/ppermute | solution.py:256
  3.8 0.0 copy-done.1
  3.8 0.0 copy-done.6
  3.8 0.3 %norm.1.normed_ref = bf16[256,1536]{1,0:T(8,128)(2,1)S(1)} custom-call(bf16[256,1536]{1,0:T(8,128)(2,1)S(1)} %copy-done.1, f32[1536]{0:T(1024)S(1)} %copy-done.6), custom_call_target="tpu_custom_call" | custom-call | flops 1572864 | tf_op jit(solution)/shard_map/norm/pallas_call | solution.py:220
  4.1 0.0 copy-start.4
  4.1 0.0 copy-start.5
  4.1 0.0 copy-start.7
  4.1 0.0 copy-start.8
  4.1 0.0 collective-permute-done.near_ref
  4.1 0.0 copy-done
  4.1 2.1 %center.1.part_ref = f32[256,768]{1,0:T(8,128)S(1)} custom-call(bf16[256,1536]{1,0:T(8,128)(2,1)S(1)} %norm.1.normed_ref, bf16[8,1536]{1,0:T(8,128)(2,1)S(1)} %collective-permute-done.near_ref, f32[1536]{0:T(1024)S(1)} %copy-done.6, bf16[3,1536,768]{2,1,0:T(8,128)(2,1)S(1)} %copy-done), custom_call_target="tpu_custom_call" | custom-call | flops 1811939328 | bytes 3932160 | tf_op jit(solution)/shard_map/center/pallas_call | solution.py:220
  6.2 0.0 copy-start.2
  6.3 0.0 collective-permute-done.1.far_ref
  6.3 0.0 copy-done.4
  6.3 0.0 copy-done.5
  6.3 0.0 copy-done.7
  6.3 0.0 copy-done.8
  6.3 1.2 %project.1 = (bf16[256,1536]{1,0:T(8,128)(2,1)S(1)}, bf16[256,1536]{1,0:T(8,128)(2,1)S(1)}, bf16[256,256]{1,0:T(8,128)(2,1)S(1)}) custom-call(bf16[256,1536]{1,0:T(8,128)(2,1)S(1)} %copy-done.1, f32[256,768]{1,0:T(8,128)S(1)} %center.1.part_ref, bf16[8,1536]{1,0:T(8,128)(2,1)S(1)} %collective-permute-done.1.far_ref, f32[1536]{0:T(1024)S(1)} %copy-done.6, ...), custom_call_target="tpu_custom_call" | custom-call | flops 201326592 | tf_op jit(solution)/shard_map/project/pallas_call | solution.py:220
  7.5 1.3 %collective-permute-start.2 = (bf16[256,256]{1,0:T(8,128)(2,1)S(1)}, bf16[256,256]{1,0:T(8,128)(2,1)S(1)}, u32[]{:S(2)}, u32[]{:S(2)}) collective-permute-start(bf16[256,256]{1,0:T(8,128)(2,1)S(1)} %get-tuple-element.17.kv_ref.rest_3_), channel_id=1, source_target_pairs={{0,2},{1,5},{2,0},{3,7},{4,6},{5,1},{6,4},{7,3},{8,10},{9,13},{10,... | collective-permute-start | bytes 393224 | tf_op jit(solution)/shard_map/ppermute | solution.py:279
  8.9 1.6 %collective-permute-start.3 = (bf16[256,256]{1,0:T(8,128)(2,1)S(1)}, bf16[256,256]{1,0:T(8,128)(2,1)S(1)}, u32[]{:S(2)}, u32[]{:S(2)}) collective-permute-start(bf16[256,256]{1,0:T(8,128)(2,1)S(1)} %get-tuple-element.17.kv_ref.rest_3_), channel_id=1, source_target_pairs={{0,4},{1,3},{2,6},{3,1},{4,0},{5,7},{6,2},{7,5},{8,12},{9,11},{10,... | collective-permute-start | bytes 393224 | tf_op jit(solution)/shard_map/ppermute | solution.py:279
  10.5 0.0 collective-permute-start.4
  10.5 2.0 %collective-permute-start.5 = (bf16[256,256]{1,0:T(8,128)(2,1)S(1)}, bf16[256,256]{1,0:T(8,128)(2,1)S(1)}, u32[]{:S(2)}, u32[]{:S(2)}) collective-permute-start(bf16[256,256]{1,0:T(8,128)(2,1)S(1)} %get-tuple-element.17.kv_ref.rest_3_), channel_id=1, source_target_pairs={{0,1},{1,0},{2,3},{3,2},{4,5},{5,4},{6,7},{7,6},{8,9},{9,8},{10,11... | collective-permute-start | bytes 393224 | tf_op jit(solution)/shard_map/ppermute | solution.py:281
  12.5 0.0 copy-done.2
  12.5 1.1 %query.1 = (bf16[1024,256]{1,0:T(8,128)(2,1)S(1)}, f32[1024,256]{1,0:T(8,128)S(1)}) custom-call(bf16[256,1536]{1,0:T(8,128)(2,1)S(1)} %get-tuple-element.16.attn_ref, bf16[1536,512]{1,0:T(8,128)(2,1)S(1)} %copy-done.2, bf16[256,256]{1,0:T(8,128)(2,1)S(1)} %get-tuple-element.17.kv_ref.rest_3_), custom_call_target="tpu_custom_call" | custom-call | flops 536870912 | tf_op jit(solution)/shard_map/query/pallas_call | solution.py:220
  13.6 0.0 collective-permute-done.2.rest_0_.rest_5_
  13.6 0.6 %fold0.1.acc_in = f32[1024,256]{1,0:T(8,128)S(1)} custom-call(bf16[1024,256]{1,0:T(8,128)(2,1)S(1)} %get-tuple-element.18.q_ref, f32[1024,256]{1,0:T(8,128)S(1)} %get-tuple-element.20.acc_in, bf16[256,256]{1,0:T(8,128)(2,1)S(1)} %collective-permute-done.2.rest_0_.rest_5_), custom_call_target="tpu_custom_call", output_to_operand_aliasing={{}: (1, {})} | custom-call | flops 134217728 | tf_op jit(solution)/shard_map/fold0/pallas_call | solution.py:220
  14.2 0.0 collective-permute-done.3.rest_0_.rest_6_
  14.2 1.7 %collective-permute-start.7 = (bf16[256,256]{1,0:T(8,128)(2,1)S(1)}, bf16[256,256]{1,0:T(8,128)(2,1)S(1)}, u32[]{:S(2)}, u32[]{:S(2)}) collective-permute-start(bf16[256,256]{1,0:T(8,128)(2,1)S(1)} %collective-permute-done.3.rest_0_.rest_6_), channel_id=1, source_target_pairs={{0,1},{1,0},{2,3},{3,2},{4,5},{5,4},{6,7},{7,6},{8,9},{9,8},{10,11... | collective-permute-start | bytes 393224 | tf_op jit(solution)/shard_map/ppermute | solution.py:295
  16.0 0.1 collective-permute-start.6
  16.0 0.6 %fold1.1.acc_in = f32[1024,256]{1,0:T(8,128)S(1)} custom-call(bf16[1024,256]{1,0:T(8,128)(2,1)S(1)} %get-tuple-element.18.q_ref, f32[1024,256]{1,0:T(8,128)S(1)} %fold0.1.acc_in, bf16[256,256]{1,0:T(8,128)(2,1)S(1)} %collective-permute-done.3.rest_0_.rest_6_), custom_call_target="tpu_custom_call", output_to_operand_aliasing={{}: (1, {})} | custom-call | flops 134217728 | tf_op jit(solution)/shard_map/fold1/pallas_call | solution.py:220
  16.7 0.0 copy-start.3
  16.7 0.0 collective-permute-done.4.rest_1_.rest_7_
  16.7 1.0 %collective-permute-start.8 = (bf16[256,256]{1,0:T(8,128)(2,1)S(1)}, bf16[256,256]{1,0:T(8,128)(2,1)S(1)}, u32[]{:S(2)}, u32[]{:S(2)}) collective-permute-start(bf16[256,256]{1,0:T(8,128)(2,1)S(1)} %collective-permute-done.4.rest_1_.rest_7_), channel_id=1, source_target_pairs={{0,1},{1,0},{2,3},{3,2},{4,5},{5,4},{6,7},{7,6},{8,9},{9,8},{10,11... | collective-permute-start | bytes 393224 | tf_op jit(solution)/shard_map/ppermute | solution.py:295
  17.7 0.0 collective-permute-done.5.rest_0_.rest_4_
  17.7 0.0 collective-permute-done.7.rest_3_.rest_2_
  17.7 0.0 collective-permute-done.6.rest_2_.rest_1_
  17.7 1.5 %fold2.1.acc_in = f32[1024,256]{1,0:T(8,128)S(1)} custom-call(bf16[1024,256]{1,0:T(8,128)(2,1)S(1)} %get-tuple-element.18.q_ref, f32[1024,256]{1,0:T(8,128)S(1)} %fold1.1.acc_in, bf16[256,256]{1,0:T(8,128)(2,1)S(1)} %collective-permute-done.5.rest_0_.rest_4_, ...), custom_call_target="tpu_custom_call", output_to_operand_aliasing={{}: (1, {})} | custom-call | flops 536870912 | tf_op jit(solution)/shard_map/fold2/pallas_call | solution.py:220
  19.2 0.0 collective-permute-done.8.rest_0_
  19.2 0.0 copy-done.3
  19.2 1.8 %last.1 = bf16[256,1536]{1,0:T(8,128)(2,1)} custom-call(bf16[1024,256]{1,0:T(8,128)(2,1)S(1)} %get-tuple-element.18.q_ref, f32[1024,256]{1,0:T(8,128)S(1)} %fold2.1.acc_in, bf16[256,1536]{1,0:T(8,128)(2,1)S(1)} %get-tuple-element.26.hidden_ref, bf16[512,1536]{1,0:T(8,128)(2,1)S(1)} %copy-done.3, bf16[256,256]{1,0:T(8,128)(2,1)S(1)} %collective-permute-done.8.rest_0_, ...), custom_call_target="tpu_custom_call" | custom-call | flops 536870912 | tf_op jit(solution)/shard_map/last/pallas_call | solution.py:220
Async XLA Ops:
  0.0 3.8 %copy-start.1 = (bf16[256,1536]{1,0:T(8,128)(2,1)S(1)}, bf16[256,1536]{1,0:T(8,128)(2,1)}, u32[]{:S(2)}) copy-start(bf16[256,1536]{1,0:T(8,128)(2,1)} %x_ref.3) | copy-start | bytes 2359300
  0.0 3.8 %copy-start.6 = (f32[1536]{0:T(1024)S(1)}, f32[1536]{0:T(1024)}, u32[]{:S(2)}) copy-start(f32[1536]{0:T(1024)} %gain_ref.5) | copy-start | bytes 18436
  0.0 4.1 %copy-start = (bf16[3,1536,768]{2,1,0:T(8,128)(2,1)S(1)}, bf16[3,1536,768]{2,1,0:T(8,128)(2,1)}, u32[]{:S(2)}) copy-start(bf16[3,1536,768]{2,1,0:T(8,128)(2,1)} %w_ref.3) | copy-start | bytes 21233668
  1.0 3.1 %collective-permute-start = (bf16[8,1536]{1,0:T(8,128)(2,1)S(1)}, bf16[8,1536]{1,0:T(8,128)(2,1)S(1)}, u32[]{:S(2)}, u32[]{:S(2)}) collective-permute-start(bf16[8,1536]{1,0:T(8,128)(2,1)S(1)} %edges.1), channel_id=1, source_target_pairs={{0,1},{1,0},{2,3},{3,2},{4,5},{5,4},{6,7},{7,6},{8,9},{9,8},{10,11... | collective-permute-start | bytes 73736 | tf_op jit(solution)/shard_map/ppermute | solution.py:254
  1.1 5.1 %collective-permute-start.1 = (bf16[8,1536]{1,0:T(8,128)(2,1)S(1)}, bf16[8,1536]{1,0:T(8,128)(2,1)S(1)}, u32[]{:S(2)}, u32[]{:S(2)}) collective-permute-start(bf16[8,1536]{1,0:T(8,128)(2,1)S(1)} %edges.1), channel_id=1, source_target_pairs={{0,7},{1,2},{2,1},{3,4},{4,3},{5,6},{6,5},{7,0},{8,15},{9,10},{10,... | collective-permute-start | bytes 73736 | tf_op jit(solution)/shard_map/ppermute | solution.py:256
  4.1 2.2 %copy-start.4 = (bf16[1536,128]{1,0:T(8,128)(2,1)S(1)}, bf16[1536,128]{1,0:T(8,128)(2,1)}, u32[]{:S(2)}) copy-start(bf16[1536,128]{1,0:T(8,128)(2,1)} %wk_ref.1) | copy-start | bytes 1179652
  4.1 2.2 %copy-start.5 = (bf16[1536,128]{1,0:T(8,128)(2,1)S(1)}, bf16[1536,128]{1,0:T(8,128)(2,1)}, u32[]{:S(2)}) copy-start(bf16[1536,128]{1,0:T(8,128)(2,1)} %wv_ref.1) | copy-start | bytes 1179652
  4.1 2.2 %copy-start.7 = (f32[1536]{0:T(1024)S(1)}, f32[1536]{0:T(1024)}, u32[]{:S(2)}) copy-start(f32[1536]{0:T(1024)} %again_ref.1) | copy-start | bytes 18436
  4.1 2.2 %copy-start.8 = (f32[768]{0:T(1024)S(1)}, f32[768]{0:T(1024)}, u32[]{:S(2)}) copy-start(f32[768]{0:T(1024)} %bias_ref.1) | copy-start | bytes 9220
  6.2 6.2 %copy-start.2 = (bf16[1536,512]{1,0:T(8,128)(2,1)S(1)}, bf16[1536,512]{1,0:T(8,128)(2,1)}, u32[]{:S(2)}) copy-start(bf16[1536,512]{1,0:T(8,128)(2,1)} %wq_ref.1) | copy-start | bytes 4718596
  7.5 6.1 %collective-permute-start.2 = (bf16[256,256]{1,0:T(8,128)(2,1)S(1)}, bf16[256,256]{1,0:T(8,128)(2,1)S(1)}, u32[]{:S(2)}, u32[]{:S(2)}) collective-permute-start(bf16[256,256]{1,0:T(8,128)(2,1)S(1)} %get-tuple-element.17.kv_ref.rest_3_), channel_id=1, source_target_pairs={{0,2},{1,5},{2,0},{3,7},{4,6},{5,1},{6,4},{7,3},{8,10},{9,13},{10,... | collective-permute-start | bytes 393224 | tf_op jit(solution)/shard_map/ppermute | solution.py:279
  8.9 5.4 %collective-permute-start.3 = (bf16[256,256]{1,0:T(8,128)(2,1)S(1)}, bf16[256,256]{1,0:T(8,128)(2,1)S(1)}, u32[]{:S(2)}, u32[]{:S(2)}) collective-permute-start(bf16[256,256]{1,0:T(8,128)(2,1)S(1)} %get-tuple-element.17.kv_ref.rest_3_), channel_id=1, source_target_pairs={{0,4},{1,3},{2,6},{3,1},{4,0},{5,7},{6,2},{7,5},{8,12},{9,11},{10,... | collective-permute-start | bytes 393224 | tf_op jit(solution)/shard_map/ppermute | solution.py:279
  10.5 6.2 %collective-permute-start.4 = (bf16[256,256]{1,0:T(8,128)(2,1)S(1)}, bf16[256,256]{1,0:T(8,128)(2,1)S(1)}, u32[]{:S(2)}, u32[]{:S(2)}) collective-permute-start(bf16[256,256]{1,0:T(8,128)(2,1)S(1)} %get-tuple-element.17.kv_ref.rest_3_), channel_id=1, source_target_pairs={{0,6},{1,7},{2,4},{3,5},{4,2},{5,3},{6,0},{7,1},{8,14},{9,15},{10,... | collective-permute-start | bytes 393224 | tf_op jit(solution)/shard_map/ppermute | solution.py:279
  10.5 7.2 %collective-permute-start.5 = (bf16[256,256]{1,0:T(8,128)(2,1)S(1)}, bf16[256,256]{1,0:T(8,128)(2,1)S(1)}, u32[]{:S(2)}, u32[]{:S(2)}) collective-permute-start(bf16[256,256]{1,0:T(8,128)(2,1)S(1)} %get-tuple-element.17.kv_ref.rest_3_), channel_id=1, source_target_pairs={{0,1},{1,0},{2,3},{3,2},{4,5},{5,4},{6,7},{7,6},{8,9},{9,8},{10,11... | collective-permute-start | bytes 393224 | tf_op jit(solution)/shard_map/ppermute | solution.py:281
  14.2 3.5 %collective-permute-start.7 = (bf16[256,256]{1,0:T(8,128)(2,1)S(1)}, bf16[256,256]{1,0:T(8,128)(2,1)S(1)}, u32[]{:S(2)}, u32[]{:S(2)}) collective-permute-start(bf16[256,256]{1,0:T(8,128)(2,1)S(1)} %collective-permute-done.3.rest_0_.rest_6_), channel_id=1, source_target_pairs={{0,1},{1,0},{2,3},{3,2},{4,5},{5,4},{6,7},{7,6},{8,9},{9,8},{10,11... | collective-permute-start | bytes 393224 | tf_op jit(solution)/shard_map/ppermute | solution.py:295
  16.0 1.7 %collective-permute-start.6 = (bf16[256,256]{1,0:T(8,128)(2,1)S(1)}, bf16[256,256]{1,0:T(8,128)(2,1)S(1)}, u32[]{:S(2)}, u32[]{:S(2)}) collective-permute-start(bf16[256,256]{1,0:T(8,128)(2,1)S(1)} %collective-permute-done.2.rest_0_.rest_5_), channel_id=1, source_target_pairs={{0,1},{1,0},{2,3},{3,2},{4,5},{5,4},{6,7},{7,6},{8,9},{9,8},{10,11... | collective-permute-start | bytes 393224 | tf_op jit(solution)/shard_map/ppermute | solution.py:295
  16.7 2.5 %copy-start.3 = (bf16[512,1536]{1,0:T(8,128)(2,1)S(1)}, bf16[512,1536]{1,0:T(8,128)(2,1)}, u32[]{:S(2)}) copy-start(bf16[512,1536]{1,0:T(8,128)(2,1)} %wo_ref.1) | copy-start | bytes 4718596
  16.7 2.5 %collective-permute-start.8 = (bf16[256,256]{1,0:T(8,128)(2,1)S(1)}, bf16[256,256]{1,0:T(8,128)(2,1)S(1)}, u32[]{:S(2)}, u32[]{:S(2)}) collective-permute-start(bf16[256,256]{1,0:T(8,128)(2,1)S(1)} %collective-permute-done.4.rest_1_.rest_7_), channel_id=1, source_target_pairs={{0,1},{1,0},{2,3},{3,2},{4,5},{5,4},{6,7},{7,6},{8,9},{9,8},{10,11... | collective-permute-start | bytes 393224 | tf_op jit(solution)/shard_map/ppermute | solution.py:295

commit v6 on v5

--- a/solution.py
+++ b/solution.py
@@ -30,19 +30,21 @@
     return jnp.dot(a, b, preferred_element_type=F32)
 
 
-def edge_kernel(reach, x_hbm, edges_ref, near_ref, sems):
+def edge_kernel(reach, x_hbm, near_ref, far_ref, ends_ref, sems):
     rows = x_hbm.shape[0]
-    tile = near_ref.shape[1]
+    tile = ends_ref.shape[1]
     copies = [
-        pltpu.make_async_copy(x_hbm.at[0:tile, :], near_ref.at[0], sems.at[0]),
-        pltpu.make_async_copy(x_hbm.at[rows - tile : rows, :], near_ref.at[1], sems.at[1]),
+        pltpu.make_async_copy(x_hbm.at[0:tile, :], ends_ref.at[0], sems.at[0]),
+        pltpu.make_async_copy(x_hbm.at[rows - tile : rows, :], ends_ref.at[1], sems.at[1]),
     ]
     for copy in copies:
         copy.start()
     for copy in copies:
         copy.wait()
-    edges_ref[0:reach, :] = near_ref[0, 0:reach, :]
-    edges_ref[reach:, :] = near_ref[1, tile - reach :, :]
+    first, last = ends_ref[0, 0:reach, :], ends_ref[1, tile - reach :, :]
+    even = lax.rem(lax.axis_index("seq"), 2) == 0
+    near_ref[...] = jnp.where(even, last, first)
+    far_ref[...] = jnp.where(even, first, last)
 
 
 def norm_kernel(x_ref, gain_ref, normed_ref):
@@ -55,10 +57,9 @@
     total = dot(normed_ref[...], w_ref[(taps - 1) // 2])
     even = lax.rem(lax.axis_index("seq"), 2) == 0
     near = normed_rows(near_ref[...], gain_ref[...])
-    row = lax.broadcasted_iota(jnp.int32, (2 * reach, 1), 0)
-    left = jnp.where((row >= reach) & jnp.logical_not(even), near, 0.0)
-    right = jnp.where((row < reach) & even, near, 0.0)
-    line = jnp.concatenate([normed_ref[...], jnp.concatenate([left, right], axis=0).astype(BF16)], axis=0)
+    spare = jnp.zeros((16 * pl.cdiv(reach, 16) - reach, chan), F32)
+    line = jnp.concatenate([normed_ref[...], jnp.concatenate([near, spare], axis=0).astype(BF16)], axis=0)
+    blank = jnp.zeros((reach, out_chan), F32)
     slots = iter(shift_refs)
     for tap in range(taps):
         shift = (tap - (taps - 1) // 2) * DILATION_STEP
@@ -66,13 +67,14 @@
             continue
         shift_ref = next(slots)
         product = dot(line, w_ref[tap])
+        beside = product[rows : rows + reach]
         if shift < 0:
-            shift_ref[0 : 2 * reach, :] = product[rows : rows + 2 * reach]
+            shift_ref[0 : 2 * reach, :] = jnp.concatenate([blank, jnp.where(even, 0.0, beside)], axis=0)
             shift_ref[2 * reach :, :] = product[0:rows]
             total = total + shift_ref[2 * reach + shift : 2 * reach + shift + rows, :]
         else:
             shift_ref[0:rows, :] = product[0:rows]
-            shift_ref[rows:, :] = product[rows + 2 * reach : rows + 4 * reach]
+            shift_ref[rows:, :] = jnp.concatenate([jnp.where(even, beside, 0.0), blank], axis=0)
             total = total + shift_ref[shift : shift + rows, :]
     part_ref[...] = total
 
@@ -87,15 +89,15 @@
     even = lax.rem(index, 2) == 0
     outside = (index == 0) | (index == count - 1)
     far = jnp.where(outside, 0.0, normed_rows(far_ref[...], gain_ref[...]))
-    far = jnp.concatenate([far, jnp.zeros_like(far)], axis=0).astype(BF16)
     edge = 16 * pl.cdiv(reach, 16)
+    far = jnp.concatenate([far, jnp.zeros((edge - reach, chan), F32)], axis=0).astype(BF16)
     top, bottom = part_ref[0:edge, :], part_ref[rows - edge :, :]
     middle = (taps - 1) // 2
     for away in range(1, middle + 1):
         shift = away * DILATION_STEP
         extra = dot(far, w_ref[jnp.where(even, middle - away, middle + away)])
         blank = jnp.zeros((edge - shift, out_chan), F32)
-        top = top + jnp.where(even, jnp.concatenate([extra[2 * reach - shift : 2 * reach], blank], axis=0), 0.0)
+        top = top + jnp.where(even, jnp.concatenate([extra[reach - shift : reach], blank], axis=0), 0.0)
         bottom = bottom + jnp.where(even, 0.0, jnp.concatenate([blank, extra[0:shift]], axis=0))
 
     def activate(span, total):
@@ -241,20 +243,19 @@
     count = lax.axis_size("seq")
     shape = jax.ShapeDtypeStruct
 
-    edges = call(
+    near, far = call(
         functools.partial(edge_kernel, reach),
-        shape((2 * reach, chan), BF16),
+        (shape((reach, chan), BF16),) * 2,
         (pltpu.with_memory_space_constraint(seq_in, pltpu.HBM),),
         specs=[pl.BlockSpec(memory_space=pltpu.HBM)],
-        scratch=[pltpu.VMEM((2, 16, chan), BF16), pltpu.SemaphoreType.DMA((2,))],
+        scratch=[pltpu.VMEM((2, 16 * pl.cdiv(reach, 16), chan), BF16), pltpu.SemaphoreType.DMA((2,))],
         flops=LOADF,
         moved=rows * chan * 4,
         name="edges",
     )
-    near = lax.ppermute(edges, "seq", [(i, i ^ 1) for i in range(count)])
     far_pairs = [(i, (i - 1 if i % 2 == 0 else i + 1) % count) for i in range(count)]
-    far = lax.ppermute(edges, "seq", far_pairs)
-
+    far = lax.ppermute(far, "seq", far_pairs)
+    near = lax.ppermute(near, "seq", [(i, i ^ 1) for i in range(count)])
     normed = call(norm_kernel, shape((rows, chan), BF16), (seq_in, conv_gain), flops=4 * rows * chan, name="norm")
     part = call(
         functools.partial(center_kernel, reach),

time: 21.1 us -> 21 us (level)
  no operation moved by 1% of the time
where the time goes in v6:
time: 21 us; the launch traced here: 20.8 us
  starting transfers between devices  10.4 us (50%)
  Pallas kernels  10.2 us (49%)
  between operations  0.21 us (1%)
    pallas_call x9, Pallas kernels, call(): pl.pallas_call(body, out_shape=outs, in_specs=specs or [VMEM] * len(args)...  10.2 us
    ppermute x3, starting transfers between devices, shards(): lax.ppermute(kv, 'seq', [(i, i ^ (step, other)[i % 2]) for i in range(cou...  2.83 us
    ppermute x3, starting transfers between devices, shards(): passed.append(lax.ppermute(block, 'seq', sibling))  2.64 us
    ppermute x1, starting transfers between devices, shards(): far = lax.ppermute(far, 'seq', far_pairs)  2.63 us
    ppermute x1, starting transfers between devices, shards(): mate = lax.ppermute(kv, 'seq', sibling)  2.14 us
  transfers between devices with their start and end apart: 9, of which 0 were waited for; matrix products, arithmetic and copies ran while one was open for 0% of the time, Pallas kernels for 30%

profile of v6, /device:TPU:1, one launch (start us, length us, event | category | flops | bytes accessed | tf_op | source)
XLA Modules:
  0.0 20.8 jit_solution(728579199285385749)
XLA Ops:
  0.0 0.0 copy-start.1
  0.0 0.0 copy-start.6
  0.0 0.0 copy-start
  0.0 1.0 %edges.1 = (bf16[4,1536]{1,0:T(4,128)(2,1)S(1)}, bf16[4,1536]{1,0:T(4,128)(2,1)S(1)}) custom-call(bf16[256,1536]{1,0:T(8,128)(2,1)} %x_ref.3), custom_call_target="tpu_custom_call" | custom-call | flops 8000000000 | bytes 1572864 | tf_op jit(solution)/shard_map/edges/pallas_call | solution.py:222
  1.0 0.1 collective-permute-start
  1.1 2.6 %collective-permute-start.1 = (bf16[4,1536]{1,0:T(4,128)(2,1)S(1)}, bf16[4,1536]{1,0:T(4,128)(2,1)S(1)}, u32[]{:S(2)}, u32[]{:S(2)}) collective-permute-start(bf16[4,1536]{1,0:T(4,128)(2,1)S(1)} %get-tuple-element.19), channel_id=1, source_target_pairs={{0,7},{1,2},{2,1},{3,4},{4,3},{5,6},{6,5},{7,0},{8,15},{9,10},{10,... | collective-permute-start | bytes 36872 | tf_op jit(solution)/shard_map/ppermute | solution.py:257
  3.8 0.0 copy-done.1
  3.8 0.0 copy-done.6
  3.8 0.3 %norm.1.normed_ref = bf16[256,1536]{1,0:T(8,128)(2,1)S(1)} custom-call(bf16[256,1536]{1,0:T(8,128)(2,1)S(1)} %copy-done.1, f32[1536]{0:T(1024)S(1)} %copy-done.6), custom_call_target="tpu_custom_call" | custom-call | flops 1572864 | tf_op jit(solution)/shard_map/norm/pallas_call | solution.py:222
  4.1 0.0 copy-start.4
  4.1 0.0 copy-start.5
  4.1 0.0 copy-start.7
  4.1 0.0 copy-start.8
  4.1 0.0 collective-permute-done.near_ref
  4.1 0.0 copy-done
  4.1 2.1 %center.1.part_ref = f32[256,768]{1,0:T(8,128)S(1)} custom-call(bf16[256,1536]{1,0:T(8,128)(2,1)S(1)} %norm.1.normed_ref, bf16[4,1536]{1,0:T(4,128)(2,1)S(1)} %collective-permute-done.near_ref, f32[1536]{0:T(1024)S(1)} %copy-done.6, bf16[3,1536,768]{2,1,0:T(8,128)(2,1)S(1)} %copy-done), custom_call_target="tpu_custom_call" | custom-call | flops 1811939328 | bytes 3932160 | tf_op jit(solution)/shard_map/center/pallas_call | solution.py:222
  6.3 0.0 copy-start.2
  6.3 0.0 collective-permute-done.1.far_ref
  6.3 0.0 copy-done.4
  6.3 0.0 copy-done.5
  6.3 0.0 copy-done.7
  6.3 0.0 copy-done.8
  6.3 1.2 %project.1 = (bf16[256,1536]{1,0:T(8,128)(2,1)S(1)}, bf16[256,1536]{1,0:T(8,128)(2,1)S(1)}, bf16[256,256]{1,0:T(8,128)(2,1)S(1)}) custom-call(bf16[256,1536]{1,0:T(8,128)(2,1)S(1)} %copy-done.1, f32[256,768]{1,0:T(8,128)S(1)} %center.1.part_ref, bf16[4,1536]{1,0:T(4,128)(2,1)S(1)} %collective-permute-done.1.far_ref, f32[1536]{0:T(1024)S(1)} %copy-done.6, ...), custom_call_target="tpu_custom_call" | custom-call | flops 201326592 | tf_op jit(solution)/shard_map/project/pallas_call | solution.py:222
  7.5 1.3 %collective-permute-start.2 = (bf16[256,256]{1,0:T(8,128)(2,1)S(1)}, bf16[256,256]{1,0:T(8,128)(2,1)S(1)}, u32[]{:S(2)}, u32[]{:S(2)}) collective-permute-start(bf16[256,256]{1,0:T(8,128)(2,1)S(1)} %get-tuple-element.21.kv_ref.rest_3_), channel_id=1, source_target_pairs={{0,2},{1,5},{2,0},{3,7},{4,6},{5,1},{6,4},{7,3},{8,10},{9,13},{10,... | collective-permute-start | bytes 393224 | tf_op jit(solution)/shard_map/ppermute | solution.py:280
  8.9 1.5 %collective-permute-start.3 = (bf16[256,256]{1,0:T(8,128)(2,1)S(1)}, bf16[256,256]{1,0:T(8,128)(2,1)S(1)}, u32[]{:S(2)}, u32[]{:S(2)}) collective-permute-start(bf16[256,256]{1,0:T(8,128)(2,1)S(1)} %get-tuple-element.21.kv_ref.rest_3_), channel_id=1, source_target_pairs={{0,4},{1,3},{2,6},{3,1},{4,0},{5,7},{6,2},{7,5},{8,12},{9,11},{10,... | collective-permute-start | bytes 393224 | tf_op jit(solution)/shard_map/ppermute | solution.py:280
  10.4 0.0 collective-permute-start.4
  10.4 2.1 %collective-permute-start.5 = (bf16[256,256]{1,0:T(8,128)(2,1)S(1)}, bf16[256,256]{1,0:T(8,128)(2,1)S(1)}, u32[]{:S(2)}, u32[]{:S(2)}) collective-permute-start(bf16[256,256]{1,0:T(8,128)(2,1)S(1)} %get-tuple-element.21.kv_ref.rest_3_), channel_id=1, source_target_pairs={{0,1},{1,0},{2,3},{3,2},{4,5},{5,4},{6,7},{7,6},{8,9},{9,8},{10,11... | collective-permute-start | bytes 393224 | tf_op jit(solution)/shard_map/ppermute | solution.py:282
  12.5 0.0 copy-done.2
  12.5 1.1 %query.1 = (bf16[1024,256]{1,0:T(8,128)(2,1)S(1)}, f32[1024,256]{1,0:T(8,128)S(1)}) custom-call(bf16[256,1536]{1,0:T(8,128)(2,1)S(1)} %get-tuple-element.20.attn_ref, bf16[1536,512]{1,0:T(8,128)(2,1)S(1)} %copy-done.2, bf16[256,256]{1,0:T(8,128)(2,1)S(1)} %get-tuple-element.21.kv_ref.rest_3_), custom_call_target="tpu_custom_call" | custom-call | flops 536870912 | tf_op jit(solution)/shard_map/query/pallas_call | solution.py:222
  13.6 0.0 collective-permute-done.2.rest_0_.rest_5_
  13.6 0.6 %fold0.1.acc_in = f32[1024,256]{1,0:T(8,128)S(1)} custom-call(bf16[1024,256]{1,0:T(8,128)(2,1)S(1)} %get-tuple-element.22.q_ref, f32[1024,256]{1,0:T(8,128)S(1)} %get-tuple-element.24.acc_in, bf16[256,256]{1,0:T(8,128)(2,1)S(1)} %collective-permute-done.2.rest_0_.rest_5_), custom_call_target="tpu_custom_call", output_to_operand_aliasing={{}: (1, {})} | custom-call | flops 134217728 | tf_op jit(solution)/shard_map/fold0/pallas_call | solution.py:222
  14.3 0.0 collective-permute-done.3.rest_0_.rest_6_
  14.3 1.8 %collective-permute-start.7 = (bf16[256,256]{1,0:T(8,128)(2,1)S(1)}, bf16[256,256]{1,0:T(8,128)(2,1)S(1)}, u32[]{:S(2)}, u32[]{:S(2)}) collective-permute-start(bf16[256,256]{1,0:T(8,128)(2,1)S(1)} %collective-permute-done.3.rest_0_.rest_6_), channel_id=1, source_target_pairs={{0,1},{1,0},{2,3},{3,2},{4,5},{5,4},{6,7},{7,6},{8,9},{9,8},{10,11... | collective-permute-start | bytes 393224 | tf_op jit(solution)/shard_map/ppermute | solution.py:296
  16.0 0.1 collective-permute-start.6
  16.1 0.6 %fold1.1.acc_in = f32[1024,256]{1,0:T(8,128)S(1)} custom-call(bf16[1024,256]{1,0:T(8,128)(2,1)S(1)} %get-tuple-element.22.q_ref, f32[1024,256]{1,0:T(8,128)S(1)} %fold0.1.acc_in, bf16[256,256]{1,0:T(8,128)(2,1)S(1)} %collective-permute-done.3.rest_0_.rest_6_), custom_call_target="tpu_custom_call", output_to_operand_aliasing={{}: (1, {})} | custom-call | flops 134217728 | tf_op jit(solution)/shard_map/fold1/pallas_call | solution.py:222
  16.7 0.0 copy-start.3
  16.8 0.0 collective-permute-done.4.rest_1_.rest_7_
  16.8 0.8 %collective-permute-start.8 = (bf16[256,256]{1,0:T(8,128)(2,1)S(1)}, bf16[256,256]{1,0:T(8,128)(2,1)S(1)}, u32[]{:S(2)}, u32[]{:S(2)}) collective-permute-start(bf16[256,256]{1,0:T(8,128)(2,1)S(1)} %collective-permute-done.4.rest_1_.rest_7_), channel_id=1, source_target_pairs={{0,1},{1,0},{2,3},{3,2},{4,5},{5,4},{6,7},{7,6},{8,9},{9,8},{10,11... | collective-permute-start | bytes 393224 | tf_op jit(solution)/shard_map/ppermute | solution.py:296
  17.6 0.0 collective-permute-done.5.rest_0_.rest_4_
  17.6 0.0 collective-permute-done.7.rest_3_.rest_2_
  17.6 0.0 collective-permute-done.6.rest_2_.rest_1_
  17.6 1.5 %fold2.1.acc_in = f32[1024,256]{1,0:T(8,128)S(1)} custom-call(bf16[1024,256]{1,0:T(8,128)(2,1)S(1)} %get-tuple-element.22.q_ref, f32[1024,256]{1,0:T(8,128)S(1)} %fold1.1.acc_in, bf16[256,256]{1,0:T(8,128)(2,1)S(1)} %collective-permute-done.5.rest_0_.rest_4_, ...), custom_call_target="tpu_custom_call", output_to_operand_aliasing={{}: (1, {})} | custom-call | flops 536870912 | tf_op jit(solution)/shard_map/fold2/pallas_call | solution.py:222
  19.1 0.0 collective-permute-done.8.rest_0_
  19.1 0.0 copy-done.3
  19.1 1.7 %last.1 = bf16[256,1536]{1,0:T(8,128)(2,1)} custom-call(bf16[1024,256]{1,0:T(8,128)(2,1)S(1)} %get-tuple-element.22.q_ref, f32[1024,256]{1,0:T(8,128)S(1)} %fold2.1.acc_in, bf16[256,1536]{1,0:T(8,128)(2,1)S(1)} %get-tuple-element.30.hidden_ref, bf16[512,1536]{1,0:T(8,128)(2,1)S(1)} %copy-done.3, bf16[256,256]{1,0:T(8,128)(2,1)S(1)} %collective-permute-done.8.rest_0_, ...), custom_call_target="tpu_custom_call" | custom-call | flops 536870912 | tf_op jit(solution)/shard_map/last/pallas_call | solution.py:222
Async XLA Ops:
  0.0 3.8 %copy-start.1 = (bf16[256,1536]{1,0:T(8,128)(2,1)S(1)}, bf16[256,1536]{1,0:T(8,128)(2,1)}, u32[]{:S(2)}) copy-start(bf16[256,1536]{1,0:T(8,128)(2,1)} %x_ref.3) | copy-start | bytes 2359300
  0.0 3.8 %copy-start.6 = (f32[1536]{0:T(1024)S(1)}, f32[1536]{0:T(1024)}, u32[]{:S(2)}) copy-start(f32[1536]{0:T(1024)} %gain_ref.5) | copy-start | bytes 18436
  0.0 4.1 %copy-start = (bf16[3,1536,768]{2,1,0:T(8,128)(2,1)S(1)}, bf16[3,1536,768]{2,1,0:T(8,128)(2,1)}, u32[]{:S(2)}) copy-start(bf16[3,1536,768]{2,1,0:T(8,128)(2,1)} %w_ref.3) | copy-start | bytes 21233668
  1.0 3.1 %collective-permute-start = (bf16[4,1536]{1,0:T(4,128)(2,1)S(1)}, bf16[4,1536]{1,0:T(4,128)(2,1)S(1)}, u32[]{:S(2)}, u32[]{:S(2)}) collective-permute-start(bf16[4,1536]{1,0:T(4,128)(2,1)S(1)} %get-tuple-element.18), channel_id=1, source_target_pairs={{0,1},{1,0},{2,3},{3,2},{4,5},{5,4},{6,7},{7,6},{8,9},{9,8},{10,11... | collective-permute-start | bytes 36872 | tf_op jit(solution)/shard_map/ppermute | solution.py:258
  1.1 5.1 %collective-permute-start.1 = (bf16[4,1536]{1,0:T(4,128)(2,1)S(1)}, bf16[4,1536]{1,0:T(4,128)(2,1)S(1)}, u32[]{:S(2)}, u32[]{:S(2)}) collective-permute-start(bf16[4,1536]{1,0:T(4,128)(2,1)S(1)} %get-tuple-element.19), channel_id=1, source_target_pairs={{0,7},{1,2},{2,1},{3,4},{4,3},{5,6},{6,5},{7,0},{8,15},{9,10},{10,... | collective-permute-start | bytes 36872 | tf_op jit(solution)/shard_map/ppermute | solution.py:257
  4.1 2.2 %copy-start.4 = (bf16[1536,128]{1,0:T(8,128)(2,1)S(1)}, bf16[1536,128]{1,0:T(8,128)(2,1)}, u32[]{:S(2)}) copy-start(bf16[1536,128]{1,0:T(8,128)(2,1)} %wk_ref.1) | copy-start | bytes 1179652
  4.1 2.2 %copy-start.5 = (bf16[1536,128]{1,0:T(8,128)(2,1)S(1)}, bf16[1536,128]{1,0:T(8,128)(2,1)}, u32[]{:S(2)}) copy-start(bf16[1536,128]{1,0:T(8,128)(2,1)} %wv_ref.1) | copy-start | bytes 1179652
  4.1 2.2 %copy-start.7 = (f32[1536]{0:T(1024)S(1)}, f32[1536]{0:T(1024)}, u32[]{:S(2)}) copy-start(f32[1536]{0:T(1024)} %again_ref.1) | copy-start | bytes 18436
  4.1 2.2 %copy-start.8 = (f32[768]{0:T(1024)S(1)}, f32[768]{0:T(1024)}, u32[]{:S(2)}) copy-start(f32[768]{0:T(1024)} %bias_ref.1) | copy-start | bytes 9220
  6.3 6.2 %copy-start.2 = (bf16[1536,512]{1,0:T(8,128)(2,1)S(1)}, bf16[1536,512]{1,0:T(8,128)(2,1)}, u32[]{:S(2)}) copy-start(bf16[1536,512]{1,0:T(8,128)(2,1)} %wq_ref.1) | copy-start | bytes 4718596
  7.5 6.1 %collective-permute-start.2 = (bf16[256,256]{1,0:T(8,128)(2,1)S(1)}, bf16[256,256]{1,0:T(8,128)(2,1)S(1)}, u32[]{:S(2)}, u32[]{:S(2)}) collective-permute-start(bf16[256,256]{1,0:T(8,128)(2,1)S(1)} %get-tuple-element.21.kv_ref.rest_3_), channel_id=1, source_target_pairs={{0,2},{1,5},{2,0},{3,7},{4,6},{5,1},{6,4},{7,3},{8,10},{9,13},{10,... | collective-permute-start | bytes 393224 | tf_op jit(solution)/shard_map/ppermute | solution.py:280
  8.9 5.4 %collective-permute-start.3 = (bf16[256,256]{1,0:T(8,128)(2,1)S(1)}, bf16[256,256]{1,0:T(8,128)(2,1)S(1)}, u32[]{:S(2)}, u32[]{:S(2)}) collective-permute-start(bf16[256,256]{1,0:T(8,128)(2,1)S(1)} %get-tuple-element.21.kv_ref.rest_3_), channel_id=1, source_target_pairs={{0,4},{1,3},{2,6},{3,1},{4,0},{5,7},{6,2},{7,5},{8,12},{9,11},{10,... | collective-permute-start | bytes 393224 | tf_op jit(solution)/shard_map/ppermute | solution.py:280
  10.4 6.4 %collective-permute-start.4 = (bf16[256,256]{1,0:T(8,128)(2,1)S(1)}, bf16[256,256]{1,0:T(8,128)(2,1)S(1)}, u32[]{:S(2)}, u32[]{:S(2)}) collective-permute-start(bf16[256,256]{1,0:T(8,128)(2,1)S(1)} %get-tuple-element.21.kv_ref.rest_3_), channel_id=1, source_target_pairs={{0,6},{1,7},{2,4},{3,5},{4,2},{5,3},{6,0},{7,1},{8,14},{9,15},{10,... | collective-permute-start | bytes 393224 | tf_op jit(solution)/shard_map/ppermute | solution.py:280
  10.4 7.2 %collective-permute-start.5 = (bf16[256,256]{1,0:T(8,128)(2,1)S(1)}, bf16[256,256]{1,0:T(8,128)(2,1)S(1)}, u32[]{:S(2)}, u32[]{:S(2)}) collective-permute-start(bf16[256,256]{1,0:T(8,128)(2,1)S(1)} %get-tuple-element.21.kv_ref.rest_3_), channel_id=1, source_target_pairs={{0,1},{1,0},{2,3},{3,2},{4,5},{5,4},{6,7},{7,6},{8,9},{9,8},{10,11... | collective-permute-start | bytes 393224 | tf_op jit(solution)/shard_map/ppermute | solution.py:282
  14.3 3.3 %collective-permute-start.7 = (bf16[256,256]{1,0:T(8,128)(2,1)S(1)}, bf16[256,256]{1,0:T(8,128)(2,1)S(1)}, u32[]{:S(2)}, u32[]{:S(2)}) collective-permute-start(bf16[256,256]{1,0:T(8,128)(2,1)S(1)} %collective-permute-done.3.rest_0_.rest_6_), channel_id=1, source_target_pairs={{0,1},{1,0},{2,3},{3,2},{4,5},{5,4},{6,7},{7,6},{8,9},{9,8},{10,11... | collective-permute-start | bytes 393224 | tf_op jit(solution)/shard_map/ppermute | solution.py:296
  16.0 1.5 %collective-permute-start.6 = (bf16[256,256]{1,0:T(8,128)(2,1)S(1)}, bf16[256,256]{1,0:T(8,128)(2,1)S(1)}, u32[]{:S(2)}, u32[]{:S(2)}) collective-permute-start(bf16[256,256]{1,0:T(8,128)(2,1)S(1)} %collective-permute-done.2.rest_0_.rest_5_), channel_id=1, source_target_pairs={{0,1},{1,0},{2,3},{3,2},{4,5},{5,4},{6,7},{7,6},{8,9},{9,8},{10,11... | collective-permute-start | bytes 393224 | tf_op jit(solution)/shard_map/ppermute | solution.py:296
  16.7 2.3 %copy-start.3 = (bf16[512,1536]{1,0:T(8,128)(2,1)S(1)}, bf16[512,1536]{1,0:T(8,128)(2,1)}, u32[]{:S(2)}) copy-start(bf16[512,1536]{1,0:T(8,128)(2,1)} %wo_ref.1) | copy-start | bytes 4718596
  16.8 2.3 %collective-permute-start.8 = (bf16[256,256]{1,0:T(8,128)(2,1)S(1)}, bf16[256,256]{1,0:T(8,128)(2,1)S(1)}, u32[]{:S(2)}, u32[]{:S(2)}) collective-permute-start(bf16[256,256]{1,0:T(8,128)(2,1)S(1)} %collective-permute-done.4.rest_1_.rest_7_), channel_id=1, source_target_pairs={{0,1},{1,0},{2,3},{3,2},{4,5},{5,4},{6,7},{7,6},{8,9},{9,8},{10,11... | collective-permute-start | bytes 393224 | tf_op jit(solution)/shard_map/ppermute | solution.py:296

commit v7 on v6

--- a/solution.py
+++ b/solution.py
@@ -81,21 +81,23 @@
 
 def project_kernel(
     reach, x_ref, part_ref, far_ref, gain_ref, w_ref, bias_ref, again_ref, wk_ref, wv_ref,
-    hidden_ref, attn_ref, kv_ref,
+    hidden_ref, attn_ref, kv_ref, keys_ref,
 ):
     rows, chan = x_ref.shape
     taps, _, out_chan = w_ref.shape
     index, count = lax.axis_index("seq"), lax.axis_size("seq")
     even = lax.rem(index, 2) == 0
     outside = (index == 0) | (index == count - 1)
-    far = jnp.where(outside, 0.0, normed_rows(far_ref[...], gain_ref[...]))
+    far = far_ref[...].astype(F32)
+    factor = jnp.where(outside, 0.0, lax.rsqrt(jnp.mean(far * far, axis=-1, keepdims=True) + EPS))
+    far = far * gain_ref[...]
     edge = 16 * pl.cdiv(reach, 16)
     far = jnp.concatenate([far, jnp.zeros((edge - reach, chan), F32)], axis=0).astype(BF16)
     top, bottom = part_ref[0:edge, :], part_ref[rows - edge :, :]
     middle = (taps - 1) // 2
     for away in range(1, middle + 1):
         shift = away * DILATION_STEP
-        extra = dot(far, w_ref[jnp.where(even, middle - away, middle + away)])
+        extra = dot(far, w_ref[jnp.where(even, middle - away, middle + away)])[0:reach] * factor
         blank = jnp.zeros((edge - shift, out_chan), F32)
         top = top + jnp.where(even, jnp.concatenate([extra[reach - shift : reach], blank], axis=0), 0.0)
         bottom = bottom + jnp.where(even, 0.0, jnp.concatenate([blank, extra[0:shift]], axis=0))
@@ -108,25 +110,36 @@
         attn_ref[span, :] = normed_rows(hidden, again_ref[...]).astype(BF16)
 
     both = jnp.concatenate([wk_ref[...], wv_ref[...]], axis=1)
-    for span in (slice(edge, rows // 2), slice(rows // 2, rows - edge)):
+    head_dim = wk_ref.shape[1]
+
+    def keep(span, pair):
+        keys_ref[span, :] = pair[:, :head_dim]
+        square = span.start // head_dim
+        at = span.start - square * head_dim
+        kv_ref[head_dim + at : head_dim + at + pair.shape[0], square * head_dim : (square + 1) * head_dim] = pair[:, head_dim:]
+
+    cuts = [edge] + list(range(head_dim, rows, head_dim)) + [rows - edge]
+    for span in [slice(*pair) for pair in zip(cuts, cuts[1:])]:
         activate(span, part_ref[span, :])
-        kv_ref[span, :] = dot(attn_ref[span, :], both).astype(BF16)
+        keep(span, dot(attn_ref[span, :], both).astype(BF16))
     activate(slice(0, edge), top)
     activate(slice(rows - edge, rows), bottom)
     ends = jnp.concatenate([attn_ref[0:edge, :], attn_ref[rows - edge :, :]], axis=0)
     ends = dot(ends, both).astype(BF16)
-    kv_ref[0:edge, :] = ends[:edge]
-    kv_ref[rows - edge :, :] = ends[edge:]
+    keep(slice(0, edge), ends[:edge])
+    keep(slice(rows - edge, rows), ends[edge:])
+    kv_ref[0:head_dim, :] = keys_ref[...].T
 
 
 def key_side(kv, head_dim):
-    rows = kv.shape[0]
-    ones = (lax.broadcasted_iota(jnp.int32, (head_dim, rows), 0) == 0).astype(BF16)
-    return jnp.concatenate([kv[:, :head_dim].T, ones], axis=0)
+    ones = (lax.broadcasted_iota(jnp.int32, (head_dim, kv.shape[1]), 0) == 0).astype(BF16)
+    return jnp.concatenate([kv[0:head_dim, :], ones], axis=0)
 
 
 def value_side(kv, head_dim):
-    return jnp.concatenate([kv[:, head_dim:], jnp.ones((kv.shape[0], head_dim), BF16)], axis=1)
+    rows = kv.shape[1]
+    values = [kv[head_dim:, at : at + head_dim] for at in range(0, rows, head_dim)]
+    return jnp.concatenate([jnp.concatenate(values, axis=0), jnp.ones((rows, head_dim), BF16)], axis=1)
 
 
 def fold(q_ref, kv_refs, acc_in, acc_out):
@@ -148,7 +161,7 @@
     many, head_dim = q_ref.shape[0], q_ref.shape[1] // 2
     scale = LOG2E * head_dim**-0.5
     step = math.gcd(many, 256)
-    pairs = [(kv[:, :head_dim].T, value_side(kv, head_dim)) for kv in kv_refs]
+    pairs = [(kv[0:head_dim, :], value_side(kv, head_dim)) for kv in kv_refs]
     for at in range(0, many, step):
         span = slice(at, at + step)
         scores = [dot(q_ref[span, :head_dim], keys) * scale for keys, _ in pairs]
@@ -165,7 +178,7 @@
     head_dim = q_ref.shape[1] // 2
     scale = LOG2E * head_dim**-0.5
     q = dot(attn_ref[...], wq_ref[...])
-    keys, values = kv_ref[:, :head_dim].T, value_side(kv_ref, head_dim)
+    keys, values = kv_ref[0:head_dim, :], value_side(kv_ref, head_dim)
     for h in range(wq_ref.shape[1] // head_dim):
         span = slice(h * rows, (h + 1) * rows)
         q_head = q[:, h * head_dim : (h + 1) * head_dim].astype(BF16)
@@ -268,8 +281,9 @@
     )
     hidden, attn_in, kv = call(
         functools.partial(project_kernel, reach),
-        (shape((rows, chan), BF16), shape((rows, chan), BF16), shape((rows, 2 * head_dim), BF16)),
+        (shape((rows, chan), BF16), shape((rows, chan), BF16), shape((2 * head_dim, rows), BF16)),
         (seq_in, part, far, conv_gain, convolution_weight, conv_bias, attn_gain, w_key, w_value),
+        scratch=[pltpu.VMEM((rows, head_dim), BF16)],
         flops=2 * rows * chan * 2 * head_dim,
         name="project",
     )

time: 21 us -> 20.9 us (level)
  transfers between devices with their start and end apart: 9 -> 9, of which waited for: 0 -> 0; matrix products, arithmetic and copies ran while one was open for 0% -> 0% of each run, Pallas kernels for 30% -> 29%
where the time goes in v7:
time: 20.9 us; the launch traced here: 20.7 us
  starting transfers between devices  10.5 us (50%)
  Pallas kernels  9.99 us (48%)
  between operations  0.21 us (1%)
    pallas_call x9, Pallas kernels, call(): pl.pallas_call(body, out_shape=outs, in_specs=specs or [VMEM] * len(args)...  9.99 us
    ppermute x3, starting transfers between devices, shards(): lax.ppermute(kv, 'seq', [(i, i ^ (step, other)[i % 2]) for i in range(cou...  2.83 us
    ppermute x3, starting transfers between devices, shards(): passed.append(lax.ppermute(block, 'seq', sibling))  2.75 us
    ppermute x1, starting transfers between devices, shards(): far = lax.ppermute(far, 'seq', far_pairs)  2.63 us
    ppermute x1, starting transfers between devices, shards(): mate = lax.ppermute(kv, 'seq', sibling)  2.14 us
  transfers between devices with their start and end apart: 9, of which 0 were waited for; matrix products, arithmetic and copies ran while one was open for 0% of the time, Pallas kernels for 29%

profile of v7, /device:TPU:1, one launch (start us, length us, event | category | flops | bytes accessed | tf_op | source)
XLA Modules:
  0.0 20.7 jit_solution(9189876834118527579)
XLA Ops:
  0.0 0.0 copy-start.1
  0.0 0.0 copy-start.6
  0.0 0.0 copy-start
  0.0 1.0 %edges.1 = (bf16[4,1536]{1,0:T(4,128)(2,1)S(1)}, bf16[4,1536]{1,0:T(4,128)(2,1)S(1)}) custom-call(bf16[256,1536]{1,0:T(8,128)(2,1)} %x_ref.3), custom_call_target="tpu_custom_call" | custom-call | flops 8000000000 | bytes 1572864 | tf_op jit(solution)/shard_map/edges/pallas_call | solution.py:235
  1.0 0.1 collective-permute-start
  1.1 2.6 %collective-permute-start.1 = (bf16[4,1536]{1,0:T(4,128)(2,1)S(1)}, bf16[4,1536]{1,0:T(4,128)(2,1)S(1)}, u32[]{:S(2)}, u32[]{:S(2)}) collective-permute-start(bf16[4,1536]{1,0:T(4,128)(2,1)S(1)} %get-tuple-element.19), channel_id=1, source_target_pairs={{0,7},{1,2},{2,1},{3,4},{4,3},{5,6},{6,5},{7,0},{8,15},{9,10},{10,... | collective-permute-start | bytes 36872 | tf_op jit(solution)/shard_map/ppermute | solution.py:270
  3.8 0.0 copy-done.1
  3.8 0.0 copy-done.6
  3.8 0.3 %norm.1.normed_ref = bf16[256,1536]{1,0:T(8,128)(2,1)S(1)} custom-call(bf16[256,1536]{1,0:T(8,128)(2,1)S(1)} %copy-done.1, f32[1536]{0:T(1024)S(1)} %copy-done.6), custom_call_target="tpu_custom_call" | custom-call | flops 1572864 | tf_op jit(solution)/shard_map/norm/pallas_call | solution.py:235
  4.1 0.0 copy-start.4
  4.1 0.0 copy-start.5
  4.1 0.0 copy-start.7
  4.1 0.0 copy-start.8
  4.1 0.0 collective-permute-done.near_ref
  4.1 0.0 copy-done
  4.1 2.1 %center.1.part_ref = f32[256,768]{1,0:T(8,128)S(1)} custom-call(bf16[256,1536]{1,0:T(8,128)(2,1)S(1)} %norm.1.normed_ref, bf16[4,1536]{1,0:T(4,128)(2,1)S(1)} %collective-permute-done.near_ref, f32[1536]{0:T(1024)S(1)} %copy-done.6, bf16[3,1536,768]{2,1,0:T(8,128)(2,1)S(1)} %copy-done), custom_call_target="tpu_custom_call" | custom-call | flops 1811939328 | bytes 3932160 | tf_op jit(solution)/shard_map/center/pallas_call | solution.py:235
  6.3 0.0 copy-start.2
  6.3 0.0 collective-permute-done.1.far_ref
  6.3 0.0 copy-done.4
  6.3 0.0 copy-done.5
  6.3 0.0 copy-done.7
  6.3 0.0 copy-done.8
  6.3 1.2 %project.1 = (bf16[256,1536]{1,0:T(8,128)(2,1)S(1)}, bf16[256,1536]{1,0:T(8,128)(2,1)S(1)}, bf16[256,256]{1,0:T(8,128)(2,1)S(1)}) custom-call(bf16[256,1536]{1,0:T(8,128)(2,1)S(1)} %copy-done.1, f32[256,768]{1,0:T(8,128)S(1)} %center.1.part_ref, bf16[4,1536]{1,0:T(4,128)(2,1)S(1)} %collective-permute-done.1.far_ref, f32[1536]{0:T(1024)S(1)} %copy-done.6, ...), custom_call_target="tpu_custom_call" | custom-call | flops 201326592 | tf_op jit(solution)/shard_map/project/pallas_call | solution.py:235
  7.6 1.3 %collective-permute-start.2 = (bf16[256,256]{1,0:T(8,128)(2,1)S(1)}, bf16[256,256]{1,0:T(8,128)(2,1)S(1)}, u32[]{:S(2)}, u32[]{:S(2)}) collective-permute-start(bf16[256,256]{1,0:T(8,128)(2,1)S(1)} %get-tuple-element.21.kv_ref.rest_3_), channel_id=1, source_target_pairs={{0,2},{1,5},{2,0},{3,7},{4,6},{5,1},{6,4},{7,3},{8,10},{9,13},{10,... | collective-permute-start | bytes 393224 | tf_op jit(solution)/shard_map/ppermute | solution.py:294
  8.9 1.5 %collective-permute-start.3 = (bf16[256,256]{1,0:T(8,128)(2,1)S(1)}, bf16[256,256]{1,0:T(8,128)(2,1)S(1)}, u32[]{:S(2)}, u32[]{:S(2)}) collective-permute-start(bf16[256,256]{1,0:T(8,128)(2,1)S(1)} %get-tuple-element.21.kv_ref.rest_3_), channel_id=1, source_target_pairs={{0,4},{1,3},{2,6},{3,1},{4,0},{5,7},{6,2},{7,5},{8,12},{9,11},{10,... | collective-permute-start | bytes 393224 | tf_op jit(solution)/shard_map/ppermute | solution.py:294
  10.4 0.0 collective-permute-start.4
  10.4 2.1 %collective-permute-start.5 = (bf16[256,256]{1,0:T(8,128)(2,1)S(1)}, bf16[256,256]{1,0:T(8,128)(2,1)S(1)}, u32[]{:S(2)}, u32[]{:S(2)}) collective-permute-start(bf16[256,256]{1,0:T(8,128)(2,1)S(1)} %get-tuple-element.21.kv_ref.rest_3_), channel_id=1, source_target_pairs={{0,1},{1,0},{2,3},{3,2},{4,5},{5,4},{6,7},{7,6},{8,9},{9,8},{10,11... | collective-permute-start | bytes 393224 | tf_op jit(solution)/shard_map/ppermute | solution.py:296
  12.5 0.0 copy-done.2
  12.5 1.1 %query.1 = (bf16[1024,256]{1,0:T(8,128)(2,1)S(1)}, f32[1024,256]{1,0:T(8,128)S(1)}) custom-call(bf16[256,1536]{1,0:T(8,128)(2,1)S(1)} %get-tuple-element.20.attn_ref, bf16[1536,512]{1,0:T(8,128)(2,1)S(1)} %copy-done.2, bf16[256,256]{1,0:T(8,128)(2,1)S(1)} %get-tuple-element.21.kv_ref.rest_3_), custom_call_target="tpu_custom_call" | custom-call | flops 536870912 | tf_op jit(solution)/shard_map/query/pallas_call | solution.py:235
  13.6 0.0 collective-permute-done.2.rest_0_.rest_5_
  13.6 0.6 %fold0.1.acc_in = f32[1024,256]{1,0:T(8,128)S(1)} custom-call(bf16[1024,256]{1,0:T(8,128)(2,1)S(1)} %get-tuple-element.22.q_ref, f32[1024,256]{1,0:T(8,128)S(1)} %get-tuple-element.24.acc_in, bf16[256,256]{1,0:T(8,128)(2,1)S(1)} %collective-permute-done.2.rest_0_.rest_5_), custom_call_target="tpu_custom_call", output_to_operand_aliasing={{}: (1, {})} | custom-call | flops 134217728 | tf_op jit(solution)/shard_map/fold0/pallas_call | solution.py:235
  14.2 0.0 collective-permute-done.3.rest_0_.rest_6_
  14.2 1.8 %collective-permute-start.7 = (bf16[256,256]{1,0:T(8,128)(2,1)S(1)}, bf16[256,256]{1,0:T(8,128)(2,1)S(1)}, u32[]{:S(2)}, u32[]{:S(2)}) collective-permute-start(bf16[256,256]{1,0:T(8,128)(2,1)S(1)} %collective-permute-done.3.rest_0_.rest_6_), channel_id=1, source_target_pairs={{0,1},{1,0},{2,3},{3,2},{4,5},{5,4},{6,7},{7,6},{8,9},{9,8},{10,11... | collective-permute-start | bytes 393224 | tf_op jit(solution)/shard_map/ppermute | solution.py:310
  16.0 0.1 collective-permute-start.6
  16.1 0.6 %fold1.1.acc_in = f32[1024,256]{1,0:T(8,128)S(1)} custom-call(bf16[1024,256]{1,0:T(8,128)(2,1)S(1)} %get-tuple-element.22.q_ref, f32[1024,256]{1,0:T(8,128)S(1)} %fold0.1.acc_in, bf16[256,256]{1,0:T(8,128)(2,1)S(1)} %collective-permute-done.3.rest_0_.rest_6_), custom_call_target="tpu_custom_call", output_to_operand_aliasing={{}: (1, {})} | custom-call | flops 134217728 | tf_op jit(solution)/shard_map/fold1/pallas_call | solution.py:235
  16.7 0.0 copy-start.3
  16.7 0.0 collective-permute-done.4.rest_1_.rest_7_
  16.7 0.9 %collective-permute-start.8 = (bf16[256,256]{1,0:T(8,128)(2,1)S(1)}, bf16[256,256]{1,0:T(8,128)(2,1)S(1)}, u32[]{:S(2)}, u32[]{:S(2)}) collective-permute-start(bf16[256,256]{1,0:T(8,128)(2,1)S(1)} %collective-permute-done.4.rest_1_.rest_7_), channel_id=1, source_target_pairs={{0,1},{1,0},{2,3},{3,2},{4,5},{5,4},{6,7},{7,6},{8,9},{9,8},{10,11... | collective-permute-start | bytes 393224 | tf_op jit(solution)/shard_map/ppermute | solution.py:310
  17.6 0.0 collective-permute-done.5.rest_0_.rest_4_
  17.6 0.0 collective-permute-done.7.rest_3_.rest_2_
  17.6 0.0 collective-permute-done.6.rest_2_.rest_1_
  17.6 1.4 %fold2.1.acc_in = f32[1024,256]{1,0:T(8,128)S(1)} custom-call(bf16[1024,256]{1,0:T(8,128)(2,1)S(1)} %get-tuple-element.22.q_ref, f32[1024,256]{1,0:T(8,128)S(1)} %fold1.1.acc_in, bf16[256,256]{1,0:T(8,128)(2,1)S(1)} %collective-permute-done.5.rest_0_.rest_4_, ...), custom_call_target="tpu_custom_call", output_to_operand_aliasing={{}: (1, {})} | custom-call | flops 536870912 | tf_op jit(solution)/shard_map/fold2/pallas_call | solution.py:235
  19.0 0.0 collective-permute-done.8.rest_0_
  19.0 0.0 copy-done.3
  19.0 1.7 %last.1 = bf16[256,1536]{1,0:T(8,128)(2,1)} custom-call(bf16[1024,256]{1,0:T(8,128)(2,1)S(1)} %get-tuple-element.22.q_ref, f32[1024,256]{1,0:T(8,128)S(1)} %fold2.1.acc_in, bf16[256,1536]{1,0:T(8,128)(2,1)S(1)} %get-tuple-element.30.hidden_ref, bf16[512,1536]{1,0:T(8,128)(2,1)S(1)} %copy-done.3, bf16[256,256]{1,0:T(8,128)(2,1)S(1)} %collective-permute-done.8.rest_0_, ...), custom_call_target="tpu_custom_call" | custom-call | flops 536870912 | tf_op jit(solution)/shard_map/last/pallas_call | solution.py:235
Async XLA Ops:
  0.0 3.8 %copy-start.1 = (bf16[256,1536]{1,0:T(8,128)(2,1)S(1)}, bf16[256,1536]{1,0:T(8,128)(2,1)}, u32[]{:S(2)}) copy-start(bf16[256,1536]{1,0:T(8,128)(2,1)} %x_ref.3) | copy-start | bytes 2359300
  0.0 3.8 %copy-start.6 = (f32[1536]{0:T(1024)S(1)}, f32[1536]{0:T(1024)}, u32[]{:S(2)}) copy-start(f32[1536]{0:T(1024)} %gain_ref.5) | copy-start | bytes 18436
  0.0 4.1 %copy-start = (bf16[3,1536,768]{2,1,0:T(8,128)(2,1)S(1)}, bf16[3,1536,768]{2,1,0:T(8,128)(2,1)}, u32[]{:S(2)}) copy-start(bf16[3,1536,768]{2,1,0:T(8,128)(2,1)} %w_ref.3) | copy-start | bytes 21233668
  1.0 3.1 %collective-permute-start = (bf16[4,1536]{1,0:T(4,128)(2,1)S(1)}, bf16[4,1536]{1,0:T(4,128)(2,1)S(1)}, u32[]{:S(2)}, u32[]{:S(2)}) collective-permute-start(bf16[4,1536]{1,0:T(4,128)(2,1)S(1)} %get-tuple-element.18), channel_id=1, source_target_pairs={{0,1},{1,0},{2,3},{3,2},{4,5},{5,4},{6,7},{7,6},{8,9},{9,8},{10,11... | collective-permute-start | bytes 36872 | tf_op jit(solution)/shard_map/ppermute | solution.py:271
  1.1 5.1 %collective-permute-start.1 = (bf16[4,1536]{1,0:T(4,128)(2,1)S(1)}, bf16[4,1536]{1,0:T(4,128)(2,1)S(1)}, u32[]{:S(2)}, u32[]{:S(2)}) collective-permute-start(bf16[4,1536]{1,0:T(4,128)(2,1)S(1)} %get-tuple-element.19), channel_id=1, source_target_pairs={{0,7},{1,2},{2,1},{3,4},{4,3},{5,6},{6,5},{7,0},{8,15},{9,10},{10,... | collective-permute-start | bytes 36872 | tf_op jit(solution)/shard_map/ppermute | solution.py:270
  4.1 2.2 %copy-start.4 = (bf16[1536,128]{1,0:T(8,128)(2,1)S(1)}, bf16[1536,128]{1,0:T(8,128)(2,1)}, u32[]{:S(2)}) copy-start(bf16[1536,128]{1,0:T(8,128)(2,1)} %wk_ref.1) | copy-start | bytes 1179652
  4.1 2.2 %copy-start.5 = (bf16[1536,128]{1,0:T(8,128)(2,1)S(1)}, bf16[1536,128]{1,0:T(8,128)(2,1)}, u32[]{:S(2)}) copy-start(bf16[1536,128]{1,0:T(8,128)(2,1)} %wv_ref.1) | copy-start | bytes 1179652
  4.1 2.2 %copy-start.7 = (f32[1536]{0:T(1024)S(1)}, f32[1536]{0:T(1024)}, u32[]{:S(2)}) copy-start(f32[1536]{0:T(1024)} %again_ref.1) | copy-start | bytes 18436
  4.1 2.2 %copy-start.8 = (f32[768]{0:T(1024)S(1)}, f32[768]{0:T(1024)}, u32[]{:S(2)}) copy-start(f32[768]{0:T(1024)} %bias_ref.1) | copy-start | bytes 9220
  6.3 6.3 %copy-start.2 = (bf16[1536,512]{1,0:T(8,128)(2,1)S(1)}, bf16[1536,512]{1,0:T(8,128)(2,1)}, u32[]{:S(2)}) copy-start(bf16[1536,512]{1,0:T(8,128)(2,1)} %wq_ref.1) | copy-start | bytes 4718596
  7.6 6.1 %collective-permute-start.2 = (bf16[256,256]{1,0:T(8,128)(2,1)S(1)}, bf16[256,256]{1,0:T(8,128)(2,1)S(1)}, u32[]{:S(2)}, u32[]{:S(2)}) collective-permute-start(bf16[256,256]{1,0:T(8,128)(2,1)S(1)} %get-tuple-element.21.kv_ref.rest_3_), channel_id=1, source_target_pairs={{0,2},{1,5},{2,0},{3,7},{4,6},{5,1},{6,4},{7,3},{8,10},{9,13},{10,... | collective-permute-start | bytes 393224 | tf_op jit(solution)/shard_map/ppermute | solution.py:294
  8.9 5.3 %collective-permute-start.3 = (bf16[256,256]{1,0:T(8,128)(2,1)S(1)}, bf16[256,256]{1,0:T(8,128)(2,1)S(1)}, u32[]{:S(2)}, u32[]{:S(2)}) collective-permute-start(bf16[256,256]{1,0:T(8,128)(2,1)S(1)} %get-tuple-element.21.kv_ref.rest_3_), channel_id=1, source_target_pairs={{0,4},{1,3},{2,6},{3,1},{4,0},{5,7},{6,2},{7,5},{8,12},{9,11},{10,... | collective-permute-start | bytes 393224 | tf_op jit(solution)/shard_map/ppermute | solution.py:294
  10.4 6.3 %collective-permute-start.4 = (bf16[256,256]{1,0:T(8,128)(2,1)S(1)}, bf16[256,256]{1,0:T(8,128)(2,1)S(1)}, u32[]{:S(2)}, u32[]{:S(2)}) collective-permute-start(bf16[256,256]{1,0:T(8,128)(2,1)S(1)} %get-tuple-element.21.kv_ref.rest_3_), channel_id=1, source_target_pairs={{0,6},{1,7},{2,4},{3,5},{4,2},{5,3},{6,0},{7,1},{8,14},{9,15},{10,... | collective-permute-start | bytes 393224 | tf_op jit(solution)/shard_map/ppermute | solution.py:294
  10.4 7.2 %collective-permute-start.5 = (bf16[256,256]{1,0:T(8,128)(2,1)S(1)}, bf16[256,256]{1,0:T(8,128)(2,1)S(1)}, u32[]{:S(2)}, u32[]{:S(2)}) collective-permute-start(bf16[256,256]{1,0:T(8,128)(2,1)S(1)} %get-tuple-element.21.kv_ref.rest_3_), channel_id=1, source_target_pairs={{0,1},{1,0},{2,3},{3,2},{4,5},{5,4},{6,7},{7,6},{8,9},{9,8},{10,11... | collective-permute-start | bytes 393224 | tf_op jit(solution)/shard_map/ppermute | solution.py:296
  14.2 3.4 %collective-permute-start.7 = (bf16[256,256]{1,0:T(8,128)(2,1)S(1)}, bf16[256,256]{1,0:T(8,128)(2,1)S(1)}, u32[]{:S(2)}, u32[]{:S(2)}) collective-permute-start(bf16[256,256]{1,0:T(8,128)(2,1)S(1)} %collective-permute-done.3.rest_0_.rest_6_), channel_id=1, source_target_pairs={{0,1},{1,0},{2,3},{3,2},{4,5},{5,4},{6,7},{7,6},{8,9},{9,8},{10,11... | collective-permute-start | bytes 393224 | tf_op jit(solution)/shard_map/ppermute | solution.py:310
  16.0 1.6 %collective-permute-start.6 = (bf16[256,256]{1,0:T(8,128)(2,1)S(1)}, bf16[256,256]{1,0:T(8,128)(2,1)S(1)}, u32[]{:S(2)}, u32[]{:S(2)}) collective-permute-start(bf16[256,256]{1,0:T(8,128)(2,1)S(1)} %collective-permute-done.2.rest_0_.rest_5_), channel_id=1, source_target_pairs={{0,1},{1,0},{2,3},{3,2},{4,5},{5,4},{6,7},{7,6},{8,9},{9,8},{10,11... | collective-permute-start | bytes 393224 | tf_op jit(solution)/shard_map/ppermute | solution.py:310
  16.7 2.4 %copy-start.3 = (bf16[512,1536]{1,0:T(8,128)(2,1)S(1)}, bf16[512,1536]{1,0:T(8,128)(2,1)}, u32[]{:S(2)}) copy-start(bf16[512,1536]{1,0:T(8,128)(2,1)} %wo_ref.1) | copy-start | bytes 4718596
  16.7 2.3 %collective-permute-start.8 = (bf16[256,256]{1,0:T(8,128)(2,1)S(1)}, bf16[256,256]{1,0:T(8,128)(2,1)S(1)}, u32[]{:S(2)}, u32[]{:S(2)}) collective-permute-start(bf16[256,256]{1,0:T(8,128)(2,1)S(1)} %collective-permute-done.4.rest_1_.rest_7_), channel_id=1, source_target_pairs={{0,1},{1,0},{2,3},{3,2},{4,5},{5,4},{6,7},{7,6},{8,9},{9,8},{10,11... | collective-permute-start | bytes 393224 | tf_op jit(solution)/shard_map/ppermute | solution.py:310

commit v8 on v7

--- a/solution.py
+++ b/solution.py
@@ -287,11 +287,24 @@
         flops=2 * rows * chan * 2 * head_dim,
         name="project",
     )
-    steps = list(range(2, count, 2))
+    chips = count // 2
+    ring = [place ^ (place >> 1) for place in range(chips)]
+    rounds = []
+    for turn in range(1, (chips + 1) // 2):
+        rounds += [(turn, chips - turn), (chips - turn, turn)]
+    if chips % 2 == 0:
+        rounds.append((chips // 2, chips // 2))
+    rounds = [(y, x) for x, y in rounds]
     blocks = []
-    for k, step in enumerate(steps):
-        other = steps[k ^ 1] if (k ^ 1) < len(steps) else step
-        blocks.append(lax.ppermute(kv, "seq", [(i, i ^ (step, other)[i % 2]) for i in range(count)]))
+    for turns in rounds:
+        moves = [(place, core) for place in range(chips) for core in range(2)]
+        blocks.append(
+            lax.ppermute(
+                kv,
+                "seq",
+                [(2 * ring[p] + core, 2 * ring[(p + turns[core]) % chips] + core) for p, core in moves],
+            )
+        )
     sibling = [(i, i ^ 1) for i in range(count)]
     mate = lax.ppermute(kv, "seq", sibling)
     fold_flops = 4 * rows * rows * heads * head_dim

time: 20.9 us -> 20.8 us (level)
    ppermute x3, starting transfers between devices: 2.83 us -> 4 us  [shards(): lax.ppermute(kv, 'seq', [(2 * ring[p] + core, 2 * ring[(p + turns[core])...]
    ppermute x1, starting transfers between devices: 2.14 us -> 1.23 us  [shards(): mate = lax.ppermute(kv, 'seq', sibling)]
    ppermute x3, starting transfers between devices: 2.75 us -> 2.3 us  [shards(): passed.append(lax.ppermute(block, 'seq', sibling))]
where the time goes in v8:
time: 20.8 us; the launch traced here: 20.6 us
  starting transfers between devices  10.3 us (50%)
  Pallas kernels  10 us (48%)
  between operations  0.21 us (1%)
    pallas_call x9, Pallas kernels, call(): pl.pallas_call(body, out_shape=outs, in_specs=specs or [VMEM] * len(args)...  10 us
    ppermute x3, starting transfers between devices, shards(): lax.ppermute(kv, 'seq', [(2 * ring[p] + core, 2 * ring[(p + turns[core])...  4 us
    ppermute x1, starting transfers between devices, shards(): far = lax.ppermute(far, 'seq', far_pairs)  2.63 us
    ppermute x3, starting transfers between devices, shards(): passed.append(lax.ppermute(block, 'seq', sibling))  2.3 us
    ppermute x1, starting transfers between devices, shards(): mate = lax.ppermute(kv, 'seq', sibling)  1.23 us
  transfers between devices with their start and end apart: 9, of which 0 were waited for; matrix products, arithmetic and copies ran while one was open for 0% of the time, Pallas kernels for 29%

profile of v8, /device:TPU:1, one launch (start us, length us, event | category | flops | bytes accessed | tf_op | source)
XLA Modules:
  0.0 20.6 jit_solution(260001407322237444)
XLA Ops:
  0.0 0.0 copy-start.1
  0.0 0.0 copy-start.6
  0.0 0.0 copy-start
  0.0 1.0 %edges.1 = (bf16[4,1536]{1,0:T(4,128)(2,1)S(1)}, bf16[4,1536]{1,0:T(4,128)(2,1)S(1)}) custom-call(bf16[256,1536]{1,0:T(8,128)(2,1)} %x_ref.3), custom_call_target="tpu_custom_call" | custom-call | flops 8000000000 | bytes 1572864 | tf_op jit(solution)/shard_map/edges/pallas_call | solution.py:235
  1.0 0.1 collective-permute-start
  1.1 2.6 %collective-permute-start.1 = (bf16[4,1536]{1,0:T(4,128)(2,1)S(1)}, bf16[4,1536]{1,0:T(4,128)(2,1)S(1)}, u32[]{:S(2)}, u32[]{:S(2)}) collective-permute-start(bf16[4,1536]{1,0:T(4,128)(2,1)S(1)} %get-tuple-element.19), channel_id=1, source_target_pairs={{0,7},{1,2},{2,1},{3,4},{4,3},{5,6},{6,5},{7,0},{8,15},{9,10},{10,... | collective-permute-start | bytes 36872 | tf_op jit(solution)/shard_map/ppermute | solution.py:270
  3.8 0.0 copy-done.1
  3.8 0.0 copy-done.6
  3.8 0.3 %norm.1.normed_ref = bf16[256,1536]{1,0:T(8,128)(2,1)S(1)} custom-call(bf16[256,1536]{1,0:T(8,128)(2,1)S(1)} %copy-done.1, f32[1536]{0:T(1024)S(1)} %copy-done.6), custom_call_target="tpu_custom_call" | custom-call | flops 1572864 | tf_op jit(solution)/shard_map/norm/pallas_call | solution.py:235
  4.1 0.0 copy-start.4
  4.1 0.0 copy-start.5
  4.1 0.0 copy-start.7
  4.1 0.0 copy-start.8
  4.1 0.0 collective-permute-done.near_ref
  4.1 0.0 copy-done
  4.1 2.1 %center.1.part_ref = f32[256,768]{1,0:T(8,128)S(1)} custom-call(bf16[256,1536]{1,0:T(8,128)(2,1)S(1)} %norm.1.normed_ref, bf16[4,1536]{1,0:T(4,128)(2,1)S(1)} %collective-permute-done.near_ref, f32[1536]{0:T(1024)S(1)} %copy-done.6, bf16[3,1536,768]{2,1,0:T(8,128)(2,1)S(1)} %copy-done), custom_call_target="tpu_custom_call" | custom-call | flops 1811939328 | bytes 3932160 | tf_op jit(solution)/shard_map/center/pallas_call | solution.py:235
  6.3 0.0 copy-start.2
  6.3 0.0 collective-permute-done.1.far_ref
  6.3 0.0 copy-done.4
  6.3 0.0 copy-done.5
  6.3 0.0 copy-done.7
  6.3 0.0 copy-done.8
  6.3 1.2 %project.1 = (bf16[256,1536]{1,0:T(8,128)(2,1)S(1)}, bf16[256,1536]{1,0:T(8,128)(2,1)S(1)}, bf16[256,256]{1,0:T(8,128)(2,1)S(1)}) custom-call(bf16[256,1536]{1,0:T(8,128)(2,1)S(1)} %copy-done.1, f32[256,768]{1,0:T(8,128)S(1)} %center.1.part_ref, bf16[4,1536]{1,0:T(4,128)(2,1)S(1)} %collective-permute-done.1.far_ref, f32[1536]{0:T(1024)S(1)} %copy-done.6, ...), custom_call_target="tpu_custom_call" | custom-call | flops 201326592 | tf_op jit(solution)/shard_map/project/pallas_call | solution.py:235
  7.6 1.6 %collective-permute-start.2 = (bf16[256,256]{1,0:T(8,128)(2,1)S(1)}, bf16[256,256]{1,0:T(8,128)(2,1)S(1)}, u32[]{:S(2)}, u32[]{:S(2)}) collective-permute-start(bf16[256,256]{1,0:T(8,128)(2,1)S(1)} %get-tuple-element.21.kv_ref.rest_3_), channel_id=1, source_target_pairs={{0,4},{1,3},{2,0},{3,7},{6,2},{7,5},{4,6},{5,1},{8,12},{9,11},{10,... | collective-permute-start | bytes 393224 | tf_op jit(solution)/shard_map/ppermute | solution.py:302
  9.1 0.0 collective-permute-start.3
  9.1 2.4 %collective-permute-start.4 = (bf16[256,256]{1,0:T(8,128)(2,1)S(1)}, bf16[256,256]{1,0:T(8,128)(2,1)S(1)}, u32[]{:S(2)}, u32[]{:S(2)}) collective-permute-start(bf16[256,256]{1,0:T(8,128)(2,1)S(1)} %get-tuple-element.21.kv_ref.rest_3_), channel_id=1, source_target_pairs={{0,6},{1,7},{2,4},{3,5},{6,0},{7,1},{4,2},{5,3},{8,14},{9,15},{10,... | collective-permute-start | bytes 393224 | tf_op jit(solution)/shard_map/ppermute | solution.py:302
  11.6 1.2 %collective-permute-start.5 = (bf16[256,256]{1,0:T(8,128)(2,1)S(1)}, bf16[256,256]{1,0:T(8,128)(2,1)S(1)}, u32[]{:S(2)}, u32[]{:S(2)}) collective-permute-start(bf16[256,256]{1,0:T(8,128)(2,1)S(1)} %get-tuple-element.21.kv_ref.rest_3_), channel_id=1, source_target_pairs={{0,1},{1,0},{2,3},{3,2},{4,5},{5,4},{6,7},{7,6},{8,9},{9,8},{10,11... | collective-permute-start | bytes 393224 | tf_op jit(solution)/shard_map/ppermute | solution.py:309
  12.8 0.0 copy-done.2
  12.8 1.1 %query.1 = (bf16[1024,256]{1,0:T(8,128)(2,1)S(1)}, f32[1024,256]{1,0:T(8,128)S(1)}) custom-call(bf16[256,1536]{1,0:T(8,128)(2,1)S(1)} %get-tuple-element.20.attn_ref, bf16[1536,512]{1,0:T(8,128)(2,1)S(1)} %copy-done.2, bf16[256,256]{1,0:T(8,128)(2,1)S(1)} %get-tuple-element.21.kv_ref.rest_3_), custom_call_target="tpu_custom_call" | custom-call | flops 536870912 | tf_op jit(solution)/shard_map/query/pallas_call | solution.py:235
  13.9 0.0 collective-permute-done.2.rest_0_.rest_5_
  13.9 0.6 %fold0.1.acc_in = f32[1024,256]{1,0:T(8,128)S(1)} custom-call(bf16[1024,256]{1,0:T(8,128)(2,1)S(1)} %get-tuple-element.22.q_ref, f32[1024,256]{1,0:T(8,128)S(1)} %get-tuple-element.24.acc_in, bf16[256,256]{1,0:T(8,128)(2,1)S(1)} %collective-permute-done.2.rest_0_.rest_5_), custom_call_target="tpu_custom_call", output_to_operand_aliasing={{}: (1, {})} | custom-call | flops 134217728 | tf_op jit(solution)/shard_map/fold0/pallas_call | solution.py:235
  14.5 0.0 collective-permute-done.3.rest_0_.rest_6_
  14.5 1.5 %collective-permute-start.7 = (bf16[256,256]{1,0:T(8,128)(2,1)S(1)}, bf16[256,256]{1,0:T(8,128)(2,1)S(1)}, u32[]{:S(2)}, u32[]{:S(2)}) collective-permute-start(bf16[256,256]{1,0:T(8,128)(2,1)S(1)} %collective-permute-done.3.rest_0_.rest_6_), channel_id=1, source_target_pairs={{0,1},{1,0},{2,3},{3,2},{4,5},{5,4},{6,7},{7,6},{8,9},{9,8},{10,11... | collective-permute-start | bytes 393224 | tf_op jit(solution)/shard_map/ppermute | solution.py:323
  16.0 0.1 collective-permute-start.6
  16.1 0.6 %fold1.1.acc_in = f32[1024,256]{1,0:T(8,128)S(1)} custom-call(bf16[1024,256]{1,0:T(8,128)(2,1)S(1)} %get-tuple-element.22.q_ref, f32[1024,256]{1,0:T(8,128)S(1)} %fold0.1.acc_in, bf16[256,256]{1,0:T(8,128)(2,1)S(1)} %collective-permute-done.3.rest_0_.rest_6_), custom_call_target="tpu_custom_call", output_to_operand_aliasing={{}: (1, {})} | custom-call | flops 134217728 | tf_op jit(solution)/shard_map/fold1/pallas_call | solution.py:235
  16.7 0.0 copy-start.3
  16.7 0.0 collective-permute-done.4.rest_1_.rest_7_
  16.7 0.7 %collective-permute-start.8 = (bf16[256,256]{1,0:T(8,128)(2,1)S(1)}, bf16[256,256]{1,0:T(8,128)(2,1)S(1)}, u32[]{:S(2)}, u32[]{:S(2)}) collective-permute-start(bf16[256,256]{1,0:T(8,128)(2,1)S(1)} %collective-permute-done.4.rest_1_.rest_7_), channel_id=1, source_target_pairs={{0,1},{1,0},{2,3},{3,2},{4,5},{5,4},{6,7},{7,6},{8,9},{9,8},{10,11... | collective-permute-start | bytes 393224 | tf_op jit(solution)/shard_map/ppermute | solution.py:323
  17.4 0.0 collective-permute-done.5.rest_0_.rest_4_
  17.4 0.0 collective-permute-done.7.rest_3_.rest_2_
  17.4 0.0 collective-permute-done.6.rest_2_.rest_1_
  17.4 1.4 %fold2.1.acc_in = f32[1024,256]{1,0:T(8,128)S(1)} custom-call(bf16[1024,256]{1,0:T(8,128)(2,1)S(1)} %get-tuple-element.22.q_ref, f32[1024,256]{1,0:T(8,128)S(1)} %fold1.1.acc_in, bf16[256,256]{1,0:T(8,128)(2,1)S(1)} %collective-permute-done.5.rest_0_.rest_4_, ...), custom_call_target="tpu_custom_call", output_to_operand_aliasing={{}: (1, {})} | custom-call | flops 536870912 | tf_op jit(solution)/shard_map/fold2/pallas_call | solution.py:235
  18.8 0.0 collective-permute-done.8.rest_0_
  18.9 0.0 copy-done.3
  18.9 1.7 %last.1 = bf16[256,1536]{1,0:T(8,128)(2,1)} custom-call(bf16[1024,256]{1,0:T(8,128)(2,1)S(1)} %get-tuple-element.22.q_ref, f32[1024,256]{1,0:T(8,128)S(1)} %fold2.1.acc_in, bf16[256,1536]{1,0:T(8,128)(2,1)S(1)} %get-tuple-element.30.hidden_ref, bf16[512,1536]{1,0:T(8,128)(2,1)S(1)} %copy-done.3, bf16[256,256]{1,0:T(8,128)(2,1)S(1)} %collective-permute-done.8.rest_0_, ...), custom_call_target="tpu_custom_call" | custom-call | flops 536870912 | tf_op jit(solution)/shard_map/last/pallas_call | solution.py:235
Async XLA Ops:
  0.0 3.8 %copy-start.1 = (bf16[256,1536]{1,0:T(8,128)(2,1)S(1)}, bf16[256,1536]{1,0:T(8,128)(2,1)}, u32[]{:S(2)}) copy-start(bf16[256,1536]{1,0:T(8,128)(2,1)} %x_ref.3) | copy-start | bytes 2359300
  0.0 3.8 %copy-start.6 = (f32[1536]{0:T(1024)S(1)}, f32[1536]{0:T(1024)}, u32[]{:S(2)}) copy-start(f32[1536]{0:T(1024)} %gain_ref.5) | copy-start | bytes 18436
  0.0 4.1 %copy-start = (bf16[3,1536,768]{2,1,0:T(8,128)(2,1)S(1)}, bf16[3,1536,768]{2,1,0:T(8,128)(2,1)}, u32[]{:S(2)}) copy-start(bf16[3,1536,768]{2,1,0:T(8,128)(2,1)} %w_ref.3) | copy-start | bytes 21233668
  1.0 3.1 %collective-permute-start = (bf16[4,1536]{1,0:T(4,128)(2,1)S(1)}, bf16[4,1536]{1,0:T(4,128)(2,1)S(1)}, u32[]{:S(2)}, u32[]{:S(2)}) collective-permute-start(bf16[4,1536]{1,0:T(4,128)(2,1)S(1)} %get-tuple-element.18), channel_id=1, source_target_pairs={{0,1},{1,0},{2,3},{3,2},{4,5},{5,4},{6,7},{7,6},{8,9},{9,8},{10,11... | collective-permute-start | bytes 36872 | tf_op jit(solution)/shard_map/ppermute | solution.py:271
  1.1 5.1 %collective-permute-start.1 = (bf16[4,1536]{1,0:T(4,128)(2,1)S(1)}, bf16[4,1536]{1,0:T(4,128)(2,1)S(1)}, u32[]{:S(2)}, u32[]{:S(2)}) collective-permute-start(bf16[4,1536]{1,0:T(4,128)(2,1)S(1)} %get-tuple-element.19), channel_id=1, source_target_pairs={{0,7},{1,2},{2,1},{3,4},{4,3},{5,6},{6,5},{7,0},{8,15},{9,10},{10,... | collective-permute-start | bytes 36872 | tf_op jit(solution)/shard_map/ppermute | solution.py:270
  4.1 2.2 %copy-start.4 = (bf16[1536,128]{1,0:T(8,128)(2,1)S(1)}, bf16[1536,128]{1,0:T(8,128)(2,1)}, u32[]{:S(2)}) copy-start(bf16[1536,128]{1,0:T(8,128)(2,1)} %wk_ref.1) | copy-start | bytes 1179652
  4.1 2.2 %copy-start.5 = (bf16[1536,128]{1,0:T(8,128)(2,1)S(1)}, bf16[1536,128]{1,0:T(8,128)(2,1)}, u32[]{:S(2)}) copy-start(bf16[1536,128]{1,0:T(8,128)(2,1)} %wv_ref.1) | copy-start | bytes 1179652
  4.1 2.2 %copy-start.7 = (f32[1536]{0:T(1024)S(1)}, f32[1536]{0:T(1024)}, u32[]{:S(2)}) copy-start(f32[1536]{0:T(1024)} %again_ref.1) | copy-start | bytes 18436
  4.1 2.2 %copy-start.8 = (f32[768]{0:T(1024)S(1)}, f32[768]{0:T(1024)}, u32[]{:S(2)}) copy-start(f32[768]{0:T(1024)} %bias_ref.1) | copy-start | bytes 9220
  6.3 6.5 %copy-start.2 = (bf16[1536,512]{1,0:T(8,128)(2,1)S(1)}, bf16[1536,512]{1,0:T(8,128)(2,1)}, u32[]{:S(2)}) copy-start(bf16[1536,512]{1,0:T(8,128)(2,1)} %wq_ref.1) | copy-start | bytes 4718596
  7.6 6.3 %collective-permute-start.2 = (bf16[256,256]{1,0:T(8,128)(2,1)S(1)}, bf16[256,256]{1,0:T(8,128)(2,1)S(1)}, u32[]{:S(2)}, u32[]{:S(2)}) collective-permute-start(bf16[256,256]{1,0:T(8,128)(2,1)S(1)} %get-tuple-element.21.kv_ref.rest_3_), channel_id=1, source_target_pairs={{0,4},{1,3},{2,0},{3,7},{6,2},{7,5},{4,6},{5,1},{8,12},{9,11},{10,... | collective-permute-start | bytes 393224 | tf_op jit(solution)/shard_map/ppermute | solution.py:302
  9.1 5.4 %collective-permute-start.3 = (bf16[256,256]{1,0:T(8,128)(2,1)S(1)}, bf16[256,256]{1,0:T(8,128)(2,1)S(1)}, u32[]{:S(2)}, u32[]{:S(2)}) collective-permute-start(bf16[256,256]{1,0:T(8,128)(2,1)S(1)} %get-tuple-element.21.kv_ref.rest_3_), channel_id=1, source_target_pairs={{0,2},{1,5},{2,6},{3,1},{6,4},{7,3},{4,0},{5,7},{8,10},{9,13},{10,... | collective-permute-start | bytes 393224 | tf_op jit(solution)/shard_map/ppermute | solution.py:302
  9.1 7.6 %collective-permute-start.4 = (bf16[256,256]{1,0:T(8,128)(2,1)S(1)}, bf16[256,256]{1,0:T(8,128)(2,1)S(1)}, u32[]{:S(2)}, u32[]{:S(2)}) collective-permute-start(bf16[256,256]{1,0:T(8,128)(2,1)S(1)} %get-tuple-element.21.kv_ref.rest_3_), channel_id=1, source_target_pairs={{0,6},{1,7},{2,4},{3,5},{6,0},{7,1},{4,2},{5,3},{8,14},{9,15},{10,... | collective-permute-start | bytes 393224 | tf_op jit(solution)/shard_map/ppermute | solution.py:302
  11.6 5.9 %collective-permute-start.5 = (bf16[256,256]{1,0:T(8,128)(2,1)S(1)}, bf16[256,256]{1,0:T(8,128)(2,1)S(1)}, u32[]{:S(2)}, u32[]{:S(2)}) collective-permute-start(bf16[256,256]{1,0:T(8,128)(2,1)S(1)} %get-tuple-element.21.kv_ref.rest_3_), channel_id=1, source_target_pairs={{0,1},{1,0},{2,3},{3,2},{4,5},{5,4},{6,7},{7,6},{8,9},{9,8},{10,11... | collective-permute-start | bytes 393224 | tf_op jit(solution)/shard_map/ppermute | solution.py:309
  14.5 2.9 %collective-permute-start.7 = (bf16[256,256]{1,0:T(8,128)(2,1)S(1)}, bf16[256,256]{1,0:T(8,128)(2,1)S(1)}, u32[]{:S(2)}, u32[]{:S(2)}) collective-permute-start(bf16[256,256]{1,0:T(8,128)(2,1)S(1)} %collective-permute-done.3.rest_0_.rest_6_), channel_id=1, source_target_pairs={{0,1},{1,0},{2,3},{3,2},{4,5},{5,4},{6,7},{7,6},{8,9},{9,8},{10,11... | collective-permute-start | bytes 393224 | tf_op jit(solution)/shard_map/ppermute | solution.py:323
  16.0 1.4 %collective-permute-start.6 = (bf16[256,256]{1,0:T(8,128)(2,1)S(1)}, bf16[256,256]{1,0:T(8,128)(2,1)S(1)}, u32[]{:S(2)}, u32[]{:S(2)}) collective-permute-start(bf16[256,256]{1,0:T(8,128)(2,1)S(1)} %collective-permute-done.2.rest_0_.rest_5_), channel_id=1, source_target_pairs={{0,1},{1,0},{2,3},{3,2},{4,5},{5,4},{6,7},{7,6},{8,9},{9,8},{10,11... | collective-permute-start | bytes 393224 | tf_op jit(solution)/shard_map/ppermute | solution.py:323
  16.7 2.2 %copy-start.3 = (bf16[512,1536]{1,0:T(8,128)(2,1)S(1)}, bf16[512,1536]{1,0:T(8,128)(2,1)}, u32[]{:S(2)}) copy-start(bf16[512,1536]{1,0:T(8,128)(2,1)} %wo_ref.1) | copy-start | bytes 4718596
  16.7 2.1 %collective-permute-start.8 = (bf16[256,256]{1,0:T(8,128)(2,1)S(1)}, bf16[256,256]{1,0:T(8,128)(2,1)S(1)}, u32[]{:S(2)}, u32[]{:S(2)}) collective-permute-start(bf16[256,256]{1,0:T(8,128)(2,1)S(1)} %collective-permute-done.4.rest_1_.rest_7_), channel_id=1, source_target_pairs={{0,1},{1,0},{2,3},{3,2},{4,5},{5,4},{6,7},{7,6},{8,9},{9,8},{10,11... | collective-permute-start | bytes 393224 | tf_op jit(solution)/shard_map/ppermute | solution.py:323
